TPU v7x, 512 devices: a whole 4x8x8 slice. The times are simulated.
512 devices in a mesh: seq: 64 (over y, z), mlp: 8 (over x, core).
Axes of the slice: x: 4, y: 8, z: 8, core: 2. Of those that a mesh axis runs over, the one named last changes fastest.
Arguments:
- queries: bfloat16 [16384, 3072], P('seq', 'mlp'), may hold values from -5 to 5
- key_vectors: bfloat16 [16384, 3072], P('seq', 'mlp'), may hold values from -5 to 5
- value_vectors: bfloat16 [16384, 3072], P('seq', 'mlp'), may hold values from -6 to 6
- head_kinds: int32 [24], P('mlp'), may hold values from 0 to 1
- block_masks: int32 [24, 2, 2], P('mlp'), may hold values from 0 to 1, as said below
- order_map: int32 [256], replicated, may hold values from 0 to 255, as said below
- out_weight: bfloat16 [3072, 3072], P('seq', 'mlp'), may hold values from -0.109375 to 0.109375
- gate_values: float32 [3072], P('mlp'), may hold values from 0.5 to 2
Outputs:
- gated_output: bfloat16 [16384, 3072], P('seq', 'mlp')
Inputs may be any that keep to these rules, and one draw needn't show every extreme that they name: block_masks[h, b, b] = 1 for every head h and block b. A permutation of the 256 positions in which order_map[2 i] is even and order_map[2 i + 1] = order_map[2 i] + 1.
All inputs are finite; a program needn't handle non-finite values.
Results may differ from a plain program's by a relative error of at most 0.0056.
Values may be sent and summed in bfloat16 or wider, within the bound.
No kernel may reach another device: no remote copies, remote signals or barrier semaphores. Data moves between devices by JAX's collectives and lax.ppermute only.
A program may use at most 64 MiB of HBM per device.

v0:
```python
import math

import jax
import jax.numpy as jnp
from jax import lax
from jax.sharding import PartitionSpec as P


def attend_rows(query_rows, key_rows, value_rows, visible):
    row_count, head_count, head_depth = query_rows.shape
    score_scale = 1.0 / math.sqrt(head_depth)
    scores = (
        jnp.einsum("qhd,khd->hqk", query_rows, key_rows, preferred_element_type=jnp.float32)
        * score_scale
    )
    row_max = jnp.max(jnp.where(visible, scores, -jnp.inf), axis=2, keepdims=True)
    weights = jnp.where(visible, jnp.exp(scores - row_max), 0.0)
    row_total = jnp.sum(weights, axis=2)
    combined = jnp.einsum(
        "hqk,khd->qhd", weights.astype(jnp.bfloat16), value_rows, preferred_element_type=jnp.float32
    )
    outputs = (combined / jnp.transpose(row_total)[:, :, None]).astype(jnp.bfloat16)
    return outputs


def to_positions(query_rows, key_rows, value_rows, frames, group_size):
    row_width = query_rows.shape[1]
    exchanged = (
        lax.all_to_all(
            query_rows.reshape(frames, group_size, 1, row_width),
            "seq",
            split_axis=0,
            concat_axis=2,
            tiled=True,
        ),
        lax.all_to_all(
            key_rows.reshape(frames, group_size, 1, row_width),
            "seq",
            split_axis=0,
            concat_axis=2,
            tiled=True,
        ),
        lax.all_to_all(
            value_rows.reshape(frames, group_size, 1, row_width),
            "seq",
            split_axis=0,
            concat_axis=2,
            tiled=True,
        ),
    )
    return tuple((member.reshape(group_size * frames, row_width) for member in exchanged))


def to_frames(results, frames, group_size):
    row_width = results.shape[1]
    exchanged = lax.all_to_all(
        results.reshape(1, group_size, frames, row_width),
        "seq",
        split_axis=2,
        concat_axis=0,
        tiled=True,
    )
    return exchanged.reshape(frames * group_size, row_width)


def split_heads(array, head_count):
    return array.reshape(array.shape[0], head_count, array.shape[1] // head_count)


def local(
    queries, key_vectors, value_vectors, head_kinds, block_masks, order_map, out_weight, gate_values
):
    row_count, row_width = queries.shape
    head_count = head_kinds.shape[0]
    frames = lax.axis_size("seq")
    group_size = row_count // frames
    block_size = row_count // block_masks.shape[1]
    inverse = (
        jnp.zeros((row_count,), jnp.int32).at[order_map].set(jnp.arange(row_count, dtype=jnp.int32))
    )
    visible = jnp.repeat(jnp.repeat(block_masks == 1, block_size, axis=1), block_size, axis=2)
    temporal = (head_kinds == 1)[None, :, None]
    moved_queries, moved_keys, moved_values = to_positions(
        queries[order_map], key_vectors[order_map], value_vectors[order_map], frames, group_size
    )
    near_result = attend_rows(
        split_heads(queries, head_count),
        split_heads(key_vectors, head_count),
        split_heads(value_vectors, head_count),
        visible,
    )
    far_result = attend_rows(
        split_heads(moved_queries, head_count),
        split_heads(moved_keys, head_count),
        split_heads(moved_values, head_count),
        visible,
    )
    returned = to_frames(far_result.reshape(row_count, row_width), frames, group_size)[inverse]
    per_head = jnp.where(temporal, split_heads(returned, head_count), near_result)
    attended = per_head.reshape(row_count, row_width)
    head_columns = lax.all_gather(attended, "mlp", axis=1, tiled=True)
    projected = jnp.dot(
        head_columns,
        lax.all_gather(out_weight, "seq", axis=0, tiled=True),
        preferred_element_type=jnp.float32,
    )
    return (gate_values[None, :] * projected).astype(jnp.bfloat16)


def solution(mesh):
    in_specs = (
        P("seq", "mlp"),
        P("seq", "mlp"),
        P("seq", "mlp"),
        P("mlp"),
        P("mlp", None, None),
        P(),
        P("seq", "mlp"),
        P("mlp"),
    )
    out_specs = P("seq", "mlp")
    return jax.shard_map(local, mesh=mesh, in_specs=in_specs, out_specs=out_specs, check_vma=False)
```

profile of v0, /device:TPU:2, one launch (start us, length us, event | category | flops | bytes accessed | tf_op | source)
XLA Modules:
  0.0 218.1 jit_solution(14154696673961762769)
XLA Ops:
  6.5 0.0 copy-start.1
  6.5 0.7 compare_select_fusion.1
  7.3 0.0 copy-start
  7.3 2.2 gather_fusion.1
  9.4 0.0 copy-start.2
  9.4 0.7 reshape.46
  10.2 16.6 %all-to-all-start.1 = ((bf16[64,4,1,384]{3,1,2,0:T(4,128)(2,1)}), bf16[64,4,1,384]{3,1,2,0:T(4,128)(2,1)S(1)}, u32[]{:S(2)}, u32[]{:S(2)}) async-start(bf16[64,4,1,384]{3,1,2,0:T(4,128)(2,1)} %bitcast.4), calls=%async_computation.1 | async-start | bytes 393216 | tf_op jit(solution)/shard_map/all_to_all | solution.py:29
  26.8 0.0 copy-done.1
  26.8 1.2 gather_fusion.2
  27.9 0.0 copy-start.3
  28.0 0.7 reshape.47
  28.7 11.8 %all-to-all-done.1 = bf16[64,4,1,384]{3,1,2,0:T(4,128)(2,1)S(1)} async-done(((bf16[64,4,1,384]{3,1,2,0:T(4,128)(2,1)}), bf16[64,4,1,384]{3,1,2,0:T(4,128)(2,1)S(1)}, u32[]{:S(2)}, u32[]{:S(2)}) %all-to-all-start.1) | async-done | bytes 196640 | tf_op jit(solution)/shard_map/all_to_all | solution.py:29
  40.5 4.6 %all-to-all-start.2 = ((bf16[64,4,1,384]{3,1,2,0:T(4,128)(2,1)}), bf16[64,4,1,384]{3,1,2,0:T(4,128)(2,1)S(1)}, u32[]{:S(2)}, u32[]{:S(2)}) async-start(bf16[64,4,1,384]{3,1,2,0:T(4,128)(2,1)} %bitcast.7), calls=%async_computation.2 | async-start | bytes 393216 | tf_op jit(solution)/shard_map/all_to_all | solution.py:36
  45.1 0.0 copy-done
  45.1 0.1 copy.51
  45.3 0.1 copy.52
  45.4 0.0 copy-done.2
  45.4 1.2 gather_fusion
  46.6 0.7 reshape.43
  47.3 11.0 %all-to-all-done.2 = bf16[64,4,1,384]{3,1,2,0:T(4,128)(2,1)S(1)} async-done(((bf16[64,4,1,384]{3,1,2,0:T(4,128)(2,1)}), bf16[64,4,1,384]{3,1,2,0:T(4,128)(2,1)S(1)}, u32[]{:S(2)}, u32[]{:S(2)}) %all-to-all-start.2) | async-done | bytes 196640 | tf_op jit(solution)/shard_map/all_to_all | solution.py:36
  58.4 4.6 %all-to-all-start = ((bf16[64,4,1,384]{3,1,2,0:T(4,128)(2,1)}), bf16[64,4,1,384]{3,1,2,0:T(4,128)(2,1)S(1)}, u32[]{:S(2)}, u32[]{:S(2)}) async-start(bf16[64,4,1,384]{3,1,2,0:T(4,128)(2,1)} %bitcast), calls=%async_computation | async-start | bytes 393216 | tf_op jit(solution)/shard_map/all_to_all | solution.py:43
  63.0 0.0 copy-done.3
  63.0 0.1 copy.38
  63.2 0.1 broadcast_in_dim.40
  63.3 1.4 scatter_custom_fusion
  64.7 0.1 reshape_reshape.13
  64.8 0.1 reshape_reshape.14
  64.9 0.3 convolution_multiply_fusion.1
  65.1 0.3 bitcast_select_fusion.1
  65.5 0.2 fusion.18
  65.7 10.3 %all-to-all-done = bf16[64,4,1,384]{3,1,2,0:T(4,128)(2,1)S(1)} async-done(((bf16[64,4,1,384]{3,1,2,0:T(4,128)(2,1)}), bf16[64,4,1,384]{3,1,2,0:T(4,128)(2,1)S(1)}, u32[]{:S(2)}, u32[]{:S(2)}) %all-to-all-start) | async-done | bytes 196640 | tf_op jit(solution)/shard_map/all_to_all | solution.py:43
  76.0 0.0 copy-start.5
  76.0 0.3 copy.61
  76.3 0.3 reshape.99
  76.6 0.2 fusion.10
  76.9 0.2 reshape.100
  77.1 0.9 copy.49
  78.0 4.6 %all-to-all-start.3 = ((bf16[1,4,64,384]{3,1,0,2:T(4,128)(2,1)}), bf16[1,4,64,384]{3,1,0,2:T(4,128)(2,1)S(1)}, u32[]{:S(2)}, u32[]{:S(2)}) async-start(bf16[1,4,64,384]{3,1,0,2:T(4,128)(2,1)} %copy.49), calls=%async_computation.3 | async-start | bytes 393216 | tf_op jit(solution)/shard_map/all_to_all | solution.py:56
  82.6 0.0 all-gather.3.cloned.1.call-start
  82.7 0.1 copy.55
  82.9 0.0 copy-done.5
  82.9 0.2 fusion.19
  83.1 12.6 %all-to-all-done.3 = bf16[1,4,64,384]{3,1,0,2:T(4,128)(2,1)S(1)} async-done(((bf16[1,4,64,384]{3,1,0,2:T(4,128)(2,1)}), bf16[1,4,64,384]{3,1,0,2:T(4,128)(2,1)S(1)}, u32[]{:S(2)}, u32[]{:S(2)}) %all-to-all-start.3) | async-done | bytes 196640 | tf_op jit(solution)/shard_map/all_to_all | solution.py:56
  95.7 0.1 reshape.48
  95.7 0.0 copy-start.4
  95.8 1.2 gather_fusion.3
  96.9 0.1 copy.50
  97.1 0.9 fusion.11
  98.0 0.0 all-gather.3.cloned.1.call-update
  98.0 0.0 all-gather.5.cloned.1.call-start
  98.1 0.7 all-gather.5.cloned.1.call-update
  98.8 19.5 %all-gather.3.cloned.1.call-done = bf16[256,3072]{0,1:T(8,128)(2,1)} async-done(((bf16[256,384]{0,1:T(8,128)(2,1)}), bf16[256,3072]{0,1:T(8,128)(2,1)}) %all-gather.3.cloned.1.call-update) | async-done | bytes 1572880 | tf_op jit(solution)/shard_map/all_gather | solution.py:101
  118.3 89.2 %all-gather.5.cloned.1.call-done = bf16[3072,384]{1,0:T(8,128)(2,1)} async-done(((bf16[48,384]{1,0:T(8,128)(2,1)}), bf16[3072,384]{1,0:T(8,128)(2,1)}) %all-gather.5.cloned.1.call-update) | async-done | bytes 2359312 | tf_op jit(solution)/shard_map/all_gather | solution.py:104
  207.4 0.0 copy-done.4
  207.4 3.8 %fusion.8 = bf16[256,384]{1,0:T(8,128)(2,1)} fusion(bf16[256,3072]{0,1:T(8,128)(2,1)} %all-gather.3.cloned.1.call-done, bf16[3072,384]{1,0:T(8,128)(2,1)} %all-gather.5.cloned.1.call-done, f32[384]{0:T(512)S(1)} %copy-done.4), kind=kOutput, calls=%fused_computation.22 | convolution fusion | flops 604176384 | bytes 4130304 | tf_op jit(solution)/shard_map/dot_general | solution.py:102
  (10 shorter events, 0.1 us)
Async XLA Ops:
  6.5 20.2 %copy-start.1 = (bf16[256,384]{1,0:T(8,128)(2,1)S(1)}, bf16[256,384]{1,0:T(8,128)(2,1)}, u32[]{:S(2)}) copy-start(bf16[256,384]{1,0:T(8,128)(2,1)} %param.9) | copy-start | bytes 589828
  7.3 37.9 %copy-start = (bf16[256,384]{1,0:T(8,128)(2,1)S(1)}, bf16[256,384]{1,0:T(8,128)(2,1)}, u32[]{:S(2)}) copy-start(bf16[256,384]{1,0:T(8,128)(2,1)} %param.8) | copy-start | bytes 589828
  9.4 36.0 %copy-start.2 = (bf16[256,384]{1,0:T(8,128)(2,1)S(1)}, bf16[256,384]{1,0:T(8,128)(2,1)}, u32[]{:S(2)}) copy-start(bf16[256,384]{1,0:T(8,128)(2,1)} %param.10) | copy-start | bytes 589828
  10.2 30.3 %all-to-all-start.1 = ((bf16[64,4,1,384]{3,1,2,0:T(4,128)(2,1)}), bf16[64,4,1,384]{3,1,2,0:T(4,128)(2,1)S(1)}, u32[]{:S(2)}, u32[]{:S(2)}) async-start(bf16[64,4,1,384]{3,1,2,0:T(4,128)(2,1)} %bitcast.4), calls=%async_computation.1 | async-start | bytes 393216 | tf_op jit(solution)/shard_map/all_to_all | solution.py:29
  27.9 35.1 %copy-start.3 = (s32[3,2,2]{0,2,1:T(2,128)S(1)}, s32[3,2,2]{0,2,1:T(2,128)}, u32[]{:S(2)}) copy-start(s32[3,2,2]{0,2,1:T(2,128)} %param.12) | copy-start | bytes 148
  40.5 17.9 %all-to-all-start.2 = ((bf16[64,4,1,384]{3,1,2,0:T(4,128)(2,1)}), bf16[64,4,1,384]{3,1,2,0:T(4,128)(2,1)S(1)}, u32[]{:S(2)}, u32[]{:S(2)}) async-start(bf16[64,4,1,384]{3,1,2,0:T(4,128)(2,1)} %bitcast.7), calls=%async_computation.2 | async-start | bytes 393216 | tf_op jit(solution)/shard_map/all_to_all | solution.py:36
  58.4 17.7 %all-to-all-start = ((bf16[64,4,1,384]{3,1,2,0:T(4,128)(2,1)}), bf16[64,4,1,384]{3,1,2,0:T(4,128)(2,1)S(1)}, u32[]{:S(2)}, u32[]{:S(2)}) async-start(bf16[64,4,1,384]{3,1,2,0:T(4,128)(2,1)} %bitcast), calls=%async_computation | async-start | bytes 393216 | tf_op jit(solution)/shard_map/all_to_all | solution.py:43
  76.0 6.8 %copy-start.5 = (s32[3]{0:T(128)S(1)}, s32[3]{0:T(128)}, u32[]{:S(2)}) copy-start(s32[3]{0:T(128)} %param.11) | copy-start | bytes 40
  78.0 17.7 %all-to-all-start.3 = ((bf16[1,4,64,384]{3,1,0,2:T(4,128)(2,1)}), bf16[1,4,64,384]{3,1,0,2:T(4,128)(2,1)S(1)}, u32[]{:S(2)}, u32[]{:S(2)}) async-start(bf16[1,4,64,384]{3,1,0,2:T(4,128)(2,1)} %copy.49), calls=%async_computation.3 | async-start | bytes 393216 | tf_op jit(solution)/shard_map/all_to_all | solution.py:56
  82.6 35.6 %all-gather.3.cloned.1.call-start = ((), (), s32[]{:S(2)}) async-start(), calls=%async_computation.4 | async-start | bytes 1769472 | tf_op jit(solution)/shard_map/all_gather | solution.py:101
  95.7 111.7 %copy-start.4 = (f32[384]{0:T(512)S(1)}, f32[384]{0:T(512)}, u32[]{:S(2)}) copy-start(f32[384]{0:T(512)} %param.15) | copy-start | bytes 4612
  98.0 109.4 %all-gather.5.cloned.1.call-start = ((), (), s32[]{:S(2)}) async-start(), calls=%async_computation.5 | async-start | bytes 2396160 | tf_op jit(solution)/shard_map/all_gather | solution.py:104
Sparse Core Ops, SparseCore 0:
  98.1 20.0 all-gather.2
  121.3 86.0 all-gather.4
where the time goes:
time: 218 us
  waiting for transfers between devices  155 us (71%)
  starting transfers between devices  30.5 us (14%)
  between operations  13.6 us (6%)
  local copies, waits for them, and re-layouts  12 us (6%)
  matrix products  5.55 us (3%)
    all_gather x1, waiting for transfers between devices, local(): lax.all_gather(out_weight, 'seq', axis=0, tiled=True)  89.2 us
    all_gather x1, waiting for transfers between devices, local(): head_columns = lax.all_gather(attended, 'mlp', axis=1, tiled=True)  19.5 us
    all_to_all x1, starting transfers between devices, to_positions(): lax.all_to_all(query_rows.reshape(frames, group_size, 1, row_width), 'seq...  16.6 us
    all_to_all x1, waiting for transfers between devices, to_frames(): lax.all_to_all(results.reshape(1, group_size, frames, row_width), 'seq',...  12.6 us
    all_to_all x1, waiting for transfers between devices, to_positions(): lax.all_to_all(query_rows.reshape(frames, group_size, 1, row_width), 'seq...  11.8 us
    all_to_all x1, waiting for transfers between devices, to_positions(): lax.all_to_all(key_rows.reshape(frames, group_size, 1, row_width), 'seq',...  11 us
    all_to_all x1, waiting for transfers between devices, to_positions(): lax.all_to_all(value_rows.reshape(frames, group_size, 1, row_width), 'seq...  10.3 us
    all_to_all x1, starting transfers between devices, to_positions(): lax.all_to_all(value_rows.reshape(frames, group_size, 1, row_width), 'seq...  4.62 us
  transfers between devices with their start and end apart: 6, of which 6 were waited for; matrix products, arithmetic and copies ran while one was open for 3% of the time, Pallas kernels for 0%

commit v1 on v0

v1 whole, which is shorter than its diff:
```python
import functools
import math

import jax
import jax.numpy as jnp
from jax import lax
from jax.experimental import pallas as pl
from jax.experimental.pallas import tpu as pltpu
from jax.sharding import PartitionSpec as P

VMEM = pl.BlockSpec(memory_space=pltpu.VMEM)
SMEM = pl.BlockSpec(memory_space=pltpu.SMEM)
PARAMS = pltpu.CompilerParams(vmem_limit_bytes=40 * 1024 * 1024)


def placement(order, rows):
    positions = lax.broadcasted_iota(jnp.int32, (rows, rows), 0)
    return (positions == order).astype(jnp.float32).astype(jnp.bfloat16)


def send_kernel(order_ref, q_ref, k_ref, v_ref, out_ref):
    rows, width = q_ref.shape
    onehot = placement(order_ref[...], rows)
    for i, ref in enumerate((q_ref, k_ref, v_ref)):
        picked = lax.dot_general(
            onehot, ref[...], (((0,), (0,)), ((), ())), preferred_element_type=jnp.float32
        )
        out_ref[:, :, i * width : (i + 1) * width] = picked.reshape(
            out_ref.shape[0], out_ref.shape[1], width
        ).astype(jnp.bfloat16)


def attend(q, k, v, masks, head, row_block, column_block):
    depth = q.shape[1]
    scores = lax.dot_general(q, k, (((1,), (1,)), ((), ())), preferred_element_type=jnp.float32)
    scores = scores * (1.0 / math.sqrt(depth))
    seen = [masks[4 * head + i] for i in range(4)]
    chosen = jnp.where(
        row_block == 0,
        jnp.where(column_block == 0, seen[0], seen[1]),
        jnp.where(column_block == 0, seen[2], seen[3]),
    )
    visible = chosen == 1
    scores = jnp.where(visible, scores, -jnp.inf)
    row_max = jnp.max(scores, axis=1, keepdims=True)
    weights = jnp.exp(scores - row_max)
    total = jnp.sum(weights, axis=1, keepdims=True)
    combined = jnp.dot(weights.astype(jnp.bfloat16), v, preferred_element_type=jnp.float32)
    return combined / total


def near_kernel(masks_ref, q_ref, k_ref, v_ref, out_ref):
    rows, width = q_ref.shape
    heads = masks_ref.shape[0] // 4
    depth = width // heads
    row_block = lax.broadcasted_iota(jnp.int32, (rows, rows), 0) // (rows // 2)
    column_block = lax.broadcasted_iota(jnp.int32, (rows, rows), 1) // (rows // 2)
    for h in range(heads):
        c = slice(h * depth, (h + 1) * depth)
        out_ref[:, c] = attend(
            q_ref[:, c], k_ref[:, c], v_ref[:, c], masks_ref, h, row_block, column_block
        ).astype(jnp.bfloat16)


def far_kernel(masks_ref, x_ref, out_ref):
    frames, group, wide = x_ref.shape
    rows, width = frames * group, wide // 3
    heads = masks_ref.shape[0] // 4
    depth = width // heads
    row_block = (lax.broadcasted_iota(jnp.int32, (rows, rows), 0) % group) // (group // 2)
    column_block = (lax.broadcasted_iota(jnp.int32, (rows, rows), 1) % group) // (group // 2)
    for h in range(heads):
        q, k, v = (
            x_ref[:, :, i * width + h * depth : i * width + (h + 1) * depth]
            .astype(jnp.float32)
            .reshape(rows, depth)
            .astype(jnp.bfloat16)
            for i in range(3)
        )
        out = attend(q, k, v, masks_ref, h, row_block, column_block)
        out_ref[:, :, h * depth : (h + 1) * depth] = out.reshape(frames, group, depth).astype(
            jnp.bfloat16
        )


def select_kernel(kinds_ref, order_ref, far_ref, near_ref, out_ref):
    rows, width = near_ref.shape
    heads = kinds_ref.shape[0]
    depth = width // heads
    onehot = placement(order_ref[...], rows)
    for h in range(heads):
        c = slice(h * depth, (h + 1) * depth)
        far = far_ref[:, :, c].astype(jnp.float32).reshape(rows, depth).astype(jnp.bfloat16)
        back = jnp.dot(onehot, far, preferred_element_type=jnp.float32)
        near = near_ref[:, c].astype(jnp.float32)
        chosen = jnp.where(kinds_ref[h] == 1, back, near).astype(jnp.bfloat16)
        for m in range(out_ref.shape[0]):
            out_ref[m, :, c] = chosen


def order_kernel(*refs):
    *blocks, out_ref = refs
    z = lax.axis_index("seq") % 8
    for offset, rows, ref in zip((0, -1, 1, -4, 2), (48, 48, 48, 144, 96), blocks, strict=True):
        for i in range(rows // 48):
            at = lax.rem(z + (offset + i + 8), 8) * 48
            out_ref[pl.ds(pl.multiple_of(at, 16), 48), :] = ref[i * 48 : (i + 1) * 48, :]


def project_kernel(offsets, gate_ref, x_ref, *refs):
    *blocks, out_ref = refs
    n = x_ref.shape[0]
    y = lax.axis_index("seq") // n
    total = None
    for offset, w_ref in zip(offsets, blocks, strict=True):
        part = jnp.dot(
            x_ref[lax.rem(y + (offset + n), n)], w_ref[...], preferred_element_type=jnp.float32
        )
        total = part if total is None else total + part
    out_ref[...] = (gate_ref[...] * total).astype(jnp.bfloat16)


def call(kernel, shape, specs, *args):
    return pl.pallas_call(
        kernel,
        out_shape=jax.ShapeDtypeStruct(shape, jnp.bfloat16),
        in_specs=specs,
        out_specs=VMEM,
        compiler_params=PARAMS,
    )(*args)


def gather_weight(out_weight):
    def along_z(block, step):
        return lax.ppermute(
            block, "seq", [(i, i // 8 * 8 + (i + step) % 8) for i in range(64)]
        )

    def along_y(block, step):
        return lax.ppermute(block, "seq", [(i, (i + 8 * step) % 64) for i in range(64)])

    before = along_z(out_weight, 1)
    after = along_z(out_weight, -1)
    two = jnp.concatenate([before, out_weight], axis=0)
    three = jnp.concatenate([before, out_weight, after], axis=0)
    far_before = along_z(three, 3)
    far_after = along_z(two, -3)
    own = call(
        order_kernel,
        (384, out_weight.shape[1]),
        [VMEM] * 5,
        out_weight,
        before,
        after,
        far_before,
        far_after,
    )
    offsets, blocks = [0], [own]
    up = down = own
    for step in (1, 2, 3):
        up, down = along_y(up, 1), along_y(down, -1)
        offsets += [-step, step]
        blocks += [up, down]
    blocks.append(along_y(up, 1))
    offsets.append(-4)
    return offsets, blocks


def local(
    queries, key_vectors, value_vectors, head_kinds, block_masks, order_map, out_weight, gate_values
):
    rows, width = queries.shape
    frames = lax.axis_size("seq")
    parts = lax.axis_size("mlp")
    group = rows // frames
    masks = block_masks.reshape(-1)
    order = order_map.reshape(1, rows)
    offsets, blocks = gather_weight(out_weight)
    sent = call(
        send_kernel, (frames, group, 3 * width), [VMEM] * 4, order, queries, key_vectors, value_vectors
    )
    moved = lax.all_to_all(sent, "seq", split_axis=0, concat_axis=0, tiled=True)
    near = call(near_kernel, (rows, width), [SMEM] + [VMEM] * 3, masks, queries, key_vectors, value_vectors)
    far = call(far_kernel, (frames, group, width), [SMEM, VMEM], masks, moved)
    returned = lax.all_to_all(far, "seq", split_axis=0, concat_axis=0, tiled=True)
    attended = call(
        select_kernel, (parts, rows, width), [SMEM] + [VMEM] * 3, head_kinds, order, returned, near
    )
    columns = lax.all_to_all(attended, "mlp", split_axis=0, concat_axis=0, tiled=True)
    return call(
        functools.partial(project_kernel, offsets),
        (rows, width),
        [VMEM] * 10,
        gate_values.reshape(1, width),
        columns,
        *blocks,
    )


def solution(mesh):
    in_specs = (
        P("seq", "mlp"),
        P("seq", "mlp"),
        P("seq", "mlp"),
        P("mlp"),
        P("mlp", None, None),
        P(),
        P("seq", "mlp"),
        P("mlp"),
    )
    out_specs = P("seq", "mlp")
    return jax.shard_map(local, mesh=mesh, in_specs=in_specs, out_specs=out_specs, check_vma=False)
```

time: 218 us -> 130 us (0.60)
  the two profiles are of different devices: /device:TPU:2 before, /device:TPU:98 now
where the time goes in v1:
time: 130 us; the launch traced here: 129 us
  starting transfers between devices  67.3 us (52%)
  waiting for transfers between devices  45.9 us (35%)
  Pallas kernels  8.51 us (7%)
  local copies, waits for them, and re-layouts  7.04 us (5%)
    ppermute x7, starting transfers between devices, along_y(): lax.ppermute(block, 'seq', [(i, (i + 8 * step) % 64) for i in range(64)])  23 us
    ppermute x7, waiting for transfers between devices, along_y(): lax.ppermute(block, 'seq', [(i, (i + 8 * step) % 64) for i in range(64)])  18.4 us
    all_to_all x1, waiting for transfers between devices, local(): moved = lax.all_to_all(sent, 'seq', split_axis=0, concat_axis=0, tiled=True)  16.8 us
    all_to_all x1, starting transfers between devices, local(): moved = lax.all_to_all(sent, 'seq', split_axis=0, concat_axis=0, tiled=True)  15.6 us
    ppermute x4, starting transfers between devices, along_z(): lax.ppermute(block, 'seq', [(i, i // 8 * 8 + (i + step) % 8) for i in ran...  14.7 us
    ppermute x4, waiting for transfers between devices, along_z(): lax.ppermute(block, 'seq', [(i, i // 8 * 8 + (i + step) % 8) for i in ran...  9.73 us
    all_to_all x1, starting transfers between devices, local(): lax.all_to_all(far, 'seq', split_axis=0, concat_axis=0, tiled=True)  9.07 us
    pallas_call x6, Pallas kernels, call(): pl.pallas_call(kernel, out_shape=jax.ShapeDtypeStruct(shape, jnp.bfloat16...  8.51 us
  transfers between devices with their start and end apart: 14, of which 7 were waited for; matrix products, arithmetic and copies ran while one was open for 0% of the time, Pallas kernels for 3%

profile of v1, /device:TPU:98, one launch (start us, length us, event | category | flops | bytes accessed | tf_op | source)
XLA Modules:
  0.0 129.0 jit_solution(11280583711133676937)
XLA Ops:
  0.0 0.0 copy-start
  0.0 0.9 copy-done
  0.9 0.0 copy-start.2
  0.9 0.9 copy-done.2
  1.9 0.0 copy-start.4
  1.9 0.9 copy-done.4
  2.8 0.0 copy-start.11
  2.8 0.7 copy-done.11
  3.5 0.0 copy-start.15
  3.5 0.0 copy-start.1
  3.5 0.0 copy-start.3
  3.5 0.0 copy-start.5
  3.5 1.2 shard_map.82
  4.7 0.0 copy-start.12
  4.7 0.0 copy-start.13
  4.7 15.6 %all-to-all-start = ((bf16[64,4,1152]{2,1,0:T(4,128)(2,1)}), bf16[64,4,1152]{2,1,0:T(4,128)(2,1)S(1)}, u32[]{:S(2)}, u32[]{:S(2)}) async-start(bf16[64,4,1152]{2,1,0:T(4,128)(2,1)} %shard_map.82), calls=%async_computation | async-start | bytes 1179648 | tf_op jit(solution)/shard_map/all_to_all | solution.py:182
  20.3 0.0 copy-done.15
  20.3 0.1 copy.10
  20.4 0.1 reshape.11.masks_ref
  20.5 16.8 %all-to-all-done.x_ref = bf16[64,4,1152]{2,1,0:T(4,128)(2,1)S(1)} async-done(((bf16[64,4,1152]{2,1,0:T(4,128)(2,1)}), bf16[64,4,1152]{2,1,0:T(4,128)(2,1)S(1)}, u32[]{:S(2)}, u32[]{:S(2)}) %all-to-all-start) | async-done | bytes 589856 | tf_op jit(solution)/shard_map/all_to_all | solution.py:182
  37.3 2.0 %shard_map.83 = bf16[64,4,384]{2,1,0:T(4,128)(2,1)} custom-call(s32[12]{0:T(128)S(1)} %reshape.11.masks_ref, bf16[64,4,1152]{2,1,0:T(4,128)(2,1)S(1)} %all-to-all-done.x_ref), custom_call_target="tpu_custom_call" | custom-call | tf_op jit(solution)/shard_map/pallas_call | solution.py:124
  39.3 9.1 %all-to-all-start.1 = ((bf16[64,4,384]{2,1,0:T(4,128)(2,1)}), bf16[64,4,384]{2,1,0:T(4,128)(2,1)S(1)}, u32[]{:S(2)}, u32[]{:S(2)}) async-start(bf16[64,4,384]{2,1,0:T(4,128)(2,1)} %shard_map.83), calls=%async_computation.1 | async-start | bytes 393216 | tf_op jit(solution)/shard_map/all_to_all | solution.py:185
  48.3 0.0 copy-done.6
  48.4 3.4 %collective-permute-start = (bf16[48,384]{1,0:T(8,128)(2,1)S(1)}, bf16[48,384]{1,0:T(8,128)(2,1)S(1)}, u32[]{:S(2)}, u32[]{:S(2)}) collective-permute-start(bf16[48,384]{1,0:T(8,128)(2,1)S(1)} %copy-done.6), channel_id=1, source_target_pairs={{0,8},{8,16},{16,24},{24,32},{32,40},{40,48},{48,56},{56,0},{64,72... | collective-permute-start | bytes 110600 | tf_op jit(solution)/shard_map/ppermute | solution.py:135
  51.7 2.5 %collective-permute-start.1 = (bf16[48,384]{1,0:T(8,128)(2,1)S(1)}, bf16[48,384]{1,0:T(8,128)(2,1)S(1)}, u32[]{:S(2)}, u32[]{:S(2)}) collective-permute-start(bf16[48,384]{1,0:T(8,128)(2,1)S(1)} %copy-done.6), channel_id=1, source_target_pairs={{0,56},{8,0},{16,8},{24,16},{32,24},{40,32},{48,40},{56,48},{64,12... | collective-permute-start | bytes 110600 | tf_op jit(solution)/shard_map/ppermute | solution.py:135
  54.2 0.0 copy-done.1
  54.2 0.0 copy-done.3
  54.2 0.0 copy-done.5
  54.2 1.3 %shard_map.84.near_ref = bf16[256,384]{1,0:T(8,128)(2,1)S(1)} custom-call(s32[12]{0:T(128)S(1)} %reshape.11.masks_ref, bf16[256,384]{1,0:T(8,128)(2,1)S(1)} %copy-done.1, bf16[256,384]{1,0:T(8,128)(2,1)S(1)} %copy-done.3, bf16[256,384]{1,0:T(8,128)(2,1)S(1)} %copy-done.5), custom_call_target="tpu_custom_call" | custom-call | tf_op jit(solution)/shard_map/pallas_call | solution.py:124
  55.5 1.0 all-to-all-done.1.far_ref
  56.5 0.0 copy-done.12
  56.5 0.0 copy-done.13
  56.5 2.1 %shard_map.85 = bf16[8,256,384]{2,1,0:T(8,128)(2,1)} custom-call(s32[3]{0:T(128)S(1)} %copy-done.13, s32[1,256]{1,0:T(1,128)S(1)} %bitcast.2, bf16[64,4,384]{2,1,0:T(4,128)(2,1)S(1)} %all-to-all-done.1.far_ref, bf16[256,384]{1,0:T(8,128)(2,1)S(1)} %shard_map.84.near_ref), custom_call_target="tpu_custom_call" | custom-call | tf_op jit(solution)/shard_map/pallas_call | solution.py:124
  58.6 0.0 copy-start.14
  58.6 5.0 %all-to-all-start.2 = ((bf16[8,256,384]{2,1,0:T(8,128)(2,1)}), bf16[8,256,384]{2,1,0:T(8,128)(2,1)S(1)}, u32[]{:S(2)}, u32[]{:S(2)}) async-start(bf16[8,256,384]{2,1,0:T(8,128)(2,1)} %shard_map.85), calls=%async_computation.2 | async-start | bytes 3145728 | tf_op jit(solution)/shard_map/all_to_all | solution.py:189
  63.6 0.0 collective-permute-done.refs_1_
  63.6 0.0 collective-permute-done.1.refs_2_
  63.6 6.7 %collective-permute-start.2 = (bf16[144,384]{1,0:T(8,128)(2,1)S(1)}, bf16[144,384]{1,0:T(8,128)(2,1)S(1)}, u32[]{:S(2)}, u32[]{:S(2)}) collective-permute-start(bf16[144,384]{1,0:T(8,128)(2,1)S(1)} %pad_maximum_fusion), channel_id=1, source_target_pairs={{0,24},{8,32},{16,40},{24,48},{32,56},{40,0},{48,8},{56,16},{64,88... | collective-permute-start | bytes 331784 | tf_op jit(solution)/shard_map/ppermute | solution.py:135
  70.3 2.2 %collective-permute-start.3 = (bf16[96,384]{1,0:T(8,128)(2,1)S(1)}, bf16[96,384]{1,0:T(8,128)(2,1)S(1)}, u32[]{:S(2)}, u32[]{:S(2)}) collective-permute-start(bf16[96,384]{1,0:T(8,128)(2,1)S(1)} %pad_maximum_fusion.1), channel_id=1, source_target_pairs={{0,40},{8,48},{16,56},{24,0},{32,8},{40,16},{48,24},{56,32},{64,10... | collective-permute-start | bytes 221192 | tf_op jit(solution)/shard_map/ppermute | solution.py:135
  72.5 9.7 %collective-permute-done.3.refs_4_ = bf16[96,384]{1,0:T(8,128)(2,1)S(1)} collective-permute-done((bf16[96,384]{1,0:T(8,128)(2,1)S(1)}, bf16[96,384]{1,0:T(8,128)(2,1)S(1)}, u32[]{:S(2)}, u32[]{:S(2)}) %collective-permute-start.3) | collective-permute-done | bytes 73760 | tf_op jit(solution)/shard_map/ppermute | solution.py:135
  82.3 0.0 collective-permute-done.2.refs_3_
  82.3 0.1 shard_map.86.refs_0_
  82.3 2.5 %collective-permute-start.4 = (bf16[384,384]{1,0:T(8,128)(2,1)S(1)}, bf16[384,384]{1,0:T(8,128)(2,1)S(1)}, u32[]{:S(2)}, u32[]{:S(2)}) collective-permute-start(bf16[384,384]{1,0:T(8,128)(2,1)S(1)} %shard_map.86.refs_0_), channel_id=1, source_target_pairs={{0,64},{8,72},{16,80},{24,88},{32,96},{40,104},{48,112},{56,120},{... | collective-permute-start | bytes 884744 | tf_op jit(solution)/shard_map/ppermute | solution.py:140
  84.8 4.5 %collective-permute-start.5 = (bf16[384,384]{1,0:T(8,128)(2,1)S(1)}, bf16[384,384]{1,0:T(8,128)(2,1)S(1)}, u32[]{:S(2)}, u32[]{:S(2)}) collective-permute-start(bf16[384,384]{1,0:T(8,128)(2,1)S(1)} %shard_map.86.refs_0_), channel_id=1, source_target_pairs={{0,448},{8,456},{16,464},{24,472},{32,480},{40,488},{48,496},{56,5... | collective-permute-start | bytes 884744 | tf_op jit(solution)/shard_map/ppermute | solution.py:140
  89.4 4.7 %collective-permute-done.4.refs_1_ = bf16[384,384]{1,0:T(8,128)(2,1)S(1)} collective-permute-done((bf16[384,384]{1,0:T(8,128)(2,1)S(1)}, bf16[384,384]{1,0:T(8,128)(2,1)S(1)}, u32[]{:S(2)}, u32[]{:S(2)}) %collective-permute-start.4) | collective-permute-done | bytes 294944 | tf_op jit(solution)/shard_map/ppermute | solution.py:140
  94.0 1.9 %collective-permute-start.6 = (bf16[384,384]{1,0:T(8,128)(2,1)S(1)}, bf16[384,384]{1,0:T(8,128)(2,1)S(1)}, u32[]{:S(2)}, u32[]{:S(2)}) collective-permute-start(bf16[384,384]{1,0:T(8,128)(2,1)S(1)} %collective-permute-done.4.refs_1_), channel_id=1, source_target_pairs={{0,64},{8,72},{16,80},{24,88},{32,96},{40,104},{48,112},{56,120},{... | collective-permute-start | bytes 884744 | tf_op jit(solution)/shard_map/ppermute | solution.py:140
  96.0 0.0 collective-permute-done.5.refs_2_
  96.0 5.1 %collective-permute-start.7 = (bf16[384,384]{1,0:T(8,128)(2,1)S(1)}, bf16[384,384]{1,0:T(8,128)(2,1)S(1)}, u32[]{:S(2)}, u32[]{:S(2)}) collective-permute-start(bf16[384,384]{1,0:T(8,128)(2,1)S(1)} %collective-permute-done.5.refs_2_), channel_id=1, source_target_pairs={{0,448},{8,456},{16,464},{24,472},{32,480},{40,488},{48,496},{56,5... | collective-permute-start | bytes 884744 | tf_op jit(solution)/shard_map/ppermute | solution.py:140
  101.1 3.8 %collective-permute-done.6.refs_3_ = bf16[384,384]{1,0:T(8,128)(2,1)S(1)} collective-permute-done((bf16[384,384]{1,0:T(8,128)(2,1)S(1)}, bf16[384,384]{1,0:T(8,128)(2,1)S(1)}, u32[]{:S(2)}, u32[]{:S(2)}) %collective-permute-start.6) | collective-permute-done | bytes 294944 | tf_op jit(solution)/shard_map/ppermute | solution.py:140
  104.9 1.9 %collective-permute-start.8 = (bf16[384,384]{1,0:T(8,128)(2,1)S(1)}, bf16[384,384]{1,0:T(8,128)(2,1)S(1)}, u32[]{:S(2)}, u32[]{:S(2)}) collective-permute-start(bf16[384,384]{1,0:T(8,128)(2,1)S(1)} %collective-permute-done.6.refs_3_), channel_id=1, source_target_pairs={{0,64},{8,72},{16,80},{24,88},{32,96},{40,104},{48,112},{56,120},{... | collective-permute-start | bytes 884744 | tf_op jit(solution)/shard_map/ppermute | solution.py:140
  106.8 0.0 collective-permute-done.7.refs_4_
  106.8 5.1 %collective-permute-start.9 = (bf16[384,384]{1,0:T(8,128)(2,1)S(1)}, bf16[384,384]{1,0:T(8,128)(2,1)S(1)}, u32[]{:S(2)}, u32[]{:S(2)}) collective-permute-start(bf16[384,384]{1,0:T(8,128)(2,1)S(1)} %collective-permute-done.7.refs_4_), channel_id=1, source_target_pairs={{0,448},{8,456},{16,464},{24,472},{32,480},{40,488},{48,496},{56,5... | collective-permute-start | bytes 884744 | tf_op jit(solution)/shard_map/ppermute | solution.py:140
  111.9 2.8 %collective-permute-done.8.refs_5_ = bf16[384,384]{1,0:T(8,128)(2,1)S(1)} collective-permute-done((bf16[384,384]{1,0:T(8,128)(2,1)S(1)}, bf16[384,384]{1,0:T(8,128)(2,1)S(1)}, u32[]{:S(2)}, u32[]{:S(2)}) %collective-permute-start.8) | collective-permute-done | bytes 294944 | tf_op jit(solution)/shard_map/ppermute | solution.py:140
  114.8 1.9 %collective-permute-start.10 = (bf16[384,384]{1,0:T(8,128)(2,1)S(1)}, bf16[384,384]{1,0:T(8,128)(2,1)S(1)}, u32[]{:S(2)}, u32[]{:S(2)}) collective-permute-start(bf16[384,384]{1,0:T(8,128)(2,1)S(1)} %collective-permute-done.8.refs_5_), channel_id=1, source_target_pairs={{0,64},{8,72},{16,80},{24,88},{32,96},{40,104},{48,112},{56,120},{... | collective-permute-start | bytes 884744 | tf_op jit(solution)/shard_map/ppermute | solution.py:140
  116.7 0.0 copy-done.14
  116.7 0.0 collective-permute-done.9.refs_6_
  116.7 0.0 copy-start.7
  116.7 0.7 copy-done.7
  117.5 7.1 %collective-permute-done.10.refs_7_ = bf16[384,384]{1,0:T(8,128)(2,1)S(1)} collective-permute-done((bf16[384,384]{1,0:T(8,128)(2,1)S(1)}, bf16[384,384]{1,0:T(8,128)(2,1)S(1)}, u32[]{:S(2)}, u32[]{:S(2)}) %collective-permute-start.10) | collective-permute-done | bytes 294944 | tf_op jit(solution)/shard_map/ppermute | solution.py:140
  124.6 0.7 copy-done.9
  125.3 0.0 all-to-all-done.2.x_ref
  125.3 1.0 copy-done.8
  126.3 1.0 copy-done.10
  127.2 1.8 %shard_map.87 = bf16[256,384]{1,0:T(8,128)(2,1)} custom-call(f32[1,384]{1,0:T(1,128)S(1)} %reshape.9.gate_ref, bf16[8,256,384]{2,1,0:T(8,128)(2,1)S(1)} %all-to-all-done.2.x_ref, bf16[384,384]{1,0:T(8,128)(2,1)S(1)} %shard_map.86.refs_0_, bf16[384,384]{1,0:T(8,128)(2,1)S(1)} %collective-permute-done.4.refs_1_, ...), custom_call_target="tpu_custom_call" | custom-call | tf_op jit(solution)/shard_map/pallas_call | solution.py:124
  (7 shorter events, 0.0 us)
Async XLA Ops:
  0.0 0.9 copy-start
  0.9 0.9 copy-start.2
  1.9 0.9 copy-start.4
  2.8 0.7 copy-start.11
  3.5 16.8 %copy-start.15 = (s32[3,2,2]{0,2,1:T(2,128)S(1)}, s32[3,2,2]{0,2,1:T(2,128)}, u32[]{:S(2)}) copy-start(s32[3,2,2]{0,2,1:T(2,128)} %param.12) | copy-start | bytes 148
  3.5 44.9 %copy-start.6 = (bf16[48,384]{1,0:T(8,128)(2,1)S(1)}, bf16[48,384]{1,0:T(8,128)(2,1)}, u32[]{:S(2)}) copy-start(bf16[48,384]{1,0:T(8,128)(2,1)} %refs_0_.1) | copy-start | bytes 110596
  3.5 50.7 %copy-start.1 = (bf16[256,384]{1,0:T(8,128)(2,1)S(1)}, bf16[256,384]{1,0:T(8,128)(2,1)}, u32[]{:S(2)}) copy-start(bf16[256,384]{1,0:T(8,128)(2,1)} %q_ref.3) | copy-start | bytes 589828
  3.5 50.8 %copy-start.3 = (bf16[256,384]{1,0:T(8,128)(2,1)S(1)}, bf16[256,384]{1,0:T(8,128)(2,1)}, u32[]{:S(2)}) copy-start(bf16[256,384]{1,0:T(8,128)(2,1)} %k_ref.3) | copy-start | bytes 589828
  3.5 50.8 %copy-start.5 = (bf16[256,384]{1,0:T(8,128)(2,1)S(1)}, bf16[256,384]{1,0:T(8,128)(2,1)}, u32[]{:S(2)}) copy-start(bf16[256,384]{1,0:T(8,128)(2,1)} %v_ref.3) | copy-start | bytes 589828
  4.7 51.8 %copy-start.12 = (s32[256]{0:T(256)S(1)}, s32[256]{0:T(256)}, u32[]{:S(2)}) copy-start(s32[256]{0:T(256)} %param.13) | copy-start | bytes 3076
  4.7 51.8 %copy-start.13 = (s32[3]{0:T(128)S(1)}, s32[3]{0:T(128)}, u32[]{:S(2)}) copy-start(s32[3]{0:T(128)} %kinds_ref.1) | copy-start | bytes 40
  4.7 32.5 %all-to-all-start = ((bf16[64,4,1152]{2,1,0:T(4,128)(2,1)}), bf16[64,4,1152]{2,1,0:T(4,128)(2,1)S(1)}, u32[]{:S(2)}, u32[]{:S(2)}) async-start(bf16[64,4,1152]{2,1,0:T(4,128)(2,1)} %shard_map.82), calls=%async_computation | async-start | bytes 1179648 | tf_op jit(solution)/shard_map/all_to_all | solution.py:182
  39.3 17.3 %all-to-all-start.1 = ((bf16[64,4,384]{2,1,0:T(4,128)(2,1)}), bf16[64,4,384]{2,1,0:T(4,128)(2,1)S(1)}, u32[]{:S(2)}, u32[]{:S(2)}) async-start(bf16[64,4,384]{2,1,0:T(4,128)(2,1)} %shard_map.83), calls=%async_computation.1 | async-start | bytes 393216 | tf_op jit(solution)/shard_map/all_to_all | solution.py:185
  48.4 15.3 %collective-permute-start = (bf16[48,384]{1,0:T(8,128)(2,1)S(1)}, bf16[48,384]{1,0:T(8,128)(2,1)S(1)}, u32[]{:S(2)}, u32[]{:S(2)}) collective-permute-start(bf16[48,384]{1,0:T(8,128)(2,1)S(1)} %copy-done.6), channel_id=1, source_target_pairs={{0,8},{8,16},{16,24},{24,32},{32,40},{40,48},{48,56},{56,0},{64,72... | collective-permute-start | bytes 110600 | tf_op jit(solution)/shard_map/ppermute | solution.py:135
  51.7 11.9 %collective-permute-start.1 = (bf16[48,384]{1,0:T(8,128)(2,1)S(1)}, bf16[48,384]{1,0:T(8,128)(2,1)S(1)}, u32[]{:S(2)}, u32[]{:S(2)}) collective-permute-start(bf16[48,384]{1,0:T(8,128)(2,1)S(1)} %copy-done.6), channel_id=1, source_target_pairs={{0,56},{8,0},{16,8},{24,16},{32,24},{40,32},{48,40},{56,48},{64,12... | collective-permute-start | bytes 110600 | tf_op jit(solution)/shard_map/ppermute | solution.py:135
  58.6 58.0 %copy-start.14 = (f32[384]{0:T(512)S(1)}, f32[384]{0:T(512)}, u32[]{:S(2)}) copy-start(f32[384]{0:T(512)} %param.15) | copy-start | bytes 4612
  58.6 66.7 %all-to-all-start.2 = ((bf16[8,256,384]{2,1,0:T(8,128)(2,1)}), bf16[8,256,384]{2,1,0:T(8,128)(2,1)S(1)}, u32[]{:S(2)}, u32[]{:S(2)}) async-start(bf16[8,256,384]{2,1,0:T(8,128)(2,1)} %shard_map.85), calls=%async_computation.2 | async-start | bytes 3145728 | tf_op jit(solution)/shard_map/all_to_all | solution.py:189
  63.6 18.6 %collective-permute-start.2 = (bf16[144,384]{1,0:T(8,128)(2,1)S(1)}, bf16[144,384]{1,0:T(8,128)(2,1)S(1)}, u32[]{:S(2)}, u32[]{:S(2)}) collective-permute-start(bf16[144,384]{1,0:T(8,128)(2,1)S(1)} %pad_maximum_fusion), channel_id=1, source_target_pairs={{0,24},{8,32},{16,40},{24,48},{32,56},{40,0},{48,8},{56,16},{64,88... | collective-permute-start | bytes 331784 | tf_op jit(solution)/shard_map/ppermute | solution.py:135
  70.3 11.9 %collective-permute-start.3 = (bf16[96,384]{1,0:T(8,128)(2,1)S(1)}, bf16[96,384]{1,0:T(8,128)(2,1)S(1)}, u32[]{:S(2)}, u32[]{:S(2)}) collective-permute-start(bf16[96,384]{1,0:T(8,128)(2,1)S(1)} %pad_maximum_fusion.1), channel_id=1, source_target_pairs={{0,40},{8,48},{16,56},{24,0},{32,8},{40,16},{48,24},{56,32},{64,10... | collective-permute-start | bytes 221192 | tf_op jit(solution)/shard_map/ppermute | solution.py:135
  82.3 11.7 %collective-permute-start.4 = (bf16[384,384]{1,0:T(8,128)(2,1)S(1)}, bf16[384,384]{1,0:T(8,128)(2,1)S(1)}, u32[]{:S(2)}, u32[]{:S(2)}) collective-permute-start(bf16[384,384]{1,0:T(8,128)(2,1)S(1)} %shard_map.86.refs_0_), channel_id=1, source_target_pairs={{0,64},{8,72},{16,80},{24,88},{32,96},{40,104},{48,112},{56,120},{... | collective-permute-start | bytes 884744 | tf_op jit(solution)/shard_map/ppermute | solution.py:140
  84.8 11.1 %collective-permute-start.5 = (bf16[384,384]{1,0:T(8,128)(2,1)S(1)}, bf16[384,384]{1,0:T(8,128)(2,1)S(1)}, u32[]{:S(2)}, u32[]{:S(2)}) collective-permute-start(bf16[384,384]{1,0:T(8,128)(2,1)S(1)} %shard_map.86.refs_0_), channel_id=1, source_target_pairs={{0,448},{8,456},{16,464},{24,472},{32,480},{40,488},{48,496},{56,5... | collective-permute-start | bytes 884744 | tf_op jit(solution)/shard_map/ppermute | solution.py:140
  94.0 10.8 %collective-permute-start.6 = (bf16[384,384]{1,0:T(8,128)(2,1)S(1)}, bf16[384,384]{1,0:T(8,128)(2,1)S(1)}, u32[]{:S(2)}, u32[]{:S(2)}) collective-permute-start(bf16[384,384]{1,0:T(8,128)(2,1)S(1)} %collective-permute-done.4.refs_1_), channel_id=1, source_target_pairs={{0,64},{8,72},{16,80},{24,88},{32,96},{40,104},{48,112},{56,120},{... | collective-permute-start | bytes 884744 | tf_op jit(solution)/shard_map/ppermute | solution.py:140
  96.0 10.8 %collective-permute-start.7 = (bf16[384,384]{1,0:T(8,128)(2,1)S(1)}, bf16[384,384]{1,0:T(8,128)(2,1)S(1)}, u32[]{:S(2)}, u32[]{:S(2)}) collective-permute-start(bf16[384,384]{1,0:T(8,128)(2,1)S(1)} %collective-permute-done.5.refs_2_), channel_id=1, source_target_pairs={{0,448},{8,456},{16,464},{24,472},{32,480},{40,488},{48,496},{56,5... | collective-permute-start | bytes 884744 | tf_op jit(solution)/shard_map/ppermute | solution.py:140
  104.9 9.9 %collective-permute-start.8 = (bf16[384,384]{1,0:T(8,128)(2,1)S(1)}, bf16[384,384]{1,0:T(8,128)(2,1)S(1)}, u32[]{:S(2)}, u32[]{:S(2)}) collective-permute-start(bf16[384,384]{1,0:T(8,128)(2,1)S(1)} %collective-permute-done.6.refs_3_), channel_id=1, source_target_pairs={{0,64},{8,72},{16,80},{24,88},{32,96},{40,104},{48,112},{56,120},{... | collective-permute-start | bytes 884744 | tf_op jit(solution)/shard_map/ppermute | solution.py:140
  106.8 9.9 %collective-permute-start.9 = (bf16[384,384]{1,0:T(8,128)(2,1)S(1)}, bf16[384,384]{1,0:T(8,128)(2,1)S(1)}, u32[]{:S(2)}, u32[]{:S(2)}) collective-permute-start(bf16[384,384]{1,0:T(8,128)(2,1)S(1)} %collective-permute-done.7.refs_4_), channel_id=1, source_target_pairs={{0,448},{8,456},{16,464},{24,472},{32,480},{40,488},{48,496},{56,5... | collective-permute-start | bytes 884744 | tf_op jit(solution)/shard_map/ppermute | solution.py:140
  114.8 9.8 %collective-permute-start.10 = (bf16[384,384]{1,0:T(8,128)(2,1)S(1)}, bf16[384,384]{1,0:T(8,128)(2,1)S(1)}, u32[]{:S(2)}, u32[]{:S(2)}) collective-permute-start(bf16[384,384]{1,0:T(8,128)(2,1)S(1)} %collective-permute-done.8.refs_5_), channel_id=1, source_target_pairs={{0,64},{8,72},{16,80},{24,88},{32,96},{40,104},{48,112},{56,120},{... | collective-permute-start | bytes 884744 | tf_op jit(solution)/shard_map/ppermute | solution.py:140
  116.7 0.7 copy-start.7
  124.6 0.7 copy-start.9
  125.3 1.0 copy-start.8
  126.3 1.0 copy-start.10

commit v2 on v1

v2 whole, which is shorter than its diff:
```python
import math

import jax
import jax.numpy as jnp
from jax import lax
from jax.experimental import pallas as pl
from jax.experimental.pallas import tpu as pltpu
from jax.sharding import PartitionSpec as P

HBM = pl.BlockSpec(memory_space=pltpu.HBM)
VMEM = pl.BlockSpec(memory_space=pltpu.VMEM)
LANES = 128
COST = 20 * 10**9
SMEM = pl.BlockSpec(memory_space=pltpu.SMEM)


def placement(order, rows):
    positions = lax.broadcasted_iota(jnp.int32, (rows, rows), 0)
    return (positions == order).astype(jnp.float32).astype(jnp.bfloat16)


def ones_where(condition):
    return condition.astype(jnp.float32).astype(jnp.bfloat16)


def iotas(shape):
    return lax.broadcasted_iota(jnp.int32, shape, 0), lax.broadcasted_iota(jnp.int32, shape, 1)


def send_kernel(order_hbm, q_hbm, k_hbm, v_hbm, out_ref, order_ref, x_ref, sems):
    pairs = [(order_hbm, order_ref)]
    pairs += [(src, x_ref.at[i]) for i, src in enumerate((q_hbm, k_hbm, v_hbm))]
    copies = [pltpu.make_async_copy(src, dst, sems.at[i]) for i, (src, dst) in enumerate(pairs)]
    for copy in copies:
        copy.start()
    rows, width = x_ref.shape[1:]
    copies[0].wait()
    onehot = placement(order_ref[...], rows)
    for i in range(3):
        copies[1 + i].wait()
        picked = lax.dot_general(
            onehot, x_ref[i], (((0,), (0,)), ((), ())), preferred_element_type=jnp.float32
        )
        out_ref[:, :, i * width : (i + 1) * width] = picked.reshape(
            out_ref.shape[0], out_ref.shape[1], width
        ).astype(jnp.bfloat16)


def attend(q, k, v, masks, head, row_block, column_block):
    depth = q.shape[1]
    scores = lax.dot_general(q, k, (((1,), (1,)), ((), ())), preferred_element_type=jnp.float32)
    scores = scores * (1.0 / math.sqrt(depth))
    seen = [masks[4 * head + i] for i in range(4)]
    chosen = jnp.where(
        row_block == 0,
        jnp.where(column_block == 0, seen[0], seen[1]),
        jnp.where(column_block == 0, seen[2], seen[3]),
    )
    visible = chosen == 1
    scores = jnp.where(visible, scores, -jnp.inf)
    row_max = jnp.max(scores, axis=1, keepdims=True)
    weights = jnp.exp(scores - row_max)
    total = jnp.sum(weights, axis=1, keepdims=True)
    combined = jnp.dot(weights.astype(jnp.bfloat16), v, preferred_element_type=jnp.float32)
    return combined / total


def near_kernel(masks_ref, q_ref, k_ref, v_ref, out_ref):
    rows, width = q_ref.shape
    heads = masks_ref.shape[0] // 4
    depth = width // heads
    row_block = lax.broadcasted_iota(jnp.int32, (rows, rows), 0) // (rows // 2)
    column_block = lax.broadcasted_iota(jnp.int32, (rows, rows), 1) // (rows // 2)
    for h in range(heads):
        c = slice(h * depth, (h + 1) * depth)
        out_ref[:, c] = attend(
            q_ref[:, c], k_ref[:, c], v_ref[:, c], masks_ref, h, row_block, column_block
        ).astype(jnp.bfloat16)


def message_kernel(w_ref, out_ref):
    place, row = iotas((64, w_ref.shape[0]))
    pick = ones_where((place % 16 >= 4) & (row == 12 * (place // 16) + place % 16 - 4))
    got = jnp.dot(pick, w_ref[...], preferred_element_type=jnp.float32)
    out_ref[...] = got.reshape(out_ref.shape).astype(jnp.bfloat16)


def far_kernel(masks_ref, x_ref, weights_ref, after_hbm, out_ref):
    frames, group, wide = x_ref.shape
    rows, width = frames * group, wide // 3
    heads = masks_ref.shape[0] // 4
    row, column = iotas((rows, rows))
    row_block, column_block = row % group // (group // 2), column % group // (group // 2)
    at, row = iotas((8 * frames, rows))
    spread = ones_where((at % 8 < group) & (at // 8 * group + at % 8 == row))
    for h in range(heads):
        q, k, v = (
            x_ref[:, :, i * width + h * LANES : i * width + (h + 1) * LANES]
            .astype(jnp.float32)
            .reshape(rows, LANES)
            .astype(jnp.bfloat16)
            for i in range(3)
        )
        out = attend(q, k, v, masks_ref, h, row_block, column_block).astype(jnp.bfloat16)
        out = jnp.dot(spread, out, preferred_element_type=jnp.float32)
        c = slice(h * LANES, (h + 1) * LANES)
        weights = weights_ref[:, :, c].astype(jnp.float32).reshape(1, 2, 1, 2, 16, LANES)
        first = out.reshape(4, 2, 4, 2, 8, LANES) + weights[:, :, :, :, :8]
        rest = jnp.broadcast_to(weights[:, :, :, :, 8:], first.shape)
        out_ref[:, :8, c] = first.reshape(frames, 8, LANES).astype(jnp.bfloat16)
        out_ref[:, 8:, c] = rest.reshape(frames, 8, LANES).astype(jnp.bfloat16)


def part_kernel(x_ref, after_hbm, out_ref):
    n, part, width = out_ref.shape
    row, at = iotas((part, 16 * n))
    take = ones_where(row // 12 * 16 + 4 + row % 12 == at)
    for y in range(n):
        block = x_ref[y * n : (y + 1) * n].astype(jnp.float32).reshape(16 * n, width)
        got = jnp.dot(take, block.astype(jnp.bfloat16), preferred_element_type=jnp.float32)
        out_ref[y] = got.astype(jnp.bfloat16)


def select_kernel(kinds_ref, order_ref, far_ref, near_ref, out_ref):
    rows, width = near_ref.shape
    frames = far_ref.shape[0]
    heads = kinds_ref.shape[0]
    row, at = iotas((rows, 8 * frames))
    take = ones_where(row // 4 * 8 + row % 4 == at)
    far = far_ref[:, :8, :].astype(jnp.float32).reshape(8 * frames, width).astype(jnp.bfloat16)
    far = jnp.dot(take, far, preferred_element_type=jnp.float32).astype(jnp.bfloat16)
    back = jnp.dot(placement(order_ref[...], rows), far, preferred_element_type=jnp.float32)
    place = lax.broadcasted_iota(jnp.int32, (1, width), 1)
    quarter = sum((place >= edge).astype(jnp.int32) for edge in (96, 192, 288))
    left = place - 96 * quarter
    z = sum((left >= 12 * i).astype(jnp.int32) for i in range(1, 8))
    column = 48 * z + 12 * quarter + left - 12 * z
    total = None
    for h in range(heads):
        c = slice(h * LANES, (h + 1) * LANES)
        near = near_ref[:, c].astype(jnp.float32)
        chosen = jnp.where(kinds_ref[h] == 1, back[:, c], near).astype(jnp.bfloat16)
        old = lax.broadcasted_iota(jnp.int32, (LANES, width), 0) + h * LANES
        moved = jnp.dot(chosen, ones_where(old == column), preferred_element_type=jnp.float32)
        total = moved if total is None else total + moved
    total = total.astype(jnp.bfloat16)
    for m in range(out_ref.shape[0]):
        out_ref[m] = total


def weight_kernel(own_ref, z_ref, y_ref, both_ref, out_ref):
    seq = lax.axis_index("seq")
    y, z = lax.rem(seq // 8, 2), lax.rem(seq, 2)
    part = own_ref.shape[1]
    for at_y, at_z, ref in (
        (y, z, own_ref),
        (y, 1 - z, z_ref),
        (1 - y, z, y_ref),
        (1 - y, 1 - z, both_ref),
    ):
        rows = pl.ds(pl.multiple_of((2 * at_y + at_z) * part, part), part)
        out_ref[:, rows, :] = ref[...]


def project_kernel(gate_ref, x_ref, others_ref, w_ref, out_ref):
    core = lax.rem(lax.axis_index("mlp"), 2)
    total = None
    for ref, parity in ((x_ref, core), (others_ref, 1 - core)):
        for x in range(x_ref.shape[0]):
            got = jnp.dot(ref[x], w_ref[2 * x + parity], preferred_element_type=jnp.float32)
            total = got if total is None else total + got
    out_ref[...] = (gate_ref[...] * total).astype(jnp.bfloat16)


def call(kernel, shape, specs, *args, scratch=(), limit=16, dtype=jnp.bfloat16, cost=None):
    return pl.pallas_call(
        kernel,
        out_shape=jax.ShapeDtypeStruct(shape, dtype),
        in_specs=specs,
        out_specs=VMEM,
        scratch_shapes=scratch,
        compiler_params=pltpu.CompilerParams(vmem_limit_bytes=limit * 1024 * 1024),
        cost_estimate=cost,
    )(*args)


def fetch(block, dy, dz):
    pairs = [
        ((y + dy) % 8 * 8 + (z + dz) % 8, 8 * y + z) for y in range(8) for z in range(8)
    ]
    return lax.ppermute(block, "seq", pairs)


def local(
    queries, key_vectors, value_vectors, head_kinds, block_masks, order_map, out_weight, gate_values
):
    rows, width = queries.shape
    frames = lax.axis_size("seq")
    parts = lax.axis_size("mlp")
    group = rows // frames
    masks = block_masks.reshape(-1)
    order = order_map.reshape(1, rows)
    sent = call(
        send_kernel,
        (frames, group, 3 * width),
        [HBM] * 4,
        order,
        queries,
        key_vectors,
        value_vectors,
        scratch=[
            pltpu.VMEM((1, rows), jnp.int32),
            pltpu.VMEM((3, rows, width), jnp.bfloat16),
            pltpu.SemaphoreType.DMA((4,)),
        ],
        limit=60,
    )
    moved = lax.all_to_all(sent, "seq", split_axis=0, concat_axis=0, tiled=True)
    near = call(near_kernel, (rows, width), [SMEM] + [VMEM] * 3, masks, queries, key_vectors, value_vectors)
    pieces = call(message_kernel, (4, 16, width), [VMEM], out_weight)
    far = call(
        far_kernel, (frames, 16, width), [SMEM, VMEM, VMEM, HBM], masks, moved, pieces, near
    )
    returned = lax.all_to_all(far, "seq", split_axis=0, concat_axis=0, tiled=True)

    attended = call(
        select_kernel,
        (parts // 2, rows, width),
        [SMEM] + [VMEM] * 3,
        head_kinds,
        order,
        returned,
        near,
    )
    own = call(part_kernel, (parts, 96, width), [VMEM, HBM], returned, attended)
    others = [fetch(own, dy, dz) for dy, dz in ((0, 1), (1, 0), (-1, -1))]
    columns = lax.all_to_all(
        attended,
        "mlp",
        split_axis=0,
        concat_axis=0,
        axis_index_groups=[[0, 2, 4, 6], [1, 3, 5, 7]],
        tiled=True,
    )
    others_columns = lax.ppermute(columns, "mlp", [(i, i ^ 1) for i in range(parts)])
    weight = call(
        weight_kernel,
        (parts, width, width),
        [VMEM] * 4,
        own,
        *others,
        cost=pl.CostEstimate(flops=COST, bytes_accessed=0, transcendentals=0),
    )
    return call(
        project_kernel,
        (rows, width),
        [VMEM] * 4,
        gate_values.reshape(1, width),
        columns,
        others_columns,
        weight,
    )


def solution(mesh):
    in_specs = (
        P("seq", "mlp"),
        P("seq", "mlp"),
        P("seq", "mlp"),
        P("mlp"),
        P("mlp", None, None),
        P(),
        P("seq", "mlp"),
        P("mlp"),
    )
    out_specs = P("seq", "mlp")
    return jax.shard_map(local, mesh=mesh, in_specs=in_specs, out_specs=out_specs, check_vma=False)
```

time: 130 us -> 104 us (0.80)
  the two profiles are of different devices: /device:TPU:98 before, /device:TPU:2 now
where the time goes in v2:
time: 104 us
  starting transfers between devices  32.6 us (31%)
  waiting for transfers between devices  31.1 us (30%)
  blocking collectives  29 us (28%)
  Pallas kernels  10.5 us (10%)
    all_to_all x1, blocking collectives, local(): lax.all_to_all(far, 'seq', split_axis=0, concat_axis=0, tiled=True)  29 us
    all_to_all x1, waiting for transfers between devices, local(): moved = lax.all_to_all(sent, 'seq', split_axis=0, concat_axis=0, tiled=True)  18.7 us
    all_to_all x1, starting transfers between devices, local(): moved = lax.all_to_all(sent, 'seq', split_axis=0, concat_axis=0, tiled=True)  16.6 us
    ppermute x3, waiting for transfers between devices, fetch(): return lax.ppermute(block, 'seq', pairs)  12.4 us
    pallas_call x8, Pallas kernels, call(): pl.pallas_call(kernel, out_shape=jax.ShapeDtypeStruct(shape, dtype), in_s...  10.5 us
    ppermute x3, starting transfers between devices, fetch(): return lax.ppermute(block, 'seq', pairs)  9.21 us
    all_to_all x1, starting transfers between devices, local(): lax.all_to_all(attended, 'mlp', split_axis=0, concat_axis=0, axis_index_g...  4.84 us
  transfers between devices with their start and end apart: 6, of which 4 were waited for; matrix products, arithmetic and copies ran while one was open for 0% of the time, Pallas kernels for 2%

profile of v2, /device:TPU:2, one launch (start us, length us, event | category | flops | bytes accessed | tf_op | source)
XLA Modules:
  0.0 103.7 jit_solution(13941473836444004121)
XLA Ops:
  0.0 0.0 copy-start.2
  0.0 0.0 copy-start
  0.0 0.0 copy-start.1
  0.0 0.0 copy-start.7
  0.0 0.0 copy-start.3
  0.0 2.6 %shard_map.82 = bf16[64,4,1152]{2,1,0:T(4,128)(2,1)} custom-call(s32[1,256]{1,0:T(1,128)} %bitcast.1, bf16[256,384]{1,0:T(8,128)(2,1)} %q_ref.1, bf16[256,384]{1,0:T(8,128)(2,1)} %k_ref.1, bf16[256,384]{1,0:T(8,128)(2,1)} %v_ref.1), custom_call_target="tpu_custom_call" | custom-call | tf_op jit(solution)/shard_map/pallas_call | solution.py:176
  2.6 0.0 copy-start.4
  2.6 0.0 copy-start.5
  2.6 16.6 %all-to-all-start = ((bf16[64,4,1152]{2,1,0:T(4,128)(2,1)}), bf16[64,4,1152]{2,1,0:T(4,128)(2,1)S(1)}, u32[]{:S(2)}, u32[]{:S(2)}) async-start(bf16[64,4,1152]{2,1,0:T(4,128)(2,1)} %shard_map.82), calls=%async_computation | async-start | bytes 1179648 | tf_op jit(solution)/shard_map/all_to_all | solution.py:218
  19.2 0.0 copy-done.7
  19.3 0.1 copy.10
  19.4 0.1 reshape.11.masks_ref
  19.4 0.0 copy-done.2
  19.4 0.0 copy-done
  19.4 0.0 copy-done.1
  19.5 1.3 %shard_map.84.after_hbm.near_ref = bf16[256,384]{1,0:T(8,128)(2,1)S(1)} custom-call(s32[12]{0:T(128)S(1)} %reshape.11.masks_ref, bf16[256,384]{1,0:T(8,128)(2,1)S(1)} %copy-done, bf16[256,384]{1,0:T(8,128)(2,1)S(1)} %copy-done.1, bf16[256,384]{1,0:T(8,128)(2,1)S(1)} %copy-done.2), custom_call_target="tpu_custom_call" | custom-call | tf_op jit(solution)/shard_map/pallas_call | solution.py:176
  20.8 0.0 copy-done.3
  20.8 0.1 shard_map.83.weights_ref
  20.9 18.7 %all-to-all-done.x_ref = bf16[64,4,1152]{2,1,0:T(4,128)(2,1)S(1)} async-done(((bf16[64,4,1152]{2,1,0:T(4,128)(2,1)}), bf16[64,4,1152]{2,1,0:T(4,128)(2,1)S(1)}, u32[]{:S(2)}, u32[]{:S(2)}) %all-to-all-start) | async-done | bytes 589856 | tf_op jit(solution)/shard_map/all_to_all | solution.py:218
  39.6 2.0 %shard_map.85 = bf16[64,16,384]{2,1,0:T(8,128)(2,1)S(1)} custom-call(s32[12]{0:T(128)S(1)} %reshape.11.masks_ref, bf16[64,4,1152]{2,1,0:T(4,128)(2,1)S(1)} %all-to-all-done.x_ref, bf16[4,16,384]{2,1,0:T(8,128)(2,1)S(1)} %shard_map.83.weights_ref, bf16[256,384]{1,0:T(8,128)(2,1)S(1)} %shard_map.84.after_hbm.near_ref), custom_call_target="tpu_custom_call" | custom-call | tf_op jit(solution)/shard_map/pallas_call | solution.py:176
  41.6 29.0 %all_to_all.15.far_ref.x_ref = bf16[64,16,384]{2,1,0:T(8,128)(2,1)S(1)} all-to-all(bf16[64,16,384]{2,1,0:T(8,128)(2,1)S(1)} %shard_map.85), channel_id=1, replica_groups=mesh['seq'=64,'mlp'=8] {'seq'}, dimensions={0} | all-to-all | bytes 1572864 | tf_op jit(solution)/shard_map/all_to_all | solution.py:224
  70.6 0.0 copy-done.4
  70.6 0.0 copy-done.5
  70.6 0.0 copy-start.6
  70.6 2.2 %shard_map.86.after_hbm = bf16[4,256,384]{2,1,0:T(8,128)(2,1)} custom-call(s32[3]{0:T(128)S(1)} %copy-done.5, s32[1,256]{1,0:T(1,128)S(1)} %bitcast.2, bf16[64,16,384]{2,1,0:T(8,128)(2,1)S(1)} %all_to_all.15.far_ref.x_ref, bf16[256,384]{1,0:T(8,128)(2,1)S(1)} %shard_map.84.after_hbm.near_ref), custom_call_target="tpu_custom_call" | custom-call | tf_op jit(solution)/shard_map/pallas_call | solution.py:176
  72.8 4.8 %all-to-all-start.2 = ((bf16[4,256,384]{2,1,0:T(8,128)(2,1)}), bf16[4,256,384]{2,1,0:T(8,128)(2,1)S(1)}, u32[]{:S(2)}, u32[]{:S(2)}) async-start(bf16[4,256,384]{2,1,0:T(8,128)(2,1)} %shard_map.86.after_hbm), calls=%async_computation.2 | async-start | bytes 1572864 | tf_op jit(solution)/shard_map/all_to_all | solution.py:237
  77.7 0.3 shard_map.87.own_ref
  78.0 3.6 %collective-permute-start.1 = (bf16[8,96,384]{2,1,0:T(8,128)(2,1)S(1)}, bf16[8,96,384]{2,1,0:T(8,128)(2,1)S(1)}, u32[]{:S(2)}, u32[]{:S(2)}) collective-permute-start(bf16[8,96,384]{2,1,0:T(8,128)(2,1)S(1)} %shard_map.87.own_ref), channel_id=1, source_target_pairs={{8,0},{16,8},{24,16},{32,24},{40,32},{48,40},{56,48},{0,56},{72,64... | collective-permute-start | bytes 1769480 | tf_op jit(solution)/shard_map/ppermute | solution.py:191
  81.6 2.6 %collective-permute-start.2 = (bf16[8,96,384]{2,1,0:T(8,128)(2,1)S(1)}, bf16[8,96,384]{2,1,0:T(8,128)(2,1)S(1)}, u32[]{:S(2)}, u32[]{:S(2)}) collective-permute-start(bf16[8,96,384]{2,1,0:T(8,128)(2,1)S(1)} %shard_map.87.own_ref), channel_id=1, source_target_pairs={{64,0},{72,8},{80,16},{88,24},{96,32},{104,40},{112,48},{120,56},{... | collective-permute-start | bytes 1769480 | tf_op jit(solution)/shard_map/ppermute | solution.py:191
  84.1 3.1 %collective-permute-start.3 = (bf16[8,96,384]{2,1,0:T(8,128)(2,1)S(1)}, bf16[8,96,384]{2,1,0:T(8,128)(2,1)S(1)}, u32[]{:S(2)}, u32[]{:S(2)}) collective-permute-start(bf16[8,96,384]{2,1,0:T(8,128)(2,1)S(1)} %shard_map.87.own_ref), channel_id=1, source_target_pairs={{504,0},{448,8},{456,16},{464,24},{472,32},{480,40},{488,48},{496,... | collective-permute-start | bytes 1769480 | tf_op jit(solution)/shard_map/ppermute | solution.py:191
  87.2 0.0 copy-done.6
  87.2 0.0 all-to-all-done.2.x_ref
  87.3 1.9 %collective-permute-start = (bf16[4,256,384]{2,1,0:T(8,128)(2,1)S(1)}, bf16[4,256,384]{2,1,0:T(8,128)(2,1)S(1)}, u32[]{:S(2)}, u32[]{:S(2)}) collective-permute-start(bf16[4,256,384]{2,1,0:T(8,128)(2,1)S(1)} %all-to-all-done.2.x_ref), channel_id=1, source_target_pairs={{0,1},{1,0},{2,3},{3,2},{4,5},{5,4},{6,7},{7,6},{8,9},{9,8},{10,11... | collective-permute-start | bytes 2359304 | tf_op jit(solution)/shard_map/ppermute | solution.py:245
  89.2 2.2 %collective-permute-done.1.z_ref = bf16[8,96,384]{2,1,0:T(8,128)(2,1)S(1)} collective-permute-done((bf16[8,96,384]{2,1,0:T(8,128)(2,1)S(1)}, bf16[8,96,384]{2,1,0:T(8,128)(2,1)S(1)}, u32[]{:S(2)}, u32[]{:S(2)}) %collective-permute-start.1) | collective-permute-done | bytes 589856 | tf_op jit(solution)/shard_map/ppermute | solution.py:191
  91.4 4.1 %collective-permute-done.2.y_ref = bf16[8,96,384]{2,1,0:T(8,128)(2,1)S(1)} collective-permute-done((bf16[8,96,384]{2,1,0:T(8,128)(2,1)S(1)}, bf16[8,96,384]{2,1,0:T(8,128)(2,1)S(1)}, u32[]{:S(2)}, u32[]{:S(2)}) %collective-permute-start.2) | collective-permute-done | bytes 589856 | tf_op jit(solution)/shard_map/ppermute | solution.py:191
  95.5 6.1 %collective-permute-done.3.both_ref = bf16[8,96,384]{2,1,0:T(8,128)(2,1)S(1)} collective-permute-done((bf16[8,96,384]{2,1,0:T(8,128)(2,1)S(1)}, bf16[8,96,384]{2,1,0:T(8,128)(2,1)S(1)}, u32[]{:S(2)}, u32[]{:S(2)}) %collective-permute-start.3) | collective-permute-done | bytes 589856 | tf_op jit(solution)/shard_map/ppermute | solution.py:191
  101.6 0.2 shard_map.88.w_ref
  101.9 0.0 collective-permute-done.others_ref
  101.9 1.8 %shard_map.89 = bf16[256,384]{1,0:T(8,128)(2,1)} custom-call(f32[1,384]{1,0:T(1,128)S(1)} %reshape.9.gate_ref, bf16[4,256,384]{2,1,0:T(8,128)(2,1)S(1)} %all-to-all-done.2.x_ref, bf16[4,256,384]{2,1,0:T(8,128)(2,1)S(1)} %collective-permute-done.others_ref, bf16[8,384,384]{2,1,0:T(8,128)(2,1)S(1)} %shard_map.88.w_ref), custom_call_target="tpu_custom_call" | custom-call | tf_op jit(solution)/shard_map/pallas_call | solution.py:176
  (1 shorter events, 0.0 us)
Async XLA Ops:
  0.0 19.4 %copy-start.2 = (bf16[256,384]{1,0:T(8,128)(2,1)S(1)}, bf16[256,384]{1,0:T(8,128)(2,1)}, u32[]{:S(2)}) copy-start(bf16[256,384]{1,0:T(8,128)(2,1)} %v_ref.1) | copy-start | bytes 589828
  0.0 19.4 %copy-start = (bf16[256,384]{1,0:T(8,128)(2,1)S(1)}, bf16[256,384]{1,0:T(8,128)(2,1)}, u32[]{:S(2)}) copy-start(bf16[256,384]{1,0:T(8,128)(2,1)} %q_ref.1) | copy-start | bytes 589828
  0.0 19.4 %copy-start.1 = (bf16[256,384]{1,0:T(8,128)(2,1)S(1)}, bf16[256,384]{1,0:T(8,128)(2,1)}, u32[]{:S(2)}) copy-start(bf16[256,384]{1,0:T(8,128)(2,1)} %k_ref.1) | copy-start | bytes 589828
  0.0 19.2 %copy-start.7 = (s32[3,2,2]{0,2,1:T(2,128)S(1)}, s32[3,2,2]{0,2,1:T(2,128)}, u32[]{:S(2)}) copy-start(s32[3,2,2]{0,2,1:T(2,128)} %param.12) | copy-start | bytes 148
  0.0 20.7 %copy-start.3 = (bf16[48,384]{1,0:T(8,128)(2,1)S(1)}, bf16[48,384]{1,0:T(8,128)(2,1)}, u32[]{:S(2)}) copy-start(bf16[48,384]{1,0:T(8,128)(2,1)} %w_ref.1) | copy-start | bytes 110596
  2.6 68.0 %copy-start.4 = (s32[256]{0:T(256)S(1)}, s32[256]{0:T(256)}, u32[]{:S(2)}) copy-start(s32[256]{0:T(256)} %param.13) | copy-start | bytes 3076
  2.6 68.0 %copy-start.5 = (s32[3]{0:T(128)S(1)}, s32[3]{0:T(128)}, u32[]{:S(2)}) copy-start(s32[3]{0:T(128)} %kinds_ref.1) | copy-start | bytes 40
  2.6 37.0 %all-to-all-start = ((bf16[64,4,1152]{2,1,0:T(4,128)(2,1)}), bf16[64,4,1152]{2,1,0:T(4,128)(2,1)S(1)}, u32[]{:S(2)}, u32[]{:S(2)}) async-start(bf16[64,4,1152]{2,1,0:T(4,128)(2,1)} %shard_map.82), calls=%async_computation | async-start | bytes 1179648 | tf_op jit(solution)/shard_map/all_to_all | solution.py:218
  70.6 16.6 %copy-start.6 = (f32[384]{0:T(512)S(1)}, f32[384]{0:T(512)}, u32[]{:S(2)}) copy-start(f32[384]{0:T(512)} %param.15) | copy-start | bytes 4612
  72.8 14.4 %all-to-all-start.2 = ((bf16[4,256,384]{2,1,0:T(8,128)(2,1)}), bf16[4,256,384]{2,1,0:T(8,128)(2,1)S(1)}, u32[]{:S(2)}, u32[]{:S(2)}) async-start(bf16[4,256,384]{2,1,0:T(8,128)(2,1)} %shard_map.86.after_hbm), calls=%async_computation.2 | async-start | bytes 1572864 | tf_op jit(solution)/shard_map/all_to_all | solution.py:237
  78.0 13.4 %collective-permute-start.1 = (bf16[8,96,384]{2,1,0:T(8,128)(2,1)S(1)}, bf16[8,96,384]{2,1,0:T(8,128)(2,1)S(1)}, u32[]{:S(2)}, u32[]{:S(2)}) collective-permute-start(bf16[8,96,384]{2,1,0:T(8,128)(2,1)S(1)} %shard_map.87.own_ref), channel_id=1, source_target_pairs={{8,0},{16,8},{24,16},{32,24},{40,32},{48,40},{56,48},{0,56},{72,64... | collective-permute-start | bytes 1769480 | tf_op jit(solution)/shard_map/ppermute | solution.py:191
  81.6 13.9 %collective-permute-start.2 = (bf16[8,96,384]{2,1,0:T(8,128)(2,1)S(1)}, bf16[8,96,384]{2,1,0:T(8,128)(2,1)S(1)}, u32[]{:S(2)}, u32[]{:S(2)}) collective-permute-start(bf16[8,96,384]{2,1,0:T(8,128)(2,1)S(1)} %shard_map.87.own_ref), channel_id=1, source_target_pairs={{64,0},{72,8},{80,16},{88,24},{96,32},{104,40},{112,48},{120,56},{... | collective-permute-start | bytes 1769480 | tf_op jit(solution)/shard_map/ppermute | solution.py:191
  84.1 17.5 %collective-permute-start.3 = (bf16[8,96,384]{2,1,0:T(8,128)(2,1)S(1)}, bf16[8,96,384]{2,1,0:T(8,128)(2,1)S(1)}, u32[]{:S(2)}, u32[]{:S(2)}) collective-permute-start(bf16[8,96,384]{2,1,0:T(8,128)(2,1)S(1)} %shard_map.87.own_ref), channel_id=1, source_target_pairs={{504,0},{448,8},{456,16},{464,24},{472,32},{480,40},{488,48},{496,... | collective-permute-start | bytes 1769480 | tf_op jit(solution)/shard_map/ppermute | solution.py:191
  87.3 14.6 %collective-permute-start = (bf16[4,256,384]{2,1,0:T(8,128)(2,1)S(1)}, bf16[4,256,384]{2,1,0:T(8,128)(2,1)S(1)}, u32[]{:S(2)}, u32[]{:S(2)}) collective-permute-start(bf16[4,256,384]{2,1,0:T(8,128)(2,1)S(1)} %all-to-all-done.2.x_ref), channel_id=1, source_target_pairs={{0,1},{1,0},{2,3},{3,2},{4,5},{5,4},{6,7},{7,6},{8,9},{9,8},{10,11... | collective-permute-start | bytes 2359304 | tf_op jit(solution)/shard_map/ppermute | solution.py:245

commit v3 on v2

--- a/solution.py
+++ b/solution.py
@@ -78,9 +78,15 @@
         ).astype(jnp.bfloat16)
 
 
+def quarter_of(core, y, z):
+    return jnp.where(core == 0, z + 2 * y, 2 * z + y) % 4
+
+
 def message_kernel(w_ref, out_ref):
-    place, row = iotas((64, w_ref.shape[0]))
-    pick = ones_where((place % 16 >= 4) & (row == 12 * (place // 16) + place % 16 - 4))
+    core = lax.rem(lax.axis_index("mlp"), 2)
+    place, row = iotas((256, w_ref.shape[0]))
+    first = 12 * quarter_of(core, place // 64, place // 16 % 4)
+    pick = ones_where((place % 16 >= 4) & (row == first + place % 16 - 4))
     got = jnp.dot(pick, w_ref[...], preferred_element_type=jnp.float32)
     out_ref[...] = got.reshape(out_ref.shape).astype(jnp.bfloat16)
 
@@ -104,8 +110,8 @@
         out = attend(q, k, v, masks_ref, h, row_block, column_block).astype(jnp.bfloat16)
         out = jnp.dot(spread, out, preferred_element_type=jnp.float32)
         c = slice(h * LANES, (h + 1) * LANES)
-        weights = weights_ref[:, :, c].astype(jnp.float32).reshape(1, 2, 1, 2, 16, LANES)
-        first = out.reshape(4, 2, 4, 2, 8, LANES) + weights[:, :, :, :, :8]
+        weights = weights_ref[:, :, c].astype(jnp.float32).reshape(1, 4, 1, 4, 16, LANES)
+        first = out.reshape(2, 4, 2, 4, 8, LANES) + weights[:, :, :, :, :8]
         rest = jnp.broadcast_to(weights[:, :, :, :, 8:], first.shape)
         out_ref[:, :8, c] = first.reshape(frames, 8, LANES).astype(jnp.bfloat16)
         out_ref[:, 8:, c] = rest.reshape(frames, 8, LANES).astype(jnp.bfloat16)
@@ -123,13 +129,8 @@
 
 def select_kernel(kinds_ref, order_ref, far_ref, near_ref, out_ref):
     rows, width = near_ref.shape
-    frames = far_ref.shape[0]
     heads = kinds_ref.shape[0]
-    row, at = iotas((rows, 8 * frames))
-    take = ones_where(row // 4 * 8 + row % 4 == at)
-    far = far_ref[:, :8, :].astype(jnp.float32).reshape(8 * frames, width).astype(jnp.bfloat16)
-    far = jnp.dot(take, far, preferred_element_type=jnp.float32).astype(jnp.bfloat16)
-    back = jnp.dot(placement(order_ref[...], rows), far, preferred_element_type=jnp.float32)
+    onehot = placement(order_ref[...], rows)
     place = lax.broadcasted_iota(jnp.int32, (1, width), 1)
     quarter = sum((place >= edge).astype(jnp.int32) for edge in (96, 192, 288))
     left = place - 96 * quarter
@@ -138,8 +139,10 @@
     total = None
     for h in range(heads):
         c = slice(h * LANES, (h + 1) * LANES)
+        far = far_ref[:, :8, c].astype(jnp.float32)[:, :4].reshape(rows, LANES)
+        back = jnp.dot(onehot, far.astype(jnp.bfloat16), preferred_element_type=jnp.float32)
         near = near_ref[:, c].astype(jnp.float32)
-        chosen = jnp.where(kinds_ref[h] == 1, back[:, c], near).astype(jnp.bfloat16)
+        chosen = jnp.where(kinds_ref[h] == 1, back, near).astype(jnp.bfloat16)
         old = lax.broadcasted_iota(jnp.int32, (LANES, width), 0) + h * LANES
         moved = jnp.dot(chosen, ones_where(old == column), preferred_element_type=jnp.float32)
         total = moved if total is None else total + moved
@@ -148,17 +151,12 @@
         out_ref[m] = total
 
 
-def weight_kernel(own_ref, z_ref, y_ref, both_ref, out_ref):
+def weight_kernel(own_ref, next_ref, last_ref, second_ref, out_ref):
     seq = lax.axis_index("seq")
-    y, z = lax.rem(seq // 8, 2), lax.rem(seq, 2)
+    quarter = quarter_of(lax.rem(lax.axis_index("mlp"), 2), seq // 8, lax.rem(seq, 8))
     part = own_ref.shape[1]
-    for at_y, at_z, ref in (
-        (y, z, own_ref),
-        (y, 1 - z, z_ref),
-        (1 - y, z, y_ref),
-        (1 - y, 1 - z, both_ref),
-    ):
-        rows = pl.ds(pl.multiple_of((2 * at_y + at_z) * part, part), part)
+    for step, ref in ((0, own_ref), (1, next_ref), (3, last_ref), (2, second_ref)):
+        rows = pl.ds(pl.multiple_of(lax.rem(quarter + step, 4) * part, part), part)
         out_ref[:, rows, :] = ref[...]
 
 
@@ -166,8 +164,10 @@
     core = lax.rem(lax.axis_index("mlp"), 2)
     total = None
     for ref, parity in ((x_ref, core), (others_ref, 1 - core)):
-        for x in range(x_ref.shape[0]):
-            got = jnp.dot(ref[x], w_ref[2 * x + parity], preferred_element_type=jnp.float32)
+        for x in range(0, x_ref.shape[0], 2):
+            heads = jnp.concatenate([ref[x], ref[x + 1]], axis=1)
+            weight = jnp.concatenate([w_ref[2 * x + parity], w_ref[2 * x + 2 + parity]], axis=0)
+            got = jnp.dot(heads, weight, preferred_element_type=jnp.float32)
             total = got if total is None else total + got
     out_ref[...] = (gate_ref[...] * total).astype(jnp.bfloat16)
 
@@ -184,11 +184,15 @@
     )(*args)
 
 
-def fetch(block, dy, dz):
-    pairs = [
-        ((y + dy) % 8 * 8 + (z + dz) % 8, 8 * y + z) for y in range(8) for z in range(8)
-    ]
-    return lax.ppermute(block, "seq", pairs)
+def fetch(block, offsets):
+    pairs = []
+    for y in range(8):
+        for z in range(8):
+            for m in range(8):
+                dy, dz = offsets[m % 2]
+                source = (y + dy) % 8 * 8 + (z + dz) % 8
+                pairs.append((8 * source + m, 8 * (8 * y + z) + m))
+    return lax.ppermute(block, ("seq", "mlp"), pairs)
 
 
 def local(
@@ -217,7 +221,7 @@
     )
     moved = lax.all_to_all(sent, "seq", split_axis=0, concat_axis=0, tiled=True)
     near = call(near_kernel, (rows, width), [SMEM] + [VMEM] * 3, masks, queries, key_vectors, value_vectors)
-    pieces = call(message_kernel, (4, 16, width), [VMEM], out_weight)
+    pieces = call(message_kernel, (16, 16, width), [VMEM], out_weight)
     far = call(
         far_kernel, (frames, 16, width), [SMEM, VMEM, VMEM, HBM], masks, moved, pieces, near
     )
@@ -233,7 +237,9 @@
         near,
     )
     own = call(part_kernel, (parts, 96, width), [VMEM, HBM], returned, attended)
-    others = [fetch(own, dy, dz) for dy, dz in ((0, 1), (1, 0), (-1, -1))]
+    others = [
+        fetch(own, offsets) for offsets in (((0, 1), (1, 0)), ((0, -1), (-1, 0)), ((1, 0), (0, 1)))
+    ]
     columns = lax.all_to_all(
         attended,
         "mlp",

time: 104 us -> 99 us (0.952)
  the two profiles are of different devices: /device:TPU:2 before, /device:TPU:19 now
where the time goes in v3:
time: 99 us; the launch traced here: 98.6 us
  starting transfers between devices  33.9 us (34%)
  blocking collectives  28.9 us (29%)
  waiting for transfers between devices  25.1 us (25%)
  Pallas kernels  10.4 us (11%)
    all_to_all x1, blocking collectives, local(): lax.all_to_all(far, 'seq', split_axis=0, concat_axis=0, tiled=True)  28.9 us
    all_to_all x1, waiting for transfers between devices, local(): moved = lax.all_to_all(sent, 'seq', split_axis=0, concat_axis=0, tiled=True)  17.4 us
    all_to_all x1, starting transfers between devices, local(): moved = lax.all_to_all(sent, 'seq', split_axis=0, concat_axis=0, tiled=True)  15.9 us
    pallas_call x8, Pallas kernels, call(): pl.pallas_call(kernel, out_shape=jax.ShapeDtypeStruct(shape, dtype), in_s...  10.4 us
    ppermute x3, waiting for transfers between devices, fetch(): return lax.ppermute(block, ('seq', 'mlp'), pairs)  7.66 us
    ppermute x3, starting transfers between devices, fetch(): return lax.ppermute(block, ('seq', 'mlp'), pairs)  7.2 us
    ppermute x1, starting transfers between devices, local(): lax.ppermute(columns, 'mlp', [(i, i ^ 1) for i in range(parts)])  6.44 us
    all_to_all x1, starting transfers between devices, local(): lax.all_to_all(attended, 'mlp', split_axis=0, concat_axis=0, axis_index_g...  4.28 us
  transfers between devices with their start and end apart: 6, of which 2 were waited for; matrix products, arithmetic and copies ran while one was open for 0% of the time, Pallas kernels for 2%

profile of v3, /device:TPU:19, one launch (start us, length us, event | category | flops | bytes accessed | tf_op | source)
XLA Modules:
  0.0 98.6 jit_solution(10971303558782920375)
XLA Ops:
  0.0 0.0 copy-start.2
  0.0 0.0 copy-start
  0.0 0.0 copy-start.1
  0.0 0.0 copy-start.7
  0.0 0.0 copy-start.3
  0.0 2.6 %shard_map.82 = bf16[64,4,1152]{2,1,0:T(4,128)(2,1)} custom-call(s32[1,256]{1,0:T(1,128)} %bitcast.1, bf16[256,384]{1,0:T(8,128)(2,1)} %q_ref.1, bf16[256,384]{1,0:T(8,128)(2,1)} %k_ref.1, bf16[256,384]{1,0:T(8,128)(2,1)} %v_ref.1), custom_call_target="tpu_custom_call" | custom-call | tf_op jit(solution)/shard_map/pallas_call | solution.py:176
  2.6 15.9 %all-to-all-start = ((bf16[64,4,1152]{2,1,0:T(4,128)(2,1)}), bf16[64,4,1152]{2,1,0:T(4,128)(2,1)S(1)}, u32[]{:S(2)}, u32[]{:S(2)}) async-start(bf16[64,4,1152]{2,1,0:T(4,128)(2,1)} %shard_map.82), calls=%async_computation | async-start | bytes 1179648 | tf_op jit(solution)/shard_map/all_to_all | solution.py:222
  18.5 0.0 copy-done.7
  18.6 0.0 copy-start.4
  18.6 0.0 copy-start.5
  18.6 0.1 copy.10
  18.7 0.1 reshape.11.masks_ref
  18.8 0.0 copy-done.2
  18.8 0.0 copy-done
  18.8 0.0 copy-done.1
  18.8 1.3 %shard_map.84.after_hbm.near_ref = bf16[256,384]{1,0:T(8,128)(2,1)S(1)} custom-call(s32[12]{0:T(128)S(1)} %reshape.11.masks_ref, bf16[256,384]{1,0:T(8,128)(2,1)S(1)} %copy-done, bf16[256,384]{1,0:T(8,128)(2,1)S(1)} %copy-done.1, bf16[256,384]{1,0:T(8,128)(2,1)S(1)} %copy-done.2), custom_call_target="tpu_custom_call" | custom-call | tf_op jit(solution)/shard_map/pallas_call | solution.py:176
  20.1 0.0 copy-done.3
  20.1 0.2 shard_map.83.weights_ref
  20.4 17.4 %all-to-all-done.x_ref = bf16[64,4,1152]{2,1,0:T(4,128)(2,1)S(1)} async-done(((bf16[64,4,1152]{2,1,0:T(4,128)(2,1)}), bf16[64,4,1152]{2,1,0:T(4,128)(2,1)S(1)}, u32[]{:S(2)}, u32[]{:S(2)}) %all-to-all-start) | async-done | bytes 589856 | tf_op jit(solution)/shard_map/all_to_all | solution.py:222
  37.8 2.0 %shard_map.85 = bf16[64,16,384]{2,1,0:T(8,128)(2,1)S(1)} custom-call(s32[12]{0:T(128)S(1)} %reshape.11.masks_ref, bf16[64,4,1152]{2,1,0:T(4,128)(2,1)S(1)} %all-to-all-done.x_ref, bf16[16,16,384]{2,1,0:T(8,128)(2,1)S(1)} %shard_map.83.weights_ref, bf16[256,384]{1,0:T(8,128)(2,1)S(1)} %shard_map.84.after_hbm.near_ref), custom_call_target="tpu_custom_call" | custom-call | tf_op jit(solution)/shard_map/pallas_call | solution.py:176
  39.7 28.9 %all_to_all.15.far_ref.x_ref = bf16[64,16,384]{2,1,0:T(8,128)(2,1)S(1)} all-to-all(bf16[64,16,384]{2,1,0:T(8,128)(2,1)S(1)} %shard_map.85), channel_id=1, replica_groups=mesh['seq'=64,'mlp'=8] {'seq'}, dimensions={0} | all-to-all | bytes 1572864 | tf_op jit(solution)/shard_map/all_to_all | solution.py:228
  68.7 0.0 copy-done.4
  68.7 0.0 copy-done.5
  68.7 0.0 copy-start.6
  68.7 2.0 %shard_map.86.after_hbm = bf16[4,256,384]{2,1,0:T(8,128)(2,1)} custom-call(s32[3]{0:T(128)S(1)} %copy-done.5, s32[1,256]{1,0:T(1,128)S(1)} %bitcast.2, bf16[64,16,384]{2,1,0:T(8,128)(2,1)S(1)} %all_to_all.15.far_ref.x_ref, bf16[256,384]{1,0:T(8,128)(2,1)S(1)} %shard_map.84.after_hbm.near_ref), custom_call_target="tpu_custom_call" | custom-call | tf_op jit(solution)/shard_map/pallas_call | solution.py:176
  70.7 4.3 %all-to-all-start.2 = ((bf16[4,256,384]{2,1,0:T(8,128)(2,1)}), bf16[4,256,384]{2,1,0:T(8,128)(2,1)S(1)}, u32[]{:S(2)}, u32[]{:S(2)}) async-start(bf16[4,256,384]{2,1,0:T(8,128)(2,1)} %shard_map.86.after_hbm), calls=%async_computation.2 | async-start | bytes 1572864 | tf_op jit(solution)/shard_map/all_to_all | solution.py:243
  75.0 0.3 shard_map.87.own_ref
  75.3 1.9 %collective-permute-start.1 = (bf16[8,96,384]{2,1,0:T(8,128)(2,1)S(1)}, bf16[8,96,384]{2,1,0:T(8,128)(2,1)S(1)}, u32[]{:S(2)}, u32[]{:S(2)}) collective-permute-start(bf16[8,96,384]{2,1,0:T(8,128)(2,1)S(1)} %shard_map.87.own_ref), channel_id=1, source_target_pairs={{8,0},{65,1},{10,2},{67,3},{12,4},{69,5},{14,6},{71,7},{16,8},{73,... | collective-permute-start | bytes 1769480 | tf_op jit(solution)/shard_map/ppermute | solution.py:195
  77.3 3.4 %collective-permute-start.2 = (bf16[8,96,384]{2,1,0:T(8,128)(2,1)S(1)}, bf16[8,96,384]{2,1,0:T(8,128)(2,1)S(1)}, u32[]{:S(2)}, u32[]{:S(2)}) collective-permute-start(bf16[8,96,384]{2,1,0:T(8,128)(2,1)S(1)} %shard_map.87.own_ref), channel_id=1, source_target_pairs={{56,0},{449,1},{58,2},{451,3},{60,4},{453,5},{62,6},{455,7},{0,8},... | collective-permute-start | bytes 1769480 | tf_op jit(solution)/shard_map/ppermute | solution.py:195
  80.6 1.9 %collective-permute-start.3 = (bf16[8,96,384]{2,1,0:T(8,128)(2,1)S(1)}, bf16[8,96,384]{2,1,0:T(8,128)(2,1)S(1)}, u32[]{:S(2)}, u32[]{:S(2)}) collective-permute-start(bf16[8,96,384]{2,1,0:T(8,128)(2,1)S(1)} %shard_map.87.own_ref), channel_id=1, source_target_pairs={{64,0},{9,1},{66,2},{11,3},{68,4},{13,5},{70,6},{15,7},{72,8},{17,... | collective-permute-start | bytes 1769480 | tf_op jit(solution)/shard_map/ppermute | solution.py:195
  82.6 0.0 copy-done.6
  82.6 0.0 all-to-all-done.2.x_ref
  82.6 6.4 %collective-permute-start = (bf16[4,256,384]{2,1,0:T(8,128)(2,1)S(1)}, bf16[4,256,384]{2,1,0:T(8,128)(2,1)S(1)}, u32[]{:S(2)}, u32[]{:S(2)}) collective-permute-start(bf16[4,256,384]{2,1,0:T(8,128)(2,1)S(1)} %all-to-all-done.2.x_ref), channel_id=1, source_target_pairs={{0,1},{1,0},{2,3},{3,2},{4,5},{5,4},{6,7},{7,6},{8,9},{9,8},{10,11... | collective-permute-start | bytes 2359304 | tf_op jit(solution)/shard_map/ppermute | solution.py:251
  89.0 0.0 collective-permute-done.1.next_ref
  89.0 0.0 collective-permute-done.2.last_ref
  89.1 7.7 %collective-permute-done.3.second_ref = bf16[8,96,384]{2,1,0:T(8,128)(2,1)S(1)} collective-permute-done((bf16[8,96,384]{2,1,0:T(8,128)(2,1)S(1)}, bf16[8,96,384]{2,1,0:T(8,128)(2,1)S(1)}, u32[]{:S(2)}, u32[]{:S(2)}) %collective-permute-start.3) | collective-permute-done | bytes 589856 | tf_op jit(solution)/shard_map/ppermute | solution.py:195
  96.7 0.2 shard_map.88.w_ref
  97.0 0.0 collective-permute-done.others_ref
  97.0 1.7 %shard_map.89 = bf16[256,384]{1,0:T(8,128)(2,1)} custom-call(f32[1,384]{1,0:T(1,128)S(1)} %reshape.9.gate_ref, bf16[4,256,384]{2,1,0:T(8,128)(2,1)S(1)} %all-to-all-done.2.x_ref, bf16[4,256,384]{2,1,0:T(8,128)(2,1)S(1)} %collective-permute-done.others_ref, bf16[8,384,384]{2,1,0:T(8,128)(2,1)S(1)} %shard_map.88.w_ref), custom_call_target="tpu_custom_call" | custom-call | tf_op jit(solution)/shard_map/pallas_call | solution.py:176
  (1 shorter events, 0.0 us)
Async XLA Ops:
  0.0 18.8 %copy-start.2 = (bf16[256,384]{1,0:T(8,128)(2,1)S(1)}, bf16[256,384]{1,0:T(8,128)(2,1)}, u32[]{:S(2)}) copy-start(bf16[256,384]{1,0:T(8,128)(2,1)} %v_ref.1) | copy-start | bytes 589828
  0.0 18.8 %copy-start = (bf16[256,384]{1,0:T(8,128)(2,1)S(1)}, bf16[256,384]{1,0:T(8,128)(2,1)}, u32[]{:S(2)}) copy-start(bf16[256,384]{1,0:T(8,128)(2,1)} %q_ref.1) | copy-start | bytes 589828
  0.0 18.8 %copy-start.1 = (bf16[256,384]{1,0:T(8,128)(2,1)S(1)}, bf16[256,384]{1,0:T(8,128)(2,1)}, u32[]{:S(2)}) copy-start(bf16[256,384]{1,0:T(8,128)(2,1)} %k_ref.1) | copy-start | bytes 589828
  0.0 18.5 %copy-start.7 = (s32[3,2,2]{0,2,1:T(2,128)S(1)}, s32[3,2,2]{0,2,1:T(2,128)}, u32[]{:S(2)}) copy-start(s32[3,2,2]{0,2,1:T(2,128)} %param.12) | copy-start | bytes 148
  0.0 20.1 %copy-start.3 = (bf16[48,384]{1,0:T(8,128)(2,1)S(1)}, bf16[48,384]{1,0:T(8,128)(2,1)}, u32[]{:S(2)}) copy-start(bf16[48,384]{1,0:T(8,128)(2,1)} %w_ref.1) | copy-start | bytes 110596
  2.6 35.1 %all-to-all-start = ((bf16[64,4,1152]{2,1,0:T(4,128)(2,1)}), bf16[64,4,1152]{2,1,0:T(4,128)(2,1)S(1)}, u32[]{:S(2)}, u32[]{:S(2)}) async-start(bf16[64,4,1152]{2,1,0:T(4,128)(2,1)} %shard_map.82), calls=%async_computation | async-start | bytes 1179648 | tf_op jit(solution)/shard_map/all_to_all | solution.py:222
  18.6 50.1 %copy-start.4 = (s32[256]{0:T(256)S(1)}, s32[256]{0:T(256)}, u32[]{:S(2)}) copy-start(s32[256]{0:T(256)} %param.13) | copy-start | bytes 3076
  18.6 50.1 %copy-start.5 = (s32[3]{0:T(128)S(1)}, s32[3]{0:T(128)}, u32[]{:S(2)}) copy-start(s32[3]{0:T(128)} %kinds_ref.1) | copy-start | bytes 40
  68.7 13.9 %copy-start.6 = (f32[384]{0:T(512)S(1)}, f32[384]{0:T(512)}, u32[]{:S(2)}) copy-start(f32[384]{0:T(512)} %param.15) | copy-start | bytes 4612
  70.7 11.9 %all-to-all-start.2 = ((bf16[4,256,384]{2,1,0:T(8,128)(2,1)}), bf16[4,256,384]{2,1,0:T(8,128)(2,1)S(1)}, u32[]{:S(2)}, u32[]{:S(2)}) async-start(bf16[4,256,384]{2,1,0:T(8,128)(2,1)} %shard_map.86.after_hbm), calls=%async_computation.2 | async-start | bytes 1572864 | tf_op jit(solution)/shard_map/all_to_all | solution.py:243
  75.3 13.7 %collective-permute-start.1 = (bf16[8,96,384]{2,1,0:T(8,128)(2,1)S(1)}, bf16[8,96,384]{2,1,0:T(8,128)(2,1)S(1)}, u32[]{:S(2)}, u32[]{:S(2)}) collective-permute-start(bf16[8,96,384]{2,1,0:T(8,128)(2,1)S(1)} %shard_map.87.own_ref), channel_id=1, source_target_pairs={{8,0},{65,1},{10,2},{67,3},{12,4},{69,5},{14,6},{71,7},{16,8},{73,... | collective-permute-start | bytes 1769480 | tf_op jit(solution)/shard_map/ppermute | solution.py:195
  77.3 11.8 %collective-permute-start.2 = (bf16[8,96,384]{2,1,0:T(8,128)(2,1)S(1)}, bf16[8,96,384]{2,1,0:T(8,128)(2,1)S(1)}, u32[]{:S(2)}, u32[]{:S(2)}) collective-permute-start(bf16[8,96,384]{2,1,0:T(8,128)(2,1)S(1)} %shard_map.87.own_ref), channel_id=1, source_target_pairs={{56,0},{449,1},{58,2},{451,3},{60,4},{453,5},{62,6},{455,7},{0,8},... | collective-permute-start | bytes 1769480 | tf_op jit(solution)/shard_map/ppermute | solution.py:195
  80.6 16.1 %collective-permute-start.3 = (bf16[8,96,384]{2,1,0:T(8,128)(2,1)S(1)}, bf16[8,96,384]{2,1,0:T(8,128)(2,1)S(1)}, u32[]{:S(2)}, u32[]{:S(2)}) collective-permute-start(bf16[8,96,384]{2,1,0:T(8,128)(2,1)S(1)} %shard_map.87.own_ref), channel_id=1, source_target_pairs={{64,0},{9,1},{66,2},{11,3},{68,4},{13,5},{70,6},{15,7},{72,8},{17,... | collective-permute-start | bytes 1769480 | tf_op jit(solution)/shard_map/ppermute | solution.py:195
  82.6 14.4 %collective-permute-start = (bf16[4,256,384]{2,1,0:T(8,128)(2,1)S(1)}, bf16[4,256,384]{2,1,0:T(8,128)(2,1)S(1)}, u32[]{:S(2)}, u32[]{:S(2)}) collective-permute-start(bf16[4,256,384]{2,1,0:T(8,128)(2,1)S(1)} %all-to-all-done.2.x_ref), channel_id=1, source_target_pairs={{0,1},{1,0},{2,3},{3,2},{4,5},{5,4},{6,7},{7,6},{8,9},{9,8},{10,11... | collective-permute-start | bytes 2359304 | tf_op jit(solution)/shard_map/ppermute | solution.py:251

commit v4 on v3

--- a/solution.py
+++ b/solution.py
@@ -27,7 +27,9 @@
     return lax.broadcasted_iota(jnp.int32, shape, 0), lax.broadcasted_iota(jnp.int32, shape, 1)
 
 
-def send_kernel(order_hbm, q_hbm, k_hbm, v_hbm, out_ref, order_ref, x_ref, sems):
+def send_kernel(
+    order_hbm, q_hbm, k_hbm, v_hbm, out_hbm, order_ref, x_ref, out_ref, sems, out_sems
+):
     pairs = [(order_hbm, order_ref)]
     pairs += [(src, x_ref.at[i]) for i, src in enumerate((q_hbm, k_hbm, v_hbm))]
     copies = [pltpu.make_async_copy(src, dst, sems.at[i]) for i, (src, dst) in enumerate(pairs)]
@@ -36,14 +38,22 @@
     rows, width = x_ref.shape[1:]
     copies[0].wait()
     onehot = placement(order_ref[...], rows)
+    outs = []
     for i in range(3):
+        c = slice(i * width, (i + 1) * width)
         copies[1 + i].wait()
         picked = lax.dot_general(
             onehot, x_ref[i], (((0,), (0,)), ((), ())), preferred_element_type=jnp.float32
         )
-        out_ref[:, :, i * width : (i + 1) * width] = picked.reshape(
-            out_ref.shape[0], out_ref.shape[1], width
-        ).astype(jnp.bfloat16)
+        out_ref[:, :, c] = picked.reshape(out_ref.shape[0], out_ref.shape[1], width).astype(
+            jnp.bfloat16
+        )
+        outs.append(
+            pltpu.make_async_copy(out_ref.at[:, :, c], out_hbm.at[:, :, c], out_sems.at[i])
+        )
+        outs[-1].start()
+    for copy in outs:
+        copy.wait()
 
 
 def attend(q, k, v, masks, head, row_block, column_block):
@@ -110,24 +120,16 @@
         out = attend(q, k, v, masks_ref, h, row_block, column_block).astype(jnp.bfloat16)
         out = jnp.dot(spread, out, preferred_element_type=jnp.float32)
         c = slice(h * LANES, (h + 1) * LANES)
-        weights = weights_ref[:, :, c].astype(jnp.float32).reshape(1, 4, 1, 4, 16, LANES)
-        first = out.reshape(2, 4, 2, 4, 8, LANES) + weights[:, :, :, :, :8]
+        weights = weights_ref[:, :, c].reshape(1, 4, 1, 4, 16, LANES)
+        first = out.reshape(2, 4, 2, 4, 8, LANES) + weights[:, :, :, :, :8].astype(jnp.float32)
         rest = jnp.broadcast_to(weights[:, :, :, :, 8:], first.shape)
         out_ref[:, :8, c] = first.reshape(frames, 8, LANES).astype(jnp.bfloat16)
-        out_ref[:, 8:, c] = rest.reshape(frames, 8, LANES).astype(jnp.bfloat16)
-
-
-def part_kernel(x_ref, after_hbm, out_ref):
-    n, part, width = out_ref.shape
-    row, at = iotas((part, 16 * n))
-    take = ones_where(row // 12 * 16 + 4 + row % 12 == at)
-    for y in range(n):
-        block = x_ref[y * n : (y + 1) * n].astype(jnp.float32).reshape(16 * n, width)
-        got = jnp.dot(take, block.astype(jnp.bfloat16), preferred_element_type=jnp.float32)
-        out_ref[y] = got.astype(jnp.bfloat16)
-
-
-def select_kernel(kinds_ref, order_ref, far_ref, near_ref, out_ref):
+        out_ref[:, 8:, c] = rest.reshape(frames, 8, LANES)
+
+
+def select_kernel(
+    kinds_ref, order_ref, far_ref, near_ref, out_hbm, own_ref, out_ref, sems
+):
     rows, width = near_ref.shape
     heads = kinds_ref.shape[0]
     onehot = placement(order_ref[...], rows)
@@ -146,9 +148,21 @@
         old = lax.broadcasted_iota(jnp.int32, (LANES, width), 0) + h * LANES
         moved = jnp.dot(chosen, ones_where(old == column), preferred_element_type=jnp.float32)
         total = moved if total is None else total + moved
-    total = total.astype(jnp.bfloat16)
-    for m in range(out_ref.shape[0]):
-        out_ref[m] = total
+    out_ref[...] = total.astype(jnp.bfloat16)
+    copies = [
+        pltpu.make_async_copy(out_ref, out_hbm.at[x], sems.at[x]) for x in range(out_hbm.shape[0])
+    ]
+    for copy in copies:
+        copy.start()
+    n, part = own_ref.shape[:2]
+    row, at = iotas((part, 16 * n))
+    take = ones_where(row // 12 * 16 + 4 + row % 12 == at)
+    for y in range(n):
+        block = far_ref[y * n : (y + 1) * n].astype(jnp.float32).reshape(16 * n, width)
+        got = jnp.dot(take, block.astype(jnp.bfloat16), preferred_element_type=jnp.float32)
+        own_ref[y] = got.astype(jnp.bfloat16)
+    for copy in copies:
+        copy.wait()
 
 
 def weight_kernel(own_ref, next_ref, last_ref, second_ref, out_ref):
@@ -172,12 +186,14 @@
     out_ref[...] = (gate_ref[...] * total).astype(jnp.bfloat16)
 
 
-def call(kernel, shape, specs, *args, scratch=(), limit=16, dtype=jnp.bfloat16, cost=None):
+def call(kernel, shape, specs, *args, out=VMEM, scratch=(), limit=16, cost=None):
+    shapes = shape if isinstance(shape, list) else [shape]
+    shapes = [jax.ShapeDtypeStruct(one, jnp.bfloat16) for one in shapes]
     return pl.pallas_call(
         kernel,
-        out_shape=jax.ShapeDtypeStruct(shape, dtype),
+        out_shape=shapes if isinstance(shape, list) else shapes[0],
         in_specs=specs,
-        out_specs=VMEM,
+        out_specs=out,
         scratch_shapes=scratch,
         compiler_params=pltpu.CompilerParams(vmem_limit_bytes=limit * 1024 * 1024),
         cost_estimate=cost,
@@ -215,8 +231,11 @@
         scratch=[
             pltpu.VMEM((1, rows), jnp.int32),
             pltpu.VMEM((3, rows, width), jnp.bfloat16),
+            pltpu.VMEM((frames, group, 3 * width), jnp.bfloat16),
             pltpu.SemaphoreType.DMA((4,)),
+            pltpu.SemaphoreType.DMA((3,)),
         ],
+        out=HBM,
         limit=60,
     )
     moved = lax.all_to_all(sent, "seq", split_axis=0, concat_axis=0, tiled=True)
@@ -227,16 +246,17 @@
     )
     returned = lax.all_to_all(far, "seq", split_axis=0, concat_axis=0, tiled=True)
 
-    attended = call(
+    attended, own = call(
         select_kernel,
-        (parts // 2, rows, width),
+        [(parts // 2, rows, width), (parts, 96, width)],
         [SMEM] + [VMEM] * 3,
         head_kinds,
         order,
         returned,
         near,
-    )
-    own = call(part_kernel, (parts, 96, width), [VMEM, HBM], returned, attended)
+        out=[HBM, VMEM],
+        scratch=[pltpu.VMEM((rows, width), jnp.bfloat16), pltpu.SemaphoreType.DMA((parts // 2,))],
+    )
     others = [
         fetch(own, offsets) for offsets in (((0, 1), (1, 0)), ((0, -1), (-1, 0)), ((1, 0), (0, 1)))
     ]

time: 99 us -> 98.6 us (level)
    pallas_call x8 -> x7, Pallas kernels: 10.4 us -> 9.96 us  [call(): pl.pallas_call(kernel, out_shape=shapes if isinstance(shape, list) else s...]
where the time goes in v4:
time: 98.6 us; the launch traced here: 98.2 us
  starting transfers between devices  34.1 us (35%)
  blocking collectives  28.9 us (29%)
  waiting for transfers between devices  24.8 us (25%)
  Pallas kernels  9.96 us (10%)
    all_to_all x1, blocking collectives, local(): lax.all_to_all(far, 'seq', split_axis=0, concat_axis=0, tiled=True)  28.9 us
    all_to_all x1, waiting for transfers between devices, local(): moved = lax.all_to_all(sent, 'seq', split_axis=0, concat_axis=0, tiled=True)  17.4 us
    all_to_all x1, starting transfers between devices, local(): moved = lax.all_to_all(sent, 'seq', split_axis=0, concat_axis=0, tiled=True)  15.9 us
    pallas_call x7, Pallas kernels, call(): pl.pallas_call(kernel, out_shape=shapes if isinstance(shape, list) else s...  9.96 us
    ppermute x3, waiting for transfers between devices, fetch(): return lax.ppermute(block, ('seq', 'mlp'), pairs)  7.38 us
    ppermute x3, starting transfers between devices, fetch(): return lax.ppermute(block, ('seq', 'mlp'), pairs)  7.19 us
    ppermute x1, starting transfers between devices, local(): lax.ppermute(columns, 'mlp', [(i, i ^ 1) for i in range(parts)])  6.71 us
    all_to_all x1, starting transfers between devices, local(): lax.all_to_all(attended, 'mlp', split_axis=0, concat_axis=0, axis_index_g...  4.29 us
  transfers between devices with their start and end apart: 6, of which 2 were waited for; matrix products, arithmetic and copies ran while one was open for 0% of the time, Pallas kernels for 2%

profile of v4, /device:TPU:19, one launch (start us, length us, event | category | flops | bytes accessed | tf_op | source)
XLA Modules:
  0.0 98.2 jit_solution(12214951041028457810)
XLA Ops:
  0.0 0.0 copy-start.2
  0.0 0.0 copy-start
  0.0 0.0 copy-start.1
  0.0 0.0 copy-start.7
  0.0 0.0 copy-start.3
  0.0 2.5 %shard_map.82 = bf16[64,4,1152]{2,1,0:T(4,128)(2,1)} custom-call(s32[1,256]{1,0:T(1,128)} %bitcast.1, bf16[256,384]{1,0:T(8,128)(2,1)} %q_ref.1, bf16[256,384]{1,0:T(8,128)(2,1)} %k_ref.1, bf16[256,384]{1,0:T(8,128)(2,1)} %v_ref.1), custom_call_target="tpu_custom_call" | custom-call | tf_op jit(solution)/shard_map/pallas_call | solution.py:192
  2.5 15.9 %all-to-all-start = ((bf16[64,4,1152]{2,1,0:T(4,128)(2,1)}), bf16[64,4,1152]{2,1,0:T(4,128)(2,1)S(1)}, u32[]{:S(2)}, u32[]{:S(2)}) async-start(bf16[64,4,1152]{2,1,0:T(4,128)(2,1)} %shard_map.82), calls=%async_computation | async-start | bytes 1179648 | tf_op jit(solution)/shard_map/all_to_all | solution.py:241
  18.5 0.0 copy-done.7
  18.5 0.0 copy-start.4
  18.5 0.0 copy-start.5
  18.5 0.1 copy.10
  18.6 0.1 reshape.11.masks_ref
  18.7 0.0 copy-done.2
  18.7 0.0 copy-done
  18.7 0.0 copy-done.1
  18.7 1.3 %shard_map.84.after_hbm.near_ref = bf16[256,384]{1,0:T(8,128)(2,1)S(1)} custom-call(s32[12]{0:T(128)S(1)} %reshape.11.masks_ref, bf16[256,384]{1,0:T(8,128)(2,1)S(1)} %copy-done, bf16[256,384]{1,0:T(8,128)(2,1)S(1)} %copy-done.1, bf16[256,384]{1,0:T(8,128)(2,1)S(1)} %copy-done.2), custom_call_target="tpu_custom_call" | custom-call | tf_op jit(solution)/shard_map/pallas_call | solution.py:192
  20.0 0.0 copy-done.3
  20.0 0.3 shard_map.83.weights_ref
  20.3 17.4 %all-to-all-done.x_ref = bf16[64,4,1152]{2,1,0:T(4,128)(2,1)S(1)} async-done(((bf16[64,4,1152]{2,1,0:T(4,128)(2,1)}), bf16[64,4,1152]{2,1,0:T(4,128)(2,1)S(1)}, u32[]{:S(2)}, u32[]{:S(2)}) %all-to-all-start) | async-done | bytes 589856 | tf_op jit(solution)/shard_map/all_to_all | solution.py:241
  37.7 2.0 %shard_map.85 = bf16[64,16,384]{2,1,0:T(8,128)(2,1)S(1)} custom-call(s32[12]{0:T(128)S(1)} %reshape.11.masks_ref, bf16[64,4,1152]{2,1,0:T(4,128)(2,1)S(1)} %all-to-all-done.x_ref, bf16[16,16,384]{2,1,0:T(8,128)(2,1)S(1)} %shard_map.83.weights_ref, bf16[256,384]{1,0:T(8,128)(2,1)S(1)} %shard_map.84.after_hbm.near_ref), custom_call_target="tpu_custom_call" | custom-call | tf_op jit(solution)/shard_map/pallas_call | solution.py:192
  39.6 0.0 copy-start.6
  39.6 28.9 %all_to_all.15.far_ref = bf16[64,16,384]{2,1,0:T(8,128)(2,1)S(1)} all-to-all(bf16[64,16,384]{2,1,0:T(8,128)(2,1)S(1)} %shard_map.85), channel_id=1, replica_groups=mesh['seq'=64,'mlp'=8] {'seq'}, dimensions={0} | all-to-all | bytes 1572864 | tf_op jit(solution)/shard_map/all_to_all | solution.py:247
  68.6 0.0 copy-done.4
  68.6 0.0 copy-done.5
  68.6 2.0 %shard_map.86 = (bf16[4,256,384]{2,1,0:T(8,128)(2,1)}, bf16[8,96,384]{2,1,0:T(8,128)(2,1)S(1)}) custom-call(s32[3]{0:T(128)S(1)} %copy-done.5, s32[1,256]{1,0:T(1,128)S(1)} %bitcast.2, bf16[64,16,384]{2,1,0:T(8,128)(2,1)S(1)} %all_to_all.15.far_ref, bf16[256,384]{1,0:T(8,128)(2,1)S(1)} %shard_map.84.after_hbm.near_ref), custom_call_target="tpu_custom_call" | custom-call | tf_op jit(solution)/shard_map/pallas_call | solution.py:192
  70.7 4.3 %all-to-all-start.2 = ((bf16[4,256,384]{2,1,0:T(8,128)(2,1)}), bf16[4,256,384]{2,1,0:T(8,128)(2,1)S(1)}, u32[]{:S(2)}, u32[]{:S(2)}) async-start(bf16[4,256,384]{2,1,0:T(8,128)(2,1)} %get-tuple-element.7), calls=%async_computation.2 | async-start | bytes 1572864 | tf_op jit(solution)/shard_map/all_to_all | solution.py:263
  74.9 1.9 %collective-permute-start.1 = (bf16[8,96,384]{2,1,0:T(8,128)(2,1)S(1)}, bf16[8,96,384]{2,1,0:T(8,128)(2,1)S(1)}, u32[]{:S(2)}, u32[]{:S(2)}) collective-permute-start(bf16[8,96,384]{2,1,0:T(8,128)(2,1)S(1)} %get-tuple-element.8.own_ref), channel_id=1, source_target_pairs={{8,0},{65,1},{10,2},{67,3},{12,4},{69,5},{14,6},{71,7},{16,8},{73,... | collective-permute-start | bytes 1769480 | tf_op jit(solution)/shard_map/ppermute | solution.py:211
  76.9 3.4 %collective-permute-start.2 = (bf16[8,96,384]{2,1,0:T(8,128)(2,1)S(1)}, bf16[8,96,384]{2,1,0:T(8,128)(2,1)S(1)}, u32[]{:S(2)}, u32[]{:S(2)}) collective-permute-start(bf16[8,96,384]{2,1,0:T(8,128)(2,1)S(1)} %get-tuple-element.8.own_ref), channel_id=1, source_target_pairs={{56,0},{449,1},{58,2},{451,3},{60,4},{453,5},{62,6},{455,7},{0,8},... | collective-permute-start | bytes 1769480 | tf_op jit(solution)/shard_map/ppermute | solution.py:211
  80.2 1.9 %collective-permute-start.3 = (bf16[8,96,384]{2,1,0:T(8,128)(2,1)S(1)}, bf16[8,96,384]{2,1,0:T(8,128)(2,1)S(1)}, u32[]{:S(2)}, u32[]{:S(2)}) collective-permute-start(bf16[8,96,384]{2,1,0:T(8,128)(2,1)S(1)} %get-tuple-element.8.own_ref), channel_id=1, source_target_pairs={{64,0},{9,1},{66,2},{11,3},{68,4},{13,5},{70,6},{15,7},{72,8},{17,... | collective-permute-start | bytes 1769480 | tf_op jit(solution)/shard_map/ppermute | solution.py:211
  82.2 0.0 copy-done.6
  82.2 0.0 all-to-all-done.2.x_ref
  82.2 6.7 %collective-permute-start = (bf16[4,256,384]{2,1,0:T(8,128)(2,1)S(1)}, bf16[4,256,384]{2,1,0:T(8,128)(2,1)S(1)}, u32[]{:S(2)}, u32[]{:S(2)}) collective-permute-start(bf16[4,256,384]{2,1,0:T(8,128)(2,1)S(1)} %all-to-all-done.2.x_ref), channel_id=1, source_target_pairs={{0,1},{1,0},{2,3},{3,2},{4,5},{5,4},{6,7},{7,6},{8,9},{9,8},{10,11... | collective-permute-start | bytes 2359304 | tf_op jit(solution)/shard_map/ppermute | solution.py:271
  88.9 0.0 collective-permute-done.1.next_ref
  88.9 0.0 collective-permute-done.2.last_ref
  88.9 7.4 %collective-permute-done.3.second_ref = bf16[8,96,384]{2,1,0:T(8,128)(2,1)S(1)} collective-permute-done((bf16[8,96,384]{2,1,0:T(8,128)(2,1)S(1)}, bf16[8,96,384]{2,1,0:T(8,128)(2,1)S(1)}, u32[]{:S(2)}, u32[]{:S(2)}) %collective-permute-start.3) | collective-permute-done | bytes 589856 | tf_op jit(solution)/shard_map/ppermute | solution.py:211
  96.3 0.2 shard_map.87.w_ref
  96.6 0.0 collective-permute-done.others_ref
  96.6 1.7 %shard_map.88 = bf16[256,384]{1,0:T(8,128)(2,1)} custom-call(f32[1,384]{1,0:T(1,128)S(1)} %reshape.9.gate_ref, bf16[4,256,384]{2,1,0:T(8,128)(2,1)S(1)} %all-to-all-done.2.x_ref, bf16[4,256,384]{2,1,0:T(8,128)(2,1)S(1)} %collective-permute-done.others_ref, bf16[8,384,384]{2,1,0:T(8,128)(2,1)S(1)} %shard_map.87.w_ref), custom_call_target="tpu_custom_call" | custom-call | tf_op jit(solution)/shard_map/pallas_call | solution.py:192
  (1 shorter events, 0.0 us)
Async XLA Ops:
  0.0 18.7 %copy-start.2 = (bf16[256,384]{1,0:T(8,128)(2,1)S(1)}, bf16[256,384]{1,0:T(8,128)(2,1)}, u32[]{:S(2)}) copy-start(bf16[256,384]{1,0:T(8,128)(2,1)} %v_ref.1) | copy-start | bytes 589828
  0.0 18.7 %copy-start = (bf16[256,384]{1,0:T(8,128)(2,1)S(1)}, bf16[256,384]{1,0:T(8,128)(2,1)}, u32[]{:S(2)}) copy-start(bf16[256,384]{1,0:T(8,128)(2,1)} %q_ref.1) | copy-start | bytes 589828
  0.0 18.7 %copy-start.1 = (bf16[256,384]{1,0:T(8,128)(2,1)S(1)}, bf16[256,384]{1,0:T(8,128)(2,1)}, u32[]{:S(2)}) copy-start(bf16[256,384]{1,0:T(8,128)(2,1)} %k_ref.1) | copy-start | bytes 589828
  0.0 18.4 %copy-start.7 = (s32[3,2,2]{0,2,1:T(2,128)S(1)}, s32[3,2,2]{0,2,1:T(2,128)}, u32[]{:S(2)}) copy-start(s32[3,2,2]{0,2,1:T(2,128)} %param.12) | copy-start | bytes 148
  0.0 20.0 %copy-start.3 = (bf16[48,384]{1,0:T(8,128)(2,1)S(1)}, bf16[48,384]{1,0:T(8,128)(2,1)}, u32[]{:S(2)}) copy-start(bf16[48,384]{1,0:T(8,128)(2,1)} %w_ref.1) | copy-start | bytes 110596
  2.5 35.1 %all-to-all-start = ((bf16[64,4,1152]{2,1,0:T(4,128)(2,1)}), bf16[64,4,1152]{2,1,0:T(4,128)(2,1)S(1)}, u32[]{:S(2)}, u32[]{:S(2)}) async-start(bf16[64,4,1152]{2,1,0:T(4,128)(2,1)} %shard_map.82), calls=%async_computation | async-start | bytes 1179648 | tf_op jit(solution)/shard_map/all_to_all | solution.py:241
  18.5 50.1 %copy-start.4 = (s32[256]{0:T(256)S(1)}, s32[256]{0:T(256)}, u32[]{:S(2)}) copy-start(s32[256]{0:T(256)} %param.13) | copy-start | bytes 3076
  18.5 50.1 %copy-start.5 = (s32[3]{0:T(128)S(1)}, s32[3]{0:T(128)}, u32[]{:S(2)}) copy-start(s32[3]{0:T(128)} %kinds_ref.1) | copy-start | bytes 40
  39.6 42.5 %copy-start.6 = (f32[384]{0:T(512)S(1)}, f32[384]{0:T(512)}, u32[]{:S(2)}) copy-start(f32[384]{0:T(512)} %param.15) | copy-start | bytes 4612
  70.7 11.5 %all-to-all-start.2 = ((bf16[4,256,384]{2,1,0:T(8,128)(2,1)}), bf16[4,256,384]{2,1,0:T(8,128)(2,1)S(1)}, u32[]{:S(2)}, u32[]{:S(2)}) async-start(bf16[4,256,384]{2,1,0:T(8,128)(2,1)} %get-tuple-element.7), calls=%async_computation.2 | async-start | bytes 1572864 | tf_op jit(solution)/shard_map/all_to_all | solution.py:263
  74.9 14.0 %collective-permute-start.1 = (bf16[8,96,384]{2,1,0:T(8,128)(2,1)S(1)}, bf16[8,96,384]{2,1,0:T(8,128)(2,1)S(1)}, u32[]{:S(2)}, u32[]{:S(2)}) collective-permute-start(bf16[8,96,384]{2,1,0:T(8,128)(2,1)S(1)} %get-tuple-element.8.own_ref), channel_id=1, source_target_pairs={{8,0},{65,1},{10,2},{67,3},{12,4},{69,5},{14,6},{71,7},{16,8},{73,... | collective-permute-start | bytes 1769480 | tf_op jit(solution)/shard_map/ppermute | solution.py:211
  76.9 12.1 %collective-permute-start.2 = (bf16[8,96,384]{2,1,0:T(8,128)(2,1)S(1)}, bf16[8,96,384]{2,1,0:T(8,128)(2,1)S(1)}, u32[]{:S(2)}, u32[]{:S(2)}) collective-permute-start(bf16[8,96,384]{2,1,0:T(8,128)(2,1)S(1)} %get-tuple-element.8.own_ref), channel_id=1, source_target_pairs={{56,0},{449,1},{58,2},{451,3},{60,4},{453,5},{62,6},{455,7},{0,8},... | collective-permute-start | bytes 1769480 | tf_op jit(solution)/shard_map/ppermute | solution.py:211
  80.2 16.1 %collective-permute-start.3 = (bf16[8,96,384]{2,1,0:T(8,128)(2,1)S(1)}, bf16[8,96,384]{2,1,0:T(8,128)(2,1)S(1)}, u32[]{:S(2)}, u32[]{:S(2)}) collective-permute-start(bf16[8,96,384]{2,1,0:T(8,128)(2,1)S(1)} %get-tuple-element.8.own_ref), channel_id=1, source_target_pairs={{64,0},{9,1},{66,2},{11,3},{68,4},{13,5},{70,6},{15,7},{72,8},{17,... | collective-permute-start | bytes 1769480 | tf_op jit(solution)/shard_map/ppermute | solution.py:211
  82.2 14.4 %collective-permute-start = (bf16[4,256,384]{2,1,0:T(8,128)(2,1)S(1)}, bf16[4,256,384]{2,1,0:T(8,128)(2,1)S(1)}, u32[]{:S(2)}, u32[]{:S(2)}) collective-permute-start(bf16[4,256,384]{2,1,0:T(8,128)(2,1)S(1)} %all-to-all-done.2.x_ref), channel_id=1, source_target_pairs={{0,1},{1,0},{2,3},{3,2},{4,5},{5,4},{6,7},{7,6},{8,9},{9,8},{10,11... | collective-permute-start | bytes 2359304 | tf_op jit(solution)/shard_map/ppermute | solution.py:271

commit v5 on v4

--- a/solution.py
+++ b/solution.py
@@ -109,6 +109,7 @@
     row_block, column_block = row % group // (group // 2), column % group // (group // 2)
     at, row = iotas((8 * frames, rows))
     spread = ones_where((at % 8 < group) & (at // 8 * group + at % 8 == row))
+    outs = []
     for h in range(heads):
         q, k, v = (
             x_ref[:, :, i * width + h * LANES : i * width + (h + 1) * LANES]
@@ -117,14 +118,14 @@
             .astype(jnp.bfloat16)
             for i in range(3)
         )
-        out = attend(q, k, v, masks_ref, h, row_block, column_block).astype(jnp.bfloat16)
-        out = jnp.dot(spread, out, preferred_element_type=jnp.float32)
-        c = slice(h * LANES, (h + 1) * LANES)
-        weights = weights_ref[:, :, c].reshape(1, 4, 1, 4, 16, LANES)
-        first = out.reshape(2, 4, 2, 4, 8, LANES) + weights[:, :, :, :, :8].astype(jnp.float32)
-        rest = jnp.broadcast_to(weights[:, :, :, :, 8:], first.shape)
-        out_ref[:, :8, c] = first.reshape(frames, 8, LANES).astype(jnp.bfloat16)
-        out_ref[:, 8:, c] = rest.reshape(frames, 8, LANES)
+        out = attend(q, k, v, masks_ref, h, row_block, column_block)
+        outs.append(out.astype(jnp.bfloat16))
+    out = jnp.dot(spread, jnp.concatenate(outs, axis=1), preferred_element_type=jnp.float32)
+    weights = weights_ref[...].reshape(1, 4, 1, 4, 16, width)
+    first = out.reshape(2, 4, 2, 4, 8, width) + weights[:, :, :, :, :8].astype(jnp.float32)
+    rest = jnp.broadcast_to(weights[:, :, :, :, 8:], first.shape)
+    out_ref[:, :8, :] = first.reshape(frames, 8, width).astype(jnp.bfloat16)
+    out_ref[:, 8:, :] = rest.reshape(frames, 8, width)
 
 
 def select_kernel(
@@ -138,22 +139,27 @@
     left = place - 96 * quarter
     z = sum((left >= 12 * i).astype(jnp.int32) for i in range(1, 8))
     column = 48 * z + 12 * quarter + left - 12 * z
-    total = None
-    for h in range(heads):
-        c = slice(h * LANES, (h + 1) * LANES)
-        far = far_ref[:, :8, c].astype(jnp.float32)[:, :4].reshape(rows, LANES)
-        back = jnp.dot(onehot, far.astype(jnp.bfloat16), preferred_element_type=jnp.float32)
-        near = near_ref[:, c].astype(jnp.float32)
-        chosen = jnp.where(kinds_ref[h] == 1, back, near).astype(jnp.bfloat16)
-        old = lax.broadcasted_iota(jnp.int32, (LANES, width), 0) + h * LANES
-        moved = jnp.dot(chosen, ones_where(old == column), preferred_element_type=jnp.float32)
-        total = moved if total is None else total + moved
-    out_ref[...] = total.astype(jnp.bfloat16)
-    copies = [
-        pltpu.make_async_copy(out_ref, out_hbm.at[x], sems.at[x]) for x in range(out_hbm.shape[0])
-    ]
-    for copy in copies:
-        copy.start()
+    old = lax.broadcasted_iota(jnp.int32, (width, width), 0)
+    to_weight = ones_where(old == column)
+    far = far_ref[:, :8, :].astype(jnp.float32)[:, :4].reshape(rows, width).astype(jnp.bfloat16)
+    copies = []
+    for half in range(2):
+        r = slice(half * rows // 2, (half + 1) * rows // 2)
+        back = jnp.dot(onehot[r], far, preferred_element_type=jnp.float32)
+        near = near_ref[r, :].astype(jnp.float32)
+        chosen = []
+        for h in range(heads):
+            c = slice(h * LANES, (h + 1) * LANES)
+            chosen.append(jnp.where(kinds_ref[h] == 1, back[:, c], near[:, c]).astype(jnp.bfloat16))
+        moved = jnp.dot(
+            jnp.concatenate(chosen, axis=1), to_weight, preferred_element_type=jnp.float32
+        )
+        out_ref[r, :] = moved.astype(jnp.bfloat16)
+        for x in range(out_hbm.shape[0]):
+            copies.append(
+                pltpu.make_async_copy(out_ref.at[r], out_hbm.at[x, r], sems.at[2 * x + half])
+            )
+            copies[-1].start()
     n, part = own_ref.shape[:2]
     row, at = iotas((part, 16 * n))
     take = ones_where(row // 12 * 16 + 4 + row % 12 == at)
@@ -255,7 +261,7 @@
         returned,
         near,
         out=[HBM, VMEM],
-        scratch=[pltpu.VMEM((rows, width), jnp.bfloat16), pltpu.SemaphoreType.DMA((parts // 2,))],
+        scratch=[pltpu.VMEM((rows, width), jnp.bfloat16), pltpu.SemaphoreType.DMA((parts,))],
     )
     others = [
         fetch(own, offsets) for offsets in (((0, 1), (1, 0)), ((0, -1), (-1, 0)), ((1, 0), (0, 1)))

time: 98.6 us -> 98.2 us (level)
  no operation moved by 1% of the time
where the time goes in v5:
time: 98.2 us; the launch traced here: 97.8 us
  starting transfers between devices  34.1 us (35%)
  blocking collectives  28.9 us (29%)
  waiting for transfers between devices  24.8 us (25%)
  Pallas kernels  9.47 us (10%)
    all_to_all x1, blocking collectives, local(): lax.all_to_all(far, 'seq', split_axis=0, concat_axis=0, tiled=True)  28.9 us
    all_to_all x1, waiting for transfers between devices, local(): moved = lax.all_to_all(sent, 'seq', split_axis=0, concat_axis=0, tiled=True)  17.4 us
    all_to_all x1, starting transfers between devices, local(): moved = lax.all_to_all(sent, 'seq', split_axis=0, concat_axis=0, tiled=True)  15.9 us
    pallas_call x7, Pallas kernels, call(): pl.pallas_call(kernel, out_shape=shapes if isinstance(shape, list) else s...  9.47 us
    ppermute x3, waiting for transfers between devices, fetch(): return lax.ppermute(block, ('seq', 'mlp'), pairs)  7.39 us
    ppermute x3, starting transfers between devices, fetch(): return lax.ppermute(block, ('seq', 'mlp'), pairs)  7.19 us
    ppermute x1, starting transfers between devices, local(): lax.ppermute(columns, 'mlp', [(i, i ^ 1) for i in range(parts)])  6.71 us
    all_to_all x1, starting transfers between devices, local(): lax.all_to_all(attended, 'mlp', split_axis=0, concat_axis=0, axis_index_g...  4.29 us
  transfers between devices with their start and end apart: 6, of which 2 were waited for; matrix products, arithmetic and copies ran while one was open for 0% of the time, Pallas kernels for 2%

profile of v5, /device:TPU:19, one launch (start us, length us, event | category | flops | bytes accessed | tf_op | source)
XLA Modules:
  0.0 97.8 jit_solution(10558136947387132146)
XLA Ops:
  0.0 0.0 copy-start.2
  0.0 0.0 copy-start
  0.0 0.0 copy-start.1
  0.0 0.0 copy-start.7
  0.0 0.0 copy-start.3
  0.0 2.5 %shard_map.82 = bf16[64,4,1152]{2,1,0:T(4,128)(2,1)} custom-call(s32[1,256]{1,0:T(1,128)} %bitcast.1, bf16[256,384]{1,0:T(8,128)(2,1)} %q_ref.1, bf16[256,384]{1,0:T(8,128)(2,1)} %k_ref.1, bf16[256,384]{1,0:T(8,128)(2,1)} %v_ref.1), custom_call_target="tpu_custom_call" | custom-call | tf_op jit(solution)/shard_map/pallas_call | solution.py:198
  2.5 15.9 %all-to-all-start = ((bf16[64,4,1152]{2,1,0:T(4,128)(2,1)}), bf16[64,4,1152]{2,1,0:T(4,128)(2,1)S(1)}, u32[]{:S(2)}, u32[]{:S(2)}) async-start(bf16[64,4,1152]{2,1,0:T(4,128)(2,1)} %shard_map.82), calls=%async_computation | async-start | bytes 1179648 | tf_op jit(solution)/shard_map/all_to_all | solution.py:247
  18.5 0.0 copy-done.7
  18.5 0.0 copy-start.4
  18.5 0.0 copy-start.5
  18.5 0.1 copy.10
  18.6 0.1 reshape.11.masks_ref
  18.7 0.0 copy-done.2
  18.7 0.0 copy-done
  18.7 0.0 copy-done.1
  18.7 1.3 %shard_map.84.after_hbm.near_ref = bf16[256,384]{1,0:T(8,128)(2,1)S(1)} custom-call(s32[12]{0:T(128)S(1)} %reshape.11.masks_ref, bf16[256,384]{1,0:T(8,128)(2,1)S(1)} %copy-done, bf16[256,384]{1,0:T(8,128)(2,1)S(1)} %copy-done.1, bf16[256,384]{1,0:T(8,128)(2,1)S(1)} %copy-done.2), custom_call_target="tpu_custom_call" | custom-call | tf_op jit(solution)/shard_map/pallas_call | solution.py:198
  20.0 0.0 copy-done.3
  20.0 0.3 shard_map.83.weights_ref
  20.3 17.4 %all-to-all-done.x_ref = bf16[64,4,1152]{2,1,0:T(4,128)(2,1)S(1)} async-done(((bf16[64,4,1152]{2,1,0:T(4,128)(2,1)}), bf16[64,4,1152]{2,1,0:T(4,128)(2,1)S(1)}, u32[]{:S(2)}, u32[]{:S(2)}) %all-to-all-start) | async-done | bytes 589856 | tf_op jit(solution)/shard_map/all_to_all | solution.py:247
  37.7 1.6 %shard_map.85 = bf16[64,16,384]{2,1,0:T(8,128)(2,1)S(1)} custom-call(s32[12]{0:T(128)S(1)} %reshape.11.masks_ref, bf16[64,4,1152]{2,1,0:T(4,128)(2,1)S(1)} %all-to-all-done.x_ref, bf16[16,16,384]{2,1,0:T(8,128)(2,1)S(1)} %shard_map.83.weights_ref, bf16[256,384]{1,0:T(8,128)(2,1)S(1)} %shard_map.84.after_hbm.near_ref), custom_call_target="tpu_custom_call" | custom-call | tf_op jit(solution)/shard_map/pallas_call | solution.py:198
  39.2 0.0 copy-start.6
  39.3 28.9 %all_to_all.15.far_ref = bf16[64,16,384]{2,1,0:T(8,128)(2,1)S(1)} all-to-all(bf16[64,16,384]{2,1,0:T(8,128)(2,1)S(1)} %shard_map.85), channel_id=1, replica_groups=mesh['seq'=64,'mlp'=8] {'seq'}, dimensions={0} | all-to-all | bytes 1572864 | tf_op jit(solution)/shard_map/all_to_all | solution.py:253
  68.2 0.0 copy-done.4
  68.2 0.0 copy-done.5
  68.2 2.0 %shard_map.86 = (bf16[4,256,384]{2,1,0:T(8,128)(2,1)}, bf16[8,96,384]{2,1,0:T(8,128)(2,1)S(1)}) custom-call(s32[3]{0:T(128)S(1)} %copy-done.5, s32[1,256]{1,0:T(1,128)S(1)} %bitcast.2, bf16[64,16,384]{2,1,0:T(8,128)(2,1)S(1)} %all_to_all.15.far_ref, bf16[256,384]{1,0:T(8,128)(2,1)S(1)} %shard_map.84.after_hbm.near_ref), custom_call_target="tpu_custom_call" | custom-call | tf_op jit(solution)/shard_map/pallas_call | solution.py:198
  70.2 4.3 %all-to-all-start.2 = ((bf16[4,256,384]{2,1,0:T(8,128)(2,1)}), bf16[4,256,384]{2,1,0:T(8,128)(2,1)S(1)}, u32[]{:S(2)}, u32[]{:S(2)}) async-start(bf16[4,256,384]{2,1,0:T(8,128)(2,1)} %get-tuple-element.7), calls=%async_computation.2 | async-start | bytes 1572864 | tf_op jit(solution)/shard_map/all_to_all | solution.py:269
  74.5 1.9 %collective-permute-start.1 = (bf16[8,96,384]{2,1,0:T(8,128)(2,1)S(1)}, bf16[8,96,384]{2,1,0:T(8,128)(2,1)S(1)}, u32[]{:S(2)}, u32[]{:S(2)}) collective-permute-start(bf16[8,96,384]{2,1,0:T(8,128)(2,1)S(1)} %get-tuple-element.8.own_ref), channel_id=1, source_target_pairs={{8,0},{65,1},{10,2},{67,3},{12,4},{69,5},{14,6},{71,7},{16,8},{73,... | collective-permute-start | bytes 1769480 | tf_op jit(solution)/shard_map/ppermute | solution.py:217
  76.4 3.4 %collective-permute-start.2 = (bf16[8,96,384]{2,1,0:T(8,128)(2,1)S(1)}, bf16[8,96,384]{2,1,0:T(8,128)(2,1)S(1)}, u32[]{:S(2)}, u32[]{:S(2)}) collective-permute-start(bf16[8,96,384]{2,1,0:T(8,128)(2,1)S(1)} %get-tuple-element.8.own_ref), channel_id=1, source_target_pairs={{56,0},{449,1},{58,2},{451,3},{60,4},{453,5},{62,6},{455,7},{0,8},... | collective-permute-start | bytes 1769480 | tf_op jit(solution)/shard_map/ppermute | solution.py:217
  79.7 1.9 %collective-permute-start.3 = (bf16[8,96,384]{2,1,0:T(8,128)(2,1)S(1)}, bf16[8,96,384]{2,1,0:T(8,128)(2,1)S(1)}, u32[]{:S(2)}, u32[]{:S(2)}) collective-permute-start(bf16[8,96,384]{2,1,0:T(8,128)(2,1)S(1)} %get-tuple-element.8.own_ref), channel_id=1, source_target_pairs={{64,0},{9,1},{66,2},{11,3},{68,4},{13,5},{70,6},{15,7},{72,8},{17,... | collective-permute-start | bytes 1769480 | tf_op jit(solution)/shard_map/ppermute | solution.py:217
  81.7 0.0 copy-done.6
  81.7 0.0 all-to-all-done.2.x_ref
  81.7 6.7 %collective-permute-start = (bf16[4,256,384]{2,1,0:T(8,128)(2,1)S(1)}, bf16[4,256,384]{2,1,0:T(8,128)(2,1)S(1)}, u32[]{:S(2)}, u32[]{:S(2)}) collective-permute-start(bf16[4,256,384]{2,1,0:T(8,128)(2,1)S(1)} %all-to-all-done.2.x_ref), channel_id=1, source_target_pairs={{0,1},{1,0},{2,3},{3,2},{4,5},{5,4},{6,7},{7,6},{8,9},{9,8},{10,11... | collective-permute-start | bytes 2359304 | tf_op jit(solution)/shard_map/ppermute | solution.py:277
  88.4 0.0 collective-permute-done.1.next_ref
  88.4 0.0 collective-permute-done.2.last_ref
  88.4 7.4 %collective-permute-done.3.second_ref = bf16[8,96,384]{2,1,0:T(8,128)(2,1)S(1)} collective-permute-done((bf16[8,96,384]{2,1,0:T(8,128)(2,1)S(1)}, bf16[8,96,384]{2,1,0:T(8,128)(2,1)S(1)}, u32[]{:S(2)}, u32[]{:S(2)}) %collective-permute-start.3) | collective-permute-done | bytes 589856 | tf_op jit(solution)/shard_map/ppermute | solution.py:217
  95.8 0.2 shard_map.87.w_ref
  96.1 0.0 collective-permute-done.others_ref
  96.1 1.7 %shard_map.88 = bf16[256,384]{1,0:T(8,128)(2,1)} custom-call(f32[1,384]{1,0:T(1,128)S(1)} %reshape.9.gate_ref, bf16[4,256,384]{2,1,0:T(8,128)(2,1)S(1)} %all-to-all-done.2.x_ref, bf16[4,256,384]{2,1,0:T(8,128)(2,1)S(1)} %collective-permute-done.others_ref, bf16[8,384,384]{2,1,0:T(8,128)(2,1)S(1)} %shard_map.87.w_ref), custom_call_target="tpu_custom_call" | custom-call | tf_op jit(solution)/shard_map/pallas_call | solution.py:198
  (1 shorter events, 0.0 us)
Async XLA Ops:
  0.0 18.7 %copy-start.2 = (bf16[256,384]{1,0:T(8,128)(2,1)S(1)}, bf16[256,384]{1,0:T(8,128)(2,1)}, u32[]{:S(2)}) copy-start(bf16[256,384]{1,0:T(8,128)(2,1)} %v_ref.1) | copy-start | bytes 589828
  0.0 18.7 %copy-start = (bf16[256,384]{1,0:T(8,128)(2,1)S(1)}, bf16[256,384]{1,0:T(8,128)(2,1)}, u32[]{:S(2)}) copy-start(bf16[256,384]{1,0:T(8,128)(2,1)} %q_ref.1) | copy-start | bytes 589828
  0.0 18.7 %copy-start.1 = (bf16[256,384]{1,0:T(8,128)(2,1)S(1)}, bf16[256,384]{1,0:T(8,128)(2,1)}, u32[]{:S(2)}) copy-start(bf16[256,384]{1,0:T(8,128)(2,1)} %k_ref.1) | copy-start | bytes 589828
  0.0 18.4 %copy-start.7 = (s32[3,2,2]{0,2,1:T(2,128)S(1)}, s32[3,2,2]{0,2,1:T(2,128)}, u32[]{:S(2)}) copy-start(s32[3,2,2]{0,2,1:T(2,128)} %param.12) | copy-start | bytes 148
  0.0 20.0 %copy-start.3 = (bf16[48,384]{1,0:T(8,128)(2,1)S(1)}, bf16[48,384]{1,0:T(8,128)(2,1)}, u32[]{:S(2)}) copy-start(bf16[48,384]{1,0:T(8,128)(2,1)} %w_ref.1) | copy-start | bytes 110596
  2.5 35.1 %all-to-all-start = ((bf16[64,4,1152]{2,1,0:T(4,128)(2,1)}), bf16[64,4,1152]{2,1,0:T(4,128)(2,1)S(1)}, u32[]{:S(2)}, u32[]{:S(2)}) async-start(bf16[64,4,1152]{2,1,0:T(4,128)(2,1)} %shard_map.82), calls=%async_computation | async-start | bytes 1179648 | tf_op jit(solution)/shard_map/all_to_all | solution.py:247
  18.5 49.7 %copy-start.4 = (s32[256]{0:T(256)S(1)}, s32[256]{0:T(256)}, u32[]{:S(2)}) copy-start(s32[256]{0:T(256)} %param.13) | copy-start | bytes 3076
  18.5 49.7 %copy-start.5 = (s32[3]{0:T(128)S(1)}, s32[3]{0:T(128)}, u32[]{:S(2)}) copy-start(s32[3]{0:T(128)} %kinds_ref.1) | copy-start | bytes 40
  39.2 42.4 %copy-start.6 = (f32[384]{0:T(512)S(1)}, f32[384]{0:T(512)}, u32[]{:S(2)}) copy-start(f32[384]{0:T(512)} %param.15) | copy-start | bytes 4612
  70.2 11.5 %all-to-all-start.2 = ((bf16[4,256,384]{2,1,0:T(8,128)(2,1)}), bf16[4,256,384]{2,1,0:T(8,128)(2,1)S(1)}, u32[]{:S(2)}, u32[]{:S(2)}) async-start(bf16[4,256,384]{2,1,0:T(8,128)(2,1)} %get-tuple-element.7), calls=%async_computation.2 | async-start | bytes 1572864 | tf_op jit(solution)/shard_map/all_to_all | solution.py:269
  74.5 14.0 %collective-permute-start.1 = (bf16[8,96,384]{2,1,0:T(8,128)(2,1)S(1)}, bf16[8,96,384]{2,1,0:T(8,128)(2,1)S(1)}, u32[]{:S(2)}, u32[]{:S(2)}) collective-permute-start(bf16[8,96,384]{2,1,0:T(8,128)(2,1)S(1)} %get-tuple-element.8.own_ref), channel_id=1, source_target_pairs={{8,0},{65,1},{10,2},{67,3},{12,4},{69,5},{14,6},{71,7},{16,8},{73,... | collective-permute-start | bytes 1769480 | tf_op jit(solution)/shard_map/ppermute | solution.py:217
  76.4 12.1 %collective-permute-start.2 = (bf16[8,96,384]{2,1,0:T(8,128)(2,1)S(1)}, bf16[8,96,384]{2,1,0:T(8,128)(2,1)S(1)}, u32[]{:S(2)}, u32[]{:S(2)}) collective-permute-start(bf16[8,96,384]{2,1,0:T(8,128)(2,1)S(1)} %get-tuple-element.8.own_ref), channel_id=1, source_target_pairs={{56,0},{449,1},{58,2},{451,3},{60,4},{453,5},{62,6},{455,7},{0,8},... | collective-permute-start | bytes 1769480 | tf_op jit(solution)/shard_map/ppermute | solution.py:217
  79.7 16.1 %collective-permute-start.3 = (bf16[8,96,384]{2,1,0:T(8,128)(2,1)S(1)}, bf16[8,96,384]{2,1,0:T(8,128)(2,1)S(1)}, u32[]{:S(2)}, u32[]{:S(2)}) collective-permute-start(bf16[8,96,384]{2,1,0:T(8,128)(2,1)S(1)} %get-tuple-element.8.own_ref), channel_id=1, source_target_pairs={{64,0},{9,1},{66,2},{11,3},{68,4},{13,5},{70,6},{15,7},{72,8},{17,... | collective-permute-start | bytes 1769480 | tf_op jit(solution)/shard_map/ppermute | solution.py:217
  81.7 14.4 %collective-permute-start = (bf16[4,256,384]{2,1,0:T(8,128)(2,1)S(1)}, bf16[4,256,384]{2,1,0:T(8,128)(2,1)S(1)}, u32[]{:S(2)}, u32[]{:S(2)}) collective-permute-start(bf16[4,256,384]{2,1,0:T(8,128)(2,1)S(1)} %all-to-all-done.2.x_ref), channel_id=1, source_target_pairs={{0,1},{1,0},{2,3},{3,2},{4,5},{5,4},{6,7},{7,6},{8,9},{9,8},{10,11... | collective-permute-start | bytes 2359304 | tf_op jit(solution)/shard_map/ppermute | solution.py:277

commit v6 on v5

--- a/solution.py
+++ b/solution.py
@@ -121,11 +121,13 @@
         out = attend(q, k, v, masks_ref, h, row_block, column_block)
         outs.append(out.astype(jnp.bfloat16))
     out = jnp.dot(spread, jnp.concatenate(outs, axis=1), preferred_element_type=jnp.float32)
-    weights = weights_ref[...].reshape(1, 4, 1, 4, 16, width)
-    first = out.reshape(2, 4, 2, 4, 8, width) + weights[:, :, :, :, :8].astype(jnp.float32)
+    weights = weights_ref[...].astype(jnp.float32).reshape(1, 4, 1, 4, 16, width)
+    first = out.reshape(2, 4, 2, 4, 8, width) + weights[:, :, :, :, :8]
     rest = jnp.broadcast_to(weights[:, :, :, :, 8:], first.shape)
-    out_ref[:, :8, :] = first.reshape(frames, 8, width).astype(jnp.bfloat16)
-    out_ref[:, 8:, :] = rest.reshape(frames, 8, width)
+    message = jnp.concatenate(
+        [first.reshape(frames, 8, width), rest.reshape(frames, 8, width)], axis=1
+    )
+    out_ref[...] = message.astype(jnp.bfloat16)
 
 
 def select_kernel(
@@ -141,7 +143,7 @@
     column = 48 * z + 12 * quarter + left - 12 * z
     old = lax.broadcasted_iota(jnp.int32, (width, width), 0)
     to_weight = ones_where(old == column)
-    far = far_ref[:, :8, :].astype(jnp.float32)[:, :4].reshape(rows, width).astype(jnp.bfloat16)
+    far = far_ref[...].astype(jnp.float32)[:, :4].reshape(rows, width).astype(jnp.bfloat16)
     copies = []
     for half in range(2):
         r = slice(half * rows // 2, (half + 1) * rows // 2)

time: 98.2 us -> 98.2 us (level)
  no operation moved by 1% of the time
where the time goes in v6:
time: 98.2 us; the launch traced here: 97.8 us
  starting transfers between devices  34.1 us (35%)
  blocking collectives  28.9 us (29%)
  waiting for transfers between devices  24.8 us (25%)
  Pallas kernels  9.47 us (10%)
    all_to_all x1, blocking collectives, local(): lax.all_to_all(far, 'seq', split_axis=0, concat_axis=0, tiled=True)  28.9 us
    all_to_all x1, waiting for transfers between devices, local(): moved = lax.all_to_all(sent, 'seq', split_axis=0, concat_axis=0, tiled=True)  17.4 us
    all_to_all x1, starting transfers between devices, local(): moved = lax.all_to_all(sent, 'seq', split_axis=0, concat_axis=0, tiled=True)  15.9 us
    pallas_call x7, Pallas kernels, call(): pl.pallas_call(kernel, out_shape=shapes if isinstance(shape, list) else s...  9.47 us
    ppermute x3, waiting for transfers between devices, fetch(): return lax.ppermute(block, ('seq', 'mlp'), pairs)  7.39 us
    ppermute x3, starting transfers between devices, fetch(): return lax.ppermute(block, ('seq', 'mlp'), pairs)  7.19 us
    ppermute x1, starting transfers between devices, local(): lax.ppermute(columns, 'mlp', [(i, i ^ 1) for i in range(parts)])  6.71 us
    all_to_all x1, starting transfers between devices, local(): lax.all_to_all(attended, 'mlp', split_axis=0, concat_axis=0, axis_index_g...  4.29 us
  transfers between devices with their start and end apart: 6, of which 2 were waited for; matrix products, arithmetic and copies ran while one was open for 0% of the time, Pallas kernels for 2%

profile of v6, /device:TPU:19, one launch (start us, length us, event | category | flops | bytes accessed | tf_op | source)
XLA Modules:
  0.0 97.8 jit_solution(2886299399489644652)
XLA Ops:
  0.0 0.0 copy-start.2
  0.0 0.0 copy-start
  0.0 0.0 copy-start.1
  0.0 0.0 copy-start.7
  0.0 0.0 copy-start.3
  0.0 2.5 %shard_map.82 = bf16[64,4,1152]{2,1,0:T(4,128)(2,1)} custom-call(s32[1,256]{1,0:T(1,128)} %bitcast.1, bf16[256,384]{1,0:T(8,128)(2,1)} %q_ref.1, bf16[256,384]{1,0:T(8,128)(2,1)} %k_ref.1, bf16[256,384]{1,0:T(8,128)(2,1)} %v_ref.1), custom_call_target="tpu_custom_call" | custom-call | tf_op jit(solution)/shard_map/pallas_call | solution.py:200
  2.5 15.9 %all-to-all-start = ((bf16[64,4,1152]{2,1,0:T(4,128)(2,1)}), bf16[64,4,1152]{2,1,0:T(4,128)(2,1)S(1)}, u32[]{:S(2)}, u32[]{:S(2)}) async-start(bf16[64,4,1152]{2,1,0:T(4,128)(2,1)} %shard_map.82), calls=%async_computation | async-start | bytes 1179648 | tf_op jit(solution)/shard_map/all_to_all | solution.py:249
  18.5 0.0 copy-done.7
  18.5 0.0 copy-start.4
  18.5 0.0 copy-start.5
  18.5 0.1 copy.10
  18.6 0.1 reshape.11.masks_ref
  18.7 0.0 copy-done.2
  18.7 0.0 copy-done
  18.7 0.0 copy-done.1
  18.7 1.3 %shard_map.84.after_hbm.near_ref = bf16[256,384]{1,0:T(8,128)(2,1)S(1)} custom-call(s32[12]{0:T(128)S(1)} %reshape.11.masks_ref, bf16[256,384]{1,0:T(8,128)(2,1)S(1)} %copy-done, bf16[256,384]{1,0:T(8,128)(2,1)S(1)} %copy-done.1, bf16[256,384]{1,0:T(8,128)(2,1)S(1)} %copy-done.2), custom_call_target="tpu_custom_call" | custom-call | tf_op jit(solution)/shard_map/pallas_call | solution.py:200
  20.0 0.0 copy-done.3
  20.0 0.3 shard_map.83.weights_ref
  20.3 17.4 %all-to-all-done.x_ref = bf16[64,4,1152]{2,1,0:T(4,128)(2,1)S(1)} async-done(((bf16[64,4,1152]{2,1,0:T(4,128)(2,1)}), bf16[64,4,1152]{2,1,0:T(4,128)(2,1)S(1)}, u32[]{:S(2)}, u32[]{:S(2)}) %all-to-all-start) | async-done | bytes 589856 | tf_op jit(solution)/shard_map/all_to_all | solution.py:249
  37.7 1.6 %shard_map.85 = bf16[64,16,384]{2,1,0:T(8,128)(2,1)S(1)} custom-call(s32[12]{0:T(128)S(1)} %reshape.11.masks_ref, bf16[64,4,1152]{2,1,0:T(4,128)(2,1)S(1)} %all-to-all-done.x_ref, bf16[16,16,384]{2,1,0:T(8,128)(2,1)S(1)} %shard_map.83.weights_ref, bf16[256,384]{1,0:T(8,128)(2,1)S(1)} %shard_map.84.after_hbm.near_ref), custom_call_target="tpu_custom_call" | custom-call | tf_op jit(solution)/shard_map/pallas_call | solution.py:200
  39.2 0.0 copy-start.6
  39.3 28.9 %all_to_all.15.far_ref = bf16[64,16,384]{2,1,0:T(8,128)(2,1)S(1)} all-to-all(bf16[64,16,384]{2,1,0:T(8,128)(2,1)S(1)} %shard_map.85), channel_id=1, replica_groups=mesh['seq'=64,'mlp'=8] {'seq'}, dimensions={0} | all-to-all | bytes 1572864 | tf_op jit(solution)/shard_map/all_to_all | solution.py:255
  68.2 0.0 copy-done.4
  68.2 0.0 copy-done.5
  68.2 2.0 %shard_map.86 = (bf16[4,256,384]{2,1,0:T(8,128)(2,1)}, bf16[8,96,384]{2,1,0:T(8,128)(2,1)S(1)}) custom-call(s32[3]{0:T(128)S(1)} %copy-done.5, s32[1,256]{1,0:T(1,128)S(1)} %bitcast.2, bf16[64,16,384]{2,1,0:T(8,128)(2,1)S(1)} %all_to_all.15.far_ref, bf16[256,384]{1,0:T(8,128)(2,1)S(1)} %shard_map.84.after_hbm.near_ref), custom_call_target="tpu_custom_call" | custom-call | tf_op jit(solution)/shard_map/pallas_call | solution.py:200
  70.2 4.3 %all-to-all-start.2 = ((bf16[4,256,384]{2,1,0:T(8,128)(2,1)}), bf16[4,256,384]{2,1,0:T(8,128)(2,1)S(1)}, u32[]{:S(2)}, u32[]{:S(2)}) async-start(bf16[4,256,384]{2,1,0:T(8,128)(2,1)} %get-tuple-element.7), calls=%async_computation.2 | async-start | bytes 1572864 | tf_op jit(solution)/shard_map/all_to_all | solution.py:271
  74.5 1.9 %collective-permute-start.1 = (bf16[8,96,384]{2,1,0:T(8,128)(2,1)S(1)}, bf16[8,96,384]{2,1,0:T(8,128)(2,1)S(1)}, u32[]{:S(2)}, u32[]{:S(2)}) collective-permute-start(bf16[8,96,384]{2,1,0:T(8,128)(2,1)S(1)} %get-tuple-element.8.own_ref), channel_id=1, source_target_pairs={{8,0},{65,1},{10,2},{67,3},{12,4},{69,5},{14,6},{71,7},{16,8},{73,... | collective-permute-start | bytes 1769480 | tf_op jit(solution)/shard_map/ppermute | solution.py:219
  76.4 3.4 %collective-permute-start.2 = (bf16[8,96,384]{2,1,0:T(8,128)(2,1)S(1)}, bf16[8,96,384]{2,1,0:T(8,128)(2,1)S(1)}, u32[]{:S(2)}, u32[]{:S(2)}) collective-permute-start(bf16[8,96,384]{2,1,0:T(8,128)(2,1)S(1)} %get-tuple-element.8.own_ref), channel_id=1, source_target_pairs={{56,0},{449,1},{58,2},{451,3},{60,4},{453,5},{62,6},{455,7},{0,8},... | collective-permute-start | bytes 1769480 | tf_op jit(solution)/shard_map/ppermute | solution.py:219
  79.7 1.9 %collective-permute-start.3 = (bf16[8,96,384]{2,1,0:T(8,128)(2,1)S(1)}, bf16[8,96,384]{2,1,0:T(8,128)(2,1)S(1)}, u32[]{:S(2)}, u32[]{:S(2)}) collective-permute-start(bf16[8,96,384]{2,1,0:T(8,128)(2,1)S(1)} %get-tuple-element.8.own_ref), channel_id=1, source_target_pairs={{64,0},{9,1},{66,2},{11,3},{68,4},{13,5},{70,6},{15,7},{72,8},{17,... | collective-permute-start | bytes 1769480 | tf_op jit(solution)/shard_map/ppermute | solution.py:219
  81.7 0.0 copy-done.6
  81.7 0.0 all-to-all-done.2.x_ref
  81.7 6.7 %collective-permute-start = (bf16[4,256,384]{2,1,0:T(8,128)(2,1)S(1)}, bf16[4,256,384]{2,1,0:T(8,128)(2,1)S(1)}, u32[]{:S(2)}, u32[]{:S(2)}) collective-permute-start(bf16[4,256,384]{2,1,0:T(8,128)(2,1)S(1)} %all-to-all-done.2.x_ref), channel_id=1, source_target_pairs={{0,1},{1,0},{2,3},{3,2},{4,5},{5,4},{6,7},{7,6},{8,9},{9,8},{10,11... | collective-permute-start | bytes 2359304 | tf_op jit(solution)/shard_map/ppermute | solution.py:279
  88.4 0.0 collective-permute-done.1.next_ref
  88.4 0.0 collective-permute-done.2.last_ref
  88.4 7.4 %collective-permute-done.3.second_ref = bf16[8,96,384]{2,1,0:T(8,128)(2,1)S(1)} collective-permute-done((bf16[8,96,384]{2,1,0:T(8,128)(2,1)S(1)}, bf16[8,96,384]{2,1,0:T(8,128)(2,1)S(1)}, u32[]{:S(2)}, u32[]{:S(2)}) %collective-permute-start.3) | collective-permute-done | bytes 589856 | tf_op jit(solution)/shard_map/ppermute | solution.py:219
  95.8 0.2 shard_map.87.w_ref
  96.1 0.0 collective-permute-done.others_ref
  96.1 1.7 %shard_map.88 = bf16[256,384]{1,0:T(8,128)(2,1)} custom-call(f32[1,384]{1,0:T(1,128)S(1)} %reshape.9.gate_ref, bf16[4,256,384]{2,1,0:T(8,128)(2,1)S(1)} %all-to-all-done.2.x_ref, bf16[4,256,384]{2,1,0:T(8,128)(2,1)S(1)} %collective-permute-done.others_ref, bf16[8,384,384]{2,1,0:T(8,128)(2,1)S(1)} %shard_map.87.w_ref), custom_call_target="tpu_custom_call" | custom-call | tf_op jit(solution)/shard_map/pallas_call | solution.py:200
  (1 shorter events, 0.0 us)
Async XLA Ops:
  0.0 18.7 %copy-start.2 = (bf16[256,384]{1,0:T(8,128)(2,1)S(1)}, bf16[256,384]{1,0:T(8,128)(2,1)}, u32[]{:S(2)}) copy-start(bf16[256,384]{1,0:T(8,128)(2,1)} %v_ref.1) | copy-start | bytes 589828
  0.0 18.7 %copy-start = (bf16[256,384]{1,0:T(8,128)(2,1)S(1)}, bf16[256,384]{1,0:T(8,128)(2,1)}, u32[]{:S(2)}) copy-start(bf16[256,384]{1,0:T(8,128)(2,1)} %q_ref.1) | copy-start | bytes 589828
  0.0 18.7 %copy-start.1 = (bf16[256,384]{1,0:T(8,128)(2,1)S(1)}, bf16[256,384]{1,0:T(8,128)(2,1)}, u32[]{:S(2)}) copy-start(bf16[256,384]{1,0:T(8,128)(2,1)} %k_ref.1) | copy-start | bytes 589828
  0.0 18.4 %copy-start.7 = (s32[3,2,2]{0,2,1:T(2,128)S(1)}, s32[3,2,2]{0,2,1:T(2,128)}, u32[]{:S(2)}) copy-start(s32[3,2,2]{0,2,1:T(2,128)} %param.12) | copy-start | bytes 148
  0.0 20.0 %copy-start.3 = (bf16[48,384]{1,0:T(8,128)(2,1)S(1)}, bf16[48,384]{1,0:T(8,128)(2,1)}, u32[]{:S(2)}) copy-start(bf16[48,384]{1,0:T(8,128)(2,1)} %w_ref.1) | copy-start | bytes 110596
  2.5 35.1 %all-to-all-start = ((bf16[64,4,1152]{2,1,0:T(4,128)(2,1)}), bf16[64,4,1152]{2,1,0:T(4,128)(2,1)S(1)}, u32[]{:S(2)}, u32[]{:S(2)}) async-start(bf16[64,4,1152]{2,1,0:T(4,128)(2,1)} %shard_map.82), calls=%async_computation | async-start | bytes 1179648 | tf_op jit(solution)/shard_map/all_to_all | solution.py:249
  18.5 49.7 %copy-start.4 = (s32[256]{0:T(256)S(1)}, s32[256]{0:T(256)}, u32[]{:S(2)}) copy-start(s32[256]{0:T(256)} %param.13) | copy-start | bytes 3076
  18.5 49.7 %copy-start.5 = (s32[3]{0:T(128)S(1)}, s32[3]{0:T(128)}, u32[]{:S(2)}) copy-start(s32[3]{0:T(128)} %kinds_ref.1) | copy-start | bytes 40
  39.2 42.4 %copy-start.6 = (f32[384]{0:T(512)S(1)}, f32[384]{0:T(512)}, u32[]{:S(2)}) copy-start(f32[384]{0:T(512)} %param.15) | copy-start | bytes 4612
  70.2 11.5 %all-to-all-start.2 = ((bf16[4,256,384]{2,1,0:T(8,128)(2,1)}), bf16[4,256,384]{2,1,0:T(8,128)(2,1)S(1)}, u32[]{:S(2)}, u32[]{:S(2)}) async-start(bf16[4,256,384]{2,1,0:T(8,128)(2,1)} %get-tuple-element.7), calls=%async_computation.2 | async-start | bytes 1572864 | tf_op jit(solution)/shard_map/all_to_all | solution.py:271
  74.5 14.0 %collective-permute-start.1 = (bf16[8,96,384]{2,1,0:T(8,128)(2,1)S(1)}, bf16[8,96,384]{2,1,0:T(8,128)(2,1)S(1)}, u32[]{:S(2)}, u32[]{:S(2)}) collective-permute-start(bf16[8,96,384]{2,1,0:T(8,128)(2,1)S(1)} %get-tuple-element.8.own_ref), channel_id=1, source_target_pairs={{8,0},{65,1},{10,2},{67,3},{12,4},{69,5},{14,6},{71,7},{16,8},{73,... | collective-permute-start | bytes 1769480 | tf_op jit(solution)/shard_map/ppermute | solution.py:219
  76.4 12.1 %collective-permute-start.2 = (bf16[8,96,384]{2,1,0:T(8,128)(2,1)S(1)}, bf16[8,96,384]{2,1,0:T(8,128)(2,1)S(1)}, u32[]{:S(2)}, u32[]{:S(2)}) collective-permute-start(bf16[8,96,384]{2,1,0:T(8,128)(2,1)S(1)} %get-tuple-element.8.own_ref), channel_id=1, source_target_pairs={{56,0},{449,1},{58,2},{451,3},{60,4},{453,5},{62,6},{455,7},{0,8},... | collective-permute-start | bytes 1769480 | tf_op jit(solution)/shard_map/ppermute | solution.py:219
  79.7 16.1 %collective-permute-start.3 = (bf16[8,96,384]{2,1,0:T(8,128)(2,1)S(1)}, bf16[8,96,384]{2,1,0:T(8,128)(2,1)S(1)}, u32[]{:S(2)}, u32[]{:S(2)}) collective-permute-start(bf16[8,96,384]{2,1,0:T(8,128)(2,1)S(1)} %get-tuple-element.8.own_ref), channel_id=1, source_target_pairs={{64,0},{9,1},{66,2},{11,3},{68,4},{13,5},{70,6},{15,7},{72,8},{17,... | collective-permute-start | bytes 1769480 | tf_op jit(solution)/shard_map/ppermute | solution.py:219
  81.7 14.4 %collective-permute-start = (bf16[4,256,384]{2,1,0:T(8,128)(2,1)S(1)}, bf16[4,256,384]{2,1,0:T(8,128)(2,1)S(1)}, u32[]{:S(2)}, u32[]{:S(2)}) collective-permute-start(bf16[4,256,384]{2,1,0:T(8,128)(2,1)S(1)} %all-to-all-done.2.x_ref), channel_id=1, source_target_pairs={{0,1},{1,0},{2,3},{3,2},{4,5},{5,4},{6,7},{7,6},{8,9},{9,8},{10,11... | collective-permute-start | bytes 2359304 | tf_op jit(solution)/shard_map/ppermute | solution.py:279

commit v7 on v6

--- a/solution.py
+++ b/solution.py
@@ -136,13 +136,6 @@
     rows, width = near_ref.shape
     heads = kinds_ref.shape[0]
     onehot = placement(order_ref[...], rows)
-    place = lax.broadcasted_iota(jnp.int32, (1, width), 1)
-    quarter = sum((place >= edge).astype(jnp.int32) for edge in (96, 192, 288))
-    left = place - 96 * quarter
-    z = sum((left >= 12 * i).astype(jnp.int32) for i in range(1, 8))
-    column = 48 * z + 12 * quarter + left - 12 * z
-    old = lax.broadcasted_iota(jnp.int32, (width, width), 0)
-    to_weight = ones_where(old == column)
     far = far_ref[...].astype(jnp.float32)[:, :4].reshape(rows, width).astype(jnp.bfloat16)
     copies = []
     for half in range(2):
@@ -153,10 +146,7 @@
         for h in range(heads):
             c = slice(h * LANES, (h + 1) * LANES)
             chosen.append(jnp.where(kinds_ref[h] == 1, back[:, c], near[:, c]).astype(jnp.bfloat16))
-        moved = jnp.dot(
-            jnp.concatenate(chosen, axis=1), to_weight, preferred_element_type=jnp.float32
-        )
-        out_ref[r, :] = moved.astype(jnp.bfloat16)
+        out_ref[r, :] = jnp.concatenate(chosen, axis=1)
         for x in range(out_hbm.shape[0]):
             copies.append(
                 pltpu.make_async_copy(out_ref.at[r], out_hbm.at[x, r], sems.at[2 * x + half])
@@ -171,6 +161,21 @@
         own_ref[y] = got.astype(jnp.bfloat16)
     for copy in copies:
         copy.wait()
+
+
+def order_kernel(x_ref, out_ref):
+    width = x_ref.shape[2]
+    place = lax.broadcasted_iota(jnp.int32, (1, width), 1)
+    quarter = sum((place >= edge).astype(jnp.int32) for edge in (96, 192, 288))
+    left = place - 96 * quarter
+    z = sum((left >= 12 * i).astype(jnp.int32) for i in range(1, 8))
+    column = 48 * z + 12 * quarter + left - 12 * z
+    old = lax.broadcasted_iota(jnp.int32, (width, width), 0)
+    to_weight = ones_where(old == column)
+    for x in range(x_ref.shape[0]):
+        out_ref[x] = jnp.dot(x_ref[x], to_weight, preferred_element_type=jnp.float32).astype(
+            jnp.bfloat16
+        )
 
 
 def weight_kernel(own_ref, next_ref, last_ref, second_ref, out_ref):
@@ -276,6 +281,7 @@
         axis_index_groups=[[0, 2, 4, 6], [1, 3, 5, 7]],
         tiled=True,
     )
+    columns = call(order_kernel, (parts // 2, rows, width), [VMEM], columns)
     others_columns = lax.ppermute(columns, "mlp", [(i, i ^ 1) for i in range(parts)])
     weight = call(
         weight_kernel,

time: 98.2 us -> 97.9 us (level)
    pallas_call x7 -> x8, Pallas kernels: 9.47 us -> 9.91 us  [call(): pl.pallas_call(kernel, out_shape=shapes if isinstance(shape, list) else s...]
  transfers between devices with their start and end apart: 6 -> 6, of which waited for: 2 -> 2; matrix products, arithmetic and copies ran while one was open for 0% -> 0% of each run, Pallas kernels for 2% -> 3%
where the time goes in v7:
time: 97.9 us; the launch traced here: 97.5 us
  starting transfers between devices  34.1 us (35%)
  blocking collectives  28.9 us (30%)
  waiting for transfers between devices  24.1 us (25%)
  Pallas kernels  9.91 us (10%)
    all_to_all x1, blocking collectives, local(): lax.all_to_all(far, 'seq', split_axis=0, concat_axis=0, tiled=True)  28.9 us
    all_to_all x1, waiting for transfers between devices, local(): moved = lax.all_to_all(sent, 'seq', split_axis=0, concat_axis=0, tiled=True)  17.4 us
    all_to_all x1, starting transfers between devices, local(): moved = lax.all_to_all(sent, 'seq', split_axis=0, concat_axis=0, tiled=True)  15.9 us
    pallas_call x8, Pallas kernels, call(): pl.pallas_call(kernel, out_shape=shapes if isinstance(shape, list) else s...  9.91 us
    ppermute x3, starting transfers between devices, fetch(): return lax.ppermute(block, ('seq', 'mlp'), pairs)  7.19 us
    ppermute x1, starting transfers between devices, local(): lax.ppermute(columns, 'mlp', [(i, i ^ 1) for i in range(parts)])  6.72 us
    ppermute x3, waiting for transfers between devices, fetch(): return lax.ppermute(block, ('seq', 'mlp'), pairs)  6.71 us
    all_to_all x1, starting transfers between devices, local(): lax.all_to_all(attended, 'mlp', split_axis=0, concat_axis=0, axis_index_g...  4.29 us
  transfers between devices with their start and end apart: 6, of which 2 were waited for; matrix products, arithmetic and copies ran while one was open for 0% of the time, Pallas kernels for 3%

profile of v7, /device:TPU:19, one launch (start us, length us, event | category | flops | bytes accessed | tf_op | source)
XLA Modules:
  0.0 97.5 jit_solution(3049446194507134998)
XLA Ops:
  0.0 0.0 copy-start.2
  0.0 0.0 copy-start
  0.0 0.0 copy-start.1
  0.0 0.0 copy-start.7
  0.0 0.0 copy-start.3
  0.0 2.5 %shard_map.82 = bf16[64,4,1152]{2,1,0:T(4,128)(2,1)} custom-call(s32[1,256]{1,0:T(1,128)} %bitcast.1, bf16[256,384]{1,0:T(8,128)(2,1)} %q_ref.1, bf16[256,384]{1,0:T(8,128)(2,1)} %k_ref.1, bf16[256,384]{1,0:T(8,128)(2,1)} %v_ref.1), custom_call_target="tpu_custom_call" | custom-call | tf_op jit(solution)/shard_map/pallas_call | solution.py:205
  2.5 15.9 %all-to-all-start = ((bf16[64,4,1152]{2,1,0:T(4,128)(2,1)}), bf16[64,4,1152]{2,1,0:T(4,128)(2,1)S(1)}, u32[]{:S(2)}, u32[]{:S(2)}) async-start(bf16[64,4,1152]{2,1,0:T(4,128)(2,1)} %shard_map.82), calls=%async_computation | async-start | bytes 1179648 | tf_op jit(solution)/shard_map/all_to_all | solution.py:254
  18.5 0.0 copy-done.7
  18.5 0.0 copy-start.4
  18.5 0.0 copy-start.5
  18.5 0.1 copy.10
  18.6 0.1 reshape.11.masks_ref
  18.7 0.0 copy-done.2
  18.7 0.0 copy-done
  18.7 0.0 copy-done.1
  18.7 1.3 %shard_map.84.after_hbm.near_ref = bf16[256,384]{1,0:T(8,128)(2,1)S(1)} custom-call(s32[12]{0:T(128)S(1)} %reshape.11.masks_ref, bf16[256,384]{1,0:T(8,128)(2,1)S(1)} %copy-done, bf16[256,384]{1,0:T(8,128)(2,1)S(1)} %copy-done.1, bf16[256,384]{1,0:T(8,128)(2,1)S(1)} %copy-done.2), custom_call_target="tpu_custom_call" | custom-call | tf_op jit(solution)/shard_map/pallas_call | solution.py:205
  20.0 0.0 copy-done.3
  20.0 0.3 shard_map.83.weights_ref
  20.3 17.4 %all-to-all-done.x_ref = bf16[64,4,1152]{2,1,0:T(4,128)(2,1)S(1)} async-done(((bf16[64,4,1152]{2,1,0:T(4,128)(2,1)}), bf16[64,4,1152]{2,1,0:T(4,128)(2,1)S(1)}, u32[]{:S(2)}, u32[]{:S(2)}) %all-to-all-start) | async-done | bytes 589856 | tf_op jit(solution)/shard_map/all_to_all | solution.py:254
  37.7 1.6 %shard_map.85 = bf16[64,16,384]{2,1,0:T(8,128)(2,1)S(1)} custom-call(s32[12]{0:T(128)S(1)} %reshape.11.masks_ref, bf16[64,4,1152]{2,1,0:T(4,128)(2,1)S(1)} %all-to-all-done.x_ref, bf16[16,16,384]{2,1,0:T(8,128)(2,1)S(1)} %shard_map.83.weights_ref, bf16[256,384]{1,0:T(8,128)(2,1)S(1)} %shard_map.84.after_hbm.near_ref), custom_call_target="tpu_custom_call" | custom-call | tf_op jit(solution)/shard_map/pallas_call | solution.py:205
  39.2 0.0 copy-start.6
  39.3 28.9 %all_to_all.15.far_ref = bf16[64,16,384]{2,1,0:T(8,128)(2,1)S(1)} all-to-all(bf16[64,16,384]{2,1,0:T(8,128)(2,1)S(1)} %shard_map.85), channel_id=1, replica_groups=mesh['seq'=64,'mlp'=8] {'seq'}, dimensions={0} | all-to-all | bytes 1572864 | tf_op jit(solution)/shard_map/all_to_all | solution.py:260
  68.2 0.0 copy-done.4
  68.2 0.0 copy-done.5
  68.2 1.7 %shard_map.86 = (bf16[4,256,384]{2,1,0:T(8,128)(2,1)}, bf16[8,96,384]{2,1,0:T(8,128)(2,1)S(1)}) custom-call(s32[3]{0:T(128)S(1)} %copy-done.5, s32[1,256]{1,0:T(1,128)S(1)} %bitcast.2, bf16[64,16,384]{2,1,0:T(8,128)(2,1)S(1)} %all_to_all.15.far_ref, bf16[256,384]{1,0:T(8,128)(2,1)S(1)} %shard_map.84.after_hbm.near_ref), custom_call_target="tpu_custom_call" | custom-call | tf_op jit(solution)/shard_map/pallas_call | solution.py:205
  69.9 4.3 %all-to-all-start.2 = ((bf16[4,256,384]{2,1,0:T(8,128)(2,1)}), bf16[4,256,384]{2,1,0:T(8,128)(2,1)S(1)}, u32[]{:S(2)}, u32[]{:S(2)}) async-start(bf16[4,256,384]{2,1,0:T(8,128)(2,1)} %get-tuple-element.7), calls=%async_computation.2 | async-start | bytes 1572864 | tf_op jit(solution)/shard_map/all_to_all | solution.py:276
  74.2 1.9 %collective-permute-start.1 = (bf16[8,96,384]{2,1,0:T(8,128)(2,1)S(1)}, bf16[8,96,384]{2,1,0:T(8,128)(2,1)S(1)}, u32[]{:S(2)}, u32[]{:S(2)}) collective-permute-start(bf16[8,96,384]{2,1,0:T(8,128)(2,1)S(1)} %get-tuple-element.8.own_ref), channel_id=1, source_target_pairs={{8,0},{65,1},{10,2},{67,3},{12,4},{69,5},{14,6},{71,7},{16,8},{73,... | collective-permute-start | bytes 1769480 | tf_op jit(solution)/shard_map/ppermute | solution.py:224
  76.2 3.4 %collective-permute-start.2 = (bf16[8,96,384]{2,1,0:T(8,128)(2,1)S(1)}, bf16[8,96,384]{2,1,0:T(8,128)(2,1)S(1)}, u32[]{:S(2)}, u32[]{:S(2)}) collective-permute-start(bf16[8,96,384]{2,1,0:T(8,128)(2,1)S(1)} %get-tuple-element.8.own_ref), channel_id=1, source_target_pairs={{56,0},{449,1},{58,2},{451,3},{60,4},{453,5},{62,6},{455,7},{0,8},... | collective-permute-start | bytes 1769480 | tf_op jit(solution)/shard_map/ppermute | solution.py:224
  79.5 1.9 %collective-permute-start.3 = (bf16[8,96,384]{2,1,0:T(8,128)(2,1)S(1)}, bf16[8,96,384]{2,1,0:T(8,128)(2,1)S(1)}, u32[]{:S(2)}, u32[]{:S(2)}) collective-permute-start(bf16[8,96,384]{2,1,0:T(8,128)(2,1)S(1)} %get-tuple-element.8.own_ref), channel_id=1, source_target_pairs={{64,0},{9,1},{66,2},{11,3},{68,4},{13,5},{70,6},{15,7},{72,8},{17,... | collective-permute-start | bytes 1769480 | tf_op jit(solution)/shard_map/ppermute | solution.py:224
  81.5 0.0 copy-done.6
  81.5 0.0 all-to-all-done.2.x_ref
  81.5 0.7 shard_map.87.x_ref
  82.2 6.7 %collective-permute-start = (bf16[4,256,384]{2,1,0:T(8,128)(2,1)S(1)}, bf16[4,256,384]{2,1,0:T(8,128)(2,1)S(1)}, u32[]{:S(2)}, u32[]{:S(2)}) collective-permute-start(bf16[4,256,384]{2,1,0:T(8,128)(2,1)S(1)} %shard_map.87.x_ref), channel_id=1, source_target_pairs={{0,1},{1,0},{2,3},{3,2},{4,5},{5,4},{6,7},{7,6},{8,9},{9,8},{10,11... | collective-permute-start | bytes 2359304 | tf_op jit(solution)/shard_map/ppermute | solution.py:285
  88.9 0.0 collective-permute-done.1.next_ref
  88.9 0.0 collective-permute-done.2.last_ref
  88.9 6.7 %collective-permute-done.3.second_ref = bf16[8,96,384]{2,1,0:T(8,128)(2,1)S(1)} collective-permute-done((bf16[8,96,384]{2,1,0:T(8,128)(2,1)S(1)}, bf16[8,96,384]{2,1,0:T(8,128)(2,1)S(1)}, u32[]{:S(2)}, u32[]{:S(2)}) %collective-permute-start.3) | collective-permute-done | bytes 589856 | tf_op jit(solution)/shard_map/ppermute | solution.py:224
  95.6 0.2 shard_map.88.w_ref
  95.9 0.0 collective-permute-done.others_ref
  95.9 1.7 %shard_map.89 = bf16[256,384]{1,0:T(8,128)(2,1)} custom-call(f32[1,384]{1,0:T(1,128)S(1)} %reshape.9.gate_ref, bf16[4,256,384]{2,1,0:T(8,128)(2,1)S(1)} %shard_map.87.x_ref, bf16[4,256,384]{2,1,0:T(8,128)(2,1)S(1)} %collective-permute-done.others_ref, bf16[8,384,384]{2,1,0:T(8,128)(2,1)S(1)} %shard_map.88.w_ref), custom_call_target="tpu_custom_call" | custom-call | tf_op jit(solution)/shard_map/pallas_call | solution.py:205
  (1 shorter events, 0.0 us)
Async XLA Ops:
  0.0 18.7 %copy-start.2 = (bf16[256,384]{1,0:T(8,128)(2,1)S(1)}, bf16[256,384]{1,0:T(8,128)(2,1)}, u32[]{:S(2)}) copy-start(bf16[256,384]{1,0:T(8,128)(2,1)} %v_ref.1) | copy-start | bytes 589828
  0.0 18.7 %copy-start = (bf16[256,384]{1,0:T(8,128)(2,1)S(1)}, bf16[256,384]{1,0:T(8,128)(2,1)}, u32[]{:S(2)}) copy-start(bf16[256,384]{1,0:T(8,128)(2,1)} %q_ref.1) | copy-start | bytes 589828
  0.0 18.7 %copy-start.1 = (bf16[256,384]{1,0:T(8,128)(2,1)S(1)}, bf16[256,384]{1,0:T(8,128)(2,1)}, u32[]{:S(2)}) copy-start(bf16[256,384]{1,0:T(8,128)(2,1)} %k_ref.1) | copy-start | bytes 589828
  0.0 18.4 %copy-start.7 = (s32[3,2,2]{0,2,1:T(2,128)S(1)}, s32[3,2,2]{0,2,1:T(2,128)}, u32[]{:S(2)}) copy-start(s32[3,2,2]{0,2,1:T(2,128)} %param.12) | copy-start | bytes 148
  0.0 20.0 %copy-start.3 = (bf16[48,384]{1,0:T(8,128)(2,1)S(1)}, bf16[48,384]{1,0:T(8,128)(2,1)}, u32[]{:S(2)}) copy-start(bf16[48,384]{1,0:T(8,128)(2,1)} %w_ref.1) | copy-start | bytes 110596
  2.5 35.1 %all-to-all-start = ((bf16[64,4,1152]{2,1,0:T(4,128)(2,1)}), bf16[64,4,1152]{2,1,0:T(4,128)(2,1)S(1)}, u32[]{:S(2)}, u32[]{:S(2)}) async-start(bf16[64,4,1152]{2,1,0:T(4,128)(2,1)} %shard_map.82), calls=%async_computation | async-start | bytes 1179648 | tf_op jit(solution)/shard_map/all_to_all | solution.py:254
  18.5 49.7 %copy-start.4 = (s32[256]{0:T(256)S(1)}, s32[256]{0:T(256)}, u32[]{:S(2)}) copy-start(s32[256]{0:T(256)} %param.13) | copy-start | bytes 3076
  18.5 49.7 %copy-start.5 = (s32[3]{0:T(128)S(1)}, s32[3]{0:T(128)}, u32[]{:S(2)}) copy-start(s32[3]{0:T(128)} %kinds_ref.1) | copy-start | bytes 40
  39.2 42.2 %copy-start.6 = (f32[384]{0:T(512)S(1)}, f32[384]{0:T(512)}, u32[]{:S(2)}) copy-start(f32[384]{0:T(512)} %param.15) | copy-start | bytes 4612
  69.9 11.5 %all-to-all-start.2 = ((bf16[4,256,384]{2,1,0:T(8,128)(2,1)}), bf16[4,256,384]{2,1,0:T(8,128)(2,1)S(1)}, u32[]{:S(2)}, u32[]{:S(2)}) async-start(bf16[4,256,384]{2,1,0:T(8,128)(2,1)} %get-tuple-element.7), calls=%async_computation.2 | async-start | bytes 1572864 | tf_op jit(solution)/shard_map/all_to_all | solution.py:276
  74.2 14.6 %collective-permute-start.1 = (bf16[8,96,384]{2,1,0:T(8,128)(2,1)S(1)}, bf16[8,96,384]{2,1,0:T(8,128)(2,1)S(1)}, u32[]{:S(2)}, u32[]{:S(2)}) collective-permute-start(bf16[8,96,384]{2,1,0:T(8,128)(2,1)S(1)} %get-tuple-element.8.own_ref), channel_id=1, source_target_pairs={{8,0},{65,1},{10,2},{67,3},{12,4},{69,5},{14,6},{71,7},{16,8},{73,... | collective-permute-start | bytes 1769480 | tf_op jit(solution)/shard_map/ppermute | solution.py:224
  76.2 12.7 %collective-permute-start.2 = (bf16[8,96,384]{2,1,0:T(8,128)(2,1)S(1)}, bf16[8,96,384]{2,1,0:T(8,128)(2,1)S(1)}, u32[]{:S(2)}, u32[]{:S(2)}) collective-permute-start(bf16[8,96,384]{2,1,0:T(8,128)(2,1)S(1)} %get-tuple-element.8.own_ref), channel_id=1, source_target_pairs={{56,0},{449,1},{58,2},{451,3},{60,4},{453,5},{62,6},{455,7},{0,8},... | collective-permute-start | bytes 1769480 | tf_op jit(solution)/shard_map/ppermute | solution.py:224
  79.5 16.1 %collective-permute-start.3 = (bf16[8,96,384]{2,1,0:T(8,128)(2,1)S(1)}, bf16[8,96,384]{2,1,0:T(8,128)(2,1)S(1)}, u32[]{:S(2)}, u32[]{:S(2)}) collective-permute-start(bf16[8,96,384]{2,1,0:T(8,128)(2,1)S(1)} %get-tuple-element.8.own_ref), channel_id=1, source_target_pairs={{64,0},{9,1},{66,2},{11,3},{68,4},{13,5},{70,6},{15,7},{72,8},{17,... | collective-permute-start | bytes 1769480 | tf_op jit(solution)/shard_map/ppermute | solution.py:224
  82.2 13.7 %collective-permute-start = (bf16[4,256,384]{2,1,0:T(8,128)(2,1)S(1)}, bf16[4,256,384]{2,1,0:T(8,128)(2,1)S(1)}, u32[]{:S(2)}, u32[]{:S(2)}) collective-permute-start(bf16[4,256,384]{2,1,0:T(8,128)(2,1)S(1)} %shard_map.87.x_ref), channel_id=1, source_target_pairs={{0,1},{1,0},{2,3},{3,2},{4,5},{5,4},{6,7},{7,6},{8,9},{9,8},{10,11... | collective-permute-start | bytes 2359304 | tf_op jit(solution)/shard_map/ppermute | solution.py:285

commit v8 on v7

--- a/solution.py
+++ b/solution.py
@@ -138,8 +138,8 @@
     onehot = placement(order_ref[...], rows)
     far = far_ref[...].astype(jnp.float32)[:, :4].reshape(rows, width).astype(jnp.bfloat16)
     copies = []
-    for half in range(2):
-        r = slice(half * rows // 2, (half + 1) * rows // 2)
+    for step in range(4):
+        r = slice(step * rows // 4, (step + 1) * rows // 4)
         back = jnp.dot(onehot[r], far, preferred_element_type=jnp.float32)
         near = near_ref[r, :].astype(jnp.float32)
         chosen = []
@@ -149,7 +149,7 @@
         out_ref[r, :] = jnp.concatenate(chosen, axis=1)
         for x in range(out_hbm.shape[0]):
             copies.append(
-                pltpu.make_async_copy(out_ref.at[r], out_hbm.at[x, r], sems.at[2 * x + half])
+                pltpu.make_async_copy(out_ref.at[r], out_hbm.at[x, r], sems.at[4 * x + step])
             )
             copies[-1].start()
     n, part = own_ref.shape[:2]
@@ -268,7 +268,7 @@
         returned,
         near,
         out=[HBM, VMEM],
-        scratch=[pltpu.VMEM((rows, width), jnp.bfloat16), pltpu.SemaphoreType.DMA((parts,))],
+        scratch=[pltpu.VMEM((rows, width), jnp.bfloat16), pltpu.SemaphoreType.DMA((2 * parts,))],
     )
     others = [
         fetch(own, offsets) for offsets in (((0, 1), (1, 0)), ((0, -1), (-1, 0)), ((1, 0), (0, 1)))

time: 97.9 us -> 98 us (level)
  no operation moved by 1% of the time
where the time goes in v8:
time: 98 us; the launch traced here: 97.6 us
  starting transfers between devices  34.1 us (35%)
  blocking collectives  28.9 us (29%)
  waiting for transfers between devices  24.1 us (25%)
  Pallas kernels  9.95 us (10%)
    all_to_all x1, blocking collectives, local(): lax.all_to_all(far, 'seq', split_axis=0, concat_axis=0, tiled=True)  28.9 us
    all_to_all x1, waiting for transfers between devices, local(): moved = lax.all_to_all(sent, 'seq', split_axis=0, concat_axis=0, tiled=True)  17.4 us
    all_to_all x1, starting transfers between devices, local(): moved = lax.all_to_all(sent, 'seq', split_axis=0, concat_axis=0, tiled=True)  15.9 us
    pallas_call x8, Pallas kernels, call(): pl.pallas_call(kernel, out_shape=shapes if isinstance(shape, list) else s...  9.95 us
    ppermute x3, starting transfers between devices, fetch(): return lax.ppermute(block, ('seq', 'mlp'), pairs)  7.19 us
    ppermute x1, starting transfers between devices, local(): lax.ppermute(columns, 'mlp', [(i, i ^ 1) for i in range(parts)])  6.73 us
    ppermute x3, waiting for transfers between devices, fetch(): return lax.ppermute(block, ('seq', 'mlp'), pairs)  6.71 us
    all_to_all x1, starting transfers between devices, local(): lax.all_to_all(attended, 'mlp', split_axis=0, concat_axis=0, axis_index_g...  4.3 us
  transfers between devices with their start and end apart: 6, of which 2 were waited for; matrix products, arithmetic and copies ran while one was open for 0% of the time, Pallas kernels for 3%

profile of v8, /device:TPU:19, one launch (start us, length us, event | category | flops | bytes accessed | tf_op | source)
XLA Modules:
  0.0 97.6 jit_solution(16081606206183786356)
XLA Ops:
  0.0 0.0 copy-start.2
  0.0 0.0 copy-start
  0.0 0.0 copy-start.1
  0.0 0.0 copy-start.7
  0.0 0.0 copy-start.3
  0.0 2.5 %shard_map.82 = bf16[64,4,1152]{2,1,0:T(4,128)(2,1)} custom-call(s32[1,256]{1,0:T(1,128)} %bitcast.1, bf16[256,384]{1,0:T(8,128)(2,1)} %q_ref.1, bf16[256,384]{1,0:T(8,128)(2,1)} %k_ref.1, bf16[256,384]{1,0:T(8,128)(2,1)} %v_ref.1), custom_call_target="tpu_custom_call" | custom-call | tf_op jit(solution)/shard_map/pallas_call | solution.py:205
  2.5 15.9 %all-to-all-start = ((bf16[64,4,1152]{2,1,0:T(4,128)(2,1)}), bf16[64,4,1152]{2,1,0:T(4,128)(2,1)S(1)}, u32[]{:S(2)}, u32[]{:S(2)}) async-start(bf16[64,4,1152]{2,1,0:T(4,128)(2,1)} %shard_map.82), calls=%async_computation | async-start | bytes 1179648 | tf_op jit(solution)/shard_map/all_to_all | solution.py:254
  18.5 0.0 copy-done.7
  18.5 0.0 copy-start.4
  18.5 0.0 copy-start.5
  18.5 0.1 copy.10
  18.6 0.1 reshape.11.masks_ref
  18.7 0.0 copy-done.2
  18.7 0.0 copy-done
  18.7 0.0 copy-done.1
  18.7 1.3 %shard_map.84.after_hbm.near_ref = bf16[256,384]{1,0:T(8,128)(2,1)S(1)} custom-call(s32[12]{0:T(128)S(1)} %reshape.11.masks_ref, bf16[256,384]{1,0:T(8,128)(2,1)S(1)} %copy-done, bf16[256,384]{1,0:T(8,128)(2,1)S(1)} %copy-done.1, bf16[256,384]{1,0:T(8,128)(2,1)S(1)} %copy-done.2), custom_call_target="tpu_custom_call" | custom-call | tf_op jit(solution)/shard_map/pallas_call | solution.py:205
  20.0 0.0 copy-done.3
  20.0 0.3 shard_map.83.weights_ref
  20.3 17.4 %all-to-all-done.x_ref = bf16[64,4,1152]{2,1,0:T(4,128)(2,1)S(1)} async-done(((bf16[64,4,1152]{2,1,0:T(4,128)(2,1)}), bf16[64,4,1152]{2,1,0:T(4,128)(2,1)S(1)}, u32[]{:S(2)}, u32[]{:S(2)}) %all-to-all-start) | async-done | bytes 589856 | tf_op jit(solution)/shard_map/all_to_all | solution.py:254
  37.7 1.6 %shard_map.85 = bf16[64,16,384]{2,1,0:T(8,128)(2,1)S(1)} custom-call(s32[12]{0:T(128)S(1)} %reshape.11.masks_ref, bf16[64,4,1152]{2,1,0:T(4,128)(2,1)S(1)} %all-to-all-done.x_ref, bf16[16,16,384]{2,1,0:T(8,128)(2,1)S(1)} %shard_map.83.weights_ref, bf16[256,384]{1,0:T(8,128)(2,1)S(1)} %shard_map.84.after_hbm.near_ref), custom_call_target="tpu_custom_call" | custom-call | tf_op jit(solution)/shard_map/pallas_call | solution.py:205
  39.2 0.0 copy-start.6
  39.3 28.9 %all_to_all.15.far_ref = bf16[64,16,384]{2,1,0:T(8,128)(2,1)S(1)} all-to-all(bf16[64,16,384]{2,1,0:T(8,128)(2,1)S(1)} %shard_map.85), channel_id=1, replica_groups=mesh['seq'=64,'mlp'=8] {'seq'}, dimensions={0} | all-to-all | bytes 1572864 | tf_op jit(solution)/shard_map/all_to_all | solution.py:260
  68.2 0.0 copy-done.4
  68.2 0.0 copy-done.5
  68.2 1.8 %shard_map.86 = (bf16[4,256,384]{2,1,0:T(8,128)(2,1)}, bf16[8,96,384]{2,1,0:T(8,128)(2,1)S(1)}) custom-call(s32[3]{0:T(128)S(1)} %copy-done.5, s32[1,256]{1,0:T(1,128)S(1)} %bitcast.2, bf16[64,16,384]{2,1,0:T(8,128)(2,1)S(1)} %all_to_all.15.far_ref, bf16[256,384]{1,0:T(8,128)(2,1)S(1)} %shard_map.84.after_hbm.near_ref), custom_call_target="tpu_custom_call" | custom-call | tf_op jit(solution)/shard_map/pallas_call | solution.py:205
  70.0 4.3 %all-to-all-start.2 = ((bf16[4,256,384]{2,1,0:T(8,128)(2,1)}), bf16[4,256,384]{2,1,0:T(8,128)(2,1)S(1)}, u32[]{:S(2)}, u32[]{:S(2)}) async-start(bf16[4,256,384]{2,1,0:T(8,128)(2,1)} %get-tuple-element.7), calls=%async_computation.2 | async-start | bytes 1572864 | tf_op jit(solution)/shard_map/all_to_all | solution.py:276
  74.3 1.9 %collective-permute-start.1 = (bf16[8,96,384]{2,1,0:T(8,128)(2,1)S(1)}, bf16[8,96,384]{2,1,0:T(8,128)(2,1)S(1)}, u32[]{:S(2)}, u32[]{:S(2)}) collective-permute-start(bf16[8,96,384]{2,1,0:T(8,128)(2,1)S(1)} %get-tuple-element.8.own_ref), channel_id=1, source_target_pairs={{8,0},{65,1},{10,2},{67,3},{12,4},{69,5},{14,6},{71,7},{16,8},{73,... | collective-permute-start | bytes 1769480 | tf_op jit(solution)/shard_map/ppermute | solution.py:224
  76.2 3.4 %collective-permute-start.2 = (bf16[8,96,384]{2,1,0:T(8,128)(2,1)S(1)}, bf16[8,96,384]{2,1,0:T(8,128)(2,1)S(1)}, u32[]{:S(2)}, u32[]{:S(2)}) collective-permute-start(bf16[8,96,384]{2,1,0:T(8,128)(2,1)S(1)} %get-tuple-element.8.own_ref), channel_id=1, source_target_pairs={{56,0},{449,1},{58,2},{451,3},{60,4},{453,5},{62,6},{455,7},{0,8},... | collective-permute-start | bytes 1769480 | tf_op jit(solution)/shard_map/ppermute | solution.py:224
  79.6 1.9 %collective-permute-start.3 = (bf16[8,96,384]{2,1,0:T(8,128)(2,1)S(1)}, bf16[8,96,384]{2,1,0:T(8,128)(2,1)S(1)}, u32[]{:S(2)}, u32[]{:S(2)}) collective-permute-start(bf16[8,96,384]{2,1,0:T(8,128)(2,1)S(1)} %get-tuple-element.8.own_ref), channel_id=1, source_target_pairs={{64,0},{9,1},{66,2},{11,3},{68,4},{13,5},{70,6},{15,7},{72,8},{17,... | collective-permute-start | bytes 1769480 | tf_op jit(solution)/shard_map/ppermute | solution.py:224
  81.5 0.0 copy-done.6
  81.5 0.0 all-to-all-done.2.x_ref
  81.5 0.7 shard_map.87.x_ref
  82.2 6.7 %collective-permute-start = (bf16[4,256,384]{2,1,0:T(8,128)(2,1)S(1)}, bf16[4,256,384]{2,1,0:T(8,128)(2,1)S(1)}, u32[]{:S(2)}, u32[]{:S(2)}) collective-permute-start(bf16[4,256,384]{2,1,0:T(8,128)(2,1)S(1)} %shard_map.87.x_ref), channel_id=1, source_target_pairs={{0,1},{1,0},{2,3},{3,2},{4,5},{5,4},{6,7},{7,6},{8,9},{9,8},{10,11... | collective-permute-start | bytes 2359304 | tf_op jit(solution)/shard_map/ppermute | solution.py:285
  88.9 0.0 collective-permute-done.1.next_ref
  88.9 0.0 collective-permute-done.2.last_ref
  88.9 6.7 %collective-permute-done.3.second_ref = bf16[8,96,384]{2,1,0:T(8,128)(2,1)S(1)} collective-permute-done((bf16[8,96,384]{2,1,0:T(8,128)(2,1)S(1)}, bf16[8,96,384]{2,1,0:T(8,128)(2,1)S(1)}, u32[]{:S(2)}, u32[]{:S(2)}) %collective-permute-start.3) | collective-permute-done | bytes 589856 | tf_op jit(solution)/shard_map/ppermute | solution.py:224
  95.7 0.2 shard_map.88.w_ref
  95.9 0.0 collective-permute-done.others_ref
  95.9 1.7 %shard_map.89 = bf16[256,384]{1,0:T(8,128)(2,1)} custom-call(f32[1,384]{1,0:T(1,128)S(1)} %reshape.9.gate_ref, bf16[4,256,384]{2,1,0:T(8,128)(2,1)S(1)} %shard_map.87.x_ref, bf16[4,256,384]{2,1,0:T(8,128)(2,1)S(1)} %collective-permute-done.others_ref, bf16[8,384,384]{2,1,0:T(8,128)(2,1)S(1)} %shard_map.88.w_ref), custom_call_target="tpu_custom_call" | custom-call | tf_op jit(solution)/shard_map/pallas_call | solution.py:205
  (1 shorter events, 0.0 us)
Async XLA Ops:
  0.0 18.7 %copy-start.2 = (bf16[256,384]{1,0:T(8,128)(2,1)S(1)}, bf16[256,384]{1,0:T(8,128)(2,1)}, u32[]{:S(2)}) copy-start(bf16[256,384]{1,0:T(8,128)(2,1)} %v_ref.1) | copy-start | bytes 589828
  0.0 18.7 %copy-start = (bf16[256,384]{1,0:T(8,128)(2,1)S(1)}, bf16[256,384]{1,0:T(8,128)(2,1)}, u32[]{:S(2)}) copy-start(bf16[256,384]{1,0:T(8,128)(2,1)} %q_ref.1) | copy-start | bytes 589828
  0.0 18.7 %copy-start.1 = (bf16[256,384]{1,0:T(8,128)(2,1)S(1)}, bf16[256,384]{1,0:T(8,128)(2,1)}, u32[]{:S(2)}) copy-start(bf16[256,384]{1,0:T(8,128)(2,1)} %k_ref.1) | copy-start | bytes 589828
  0.0 18.4 %copy-start.7 = (s32[3,2,2]{0,2,1:T(2,128)S(1)}, s32[3,2,2]{0,2,1:T(2,128)}, u32[]{:S(2)}) copy-start(s32[3,2,2]{0,2,1:T(2,128)} %param.12) | copy-start | bytes 148
  0.0 20.0 %copy-start.3 = (bf16[48,384]{1,0:T(8,128)(2,1)S(1)}, bf16[48,384]{1,0:T(8,128)(2,1)}, u32[]{:S(2)}) copy-start(bf16[48,384]{1,0:T(8,128)(2,1)} %w_ref.1) | copy-start | bytes 110596
  2.5 35.1 %all-to-all-start = ((bf16[64,4,1152]{2,1,0:T(4,128)(2,1)}), bf16[64,4,1152]{2,1,0:T(4,128)(2,1)S(1)}, u32[]{:S(2)}, u32[]{:S(2)}) async-start(bf16[64,4,1152]{2,1,0:T(4,128)(2,1)} %shard_map.82), calls=%async_computation | async-start | bytes 1179648 | tf_op jit(solution)/shard_map/all_to_all | solution.py:254
  18.5 49.7 %copy-start.4 = (s32[256]{0:T(256)S(1)}, s32[256]{0:T(256)}, u32[]{:S(2)}) copy-start(s32[256]{0:T(256)} %param.13) | copy-start | bytes 3076
  18.5 49.7 %copy-start.5 = (s32[3]{0:T(128)S(1)}, s32[3]{0:T(128)}, u32[]{:S(2)}) copy-start(s32[3]{0:T(128)} %kinds_ref.1) | copy-start | bytes 40
  39.2 42.3 %copy-start.6 = (f32[384]{0:T(512)S(1)}, f32[384]{0:T(512)}, u32[]{:S(2)}) copy-start(f32[384]{0:T(512)} %param.15) | copy-start | bytes 4612
  70.0 11.5 %all-to-all-start.2 = ((bf16[4,256,384]{2,1,0:T(8,128)(2,1)}), bf16[4,256,384]{2,1,0:T(8,128)(2,1)S(1)}, u32[]{:S(2)}, u32[]{:S(2)}) async-start(bf16[4,256,384]{2,1,0:T(8,128)(2,1)} %get-tuple-element.7), calls=%async_computation.2 | async-start | bytes 1572864 | tf_op jit(solution)/shard_map/all_to_all | solution.py:276
  74.3 14.6 %collective-permute-start.1 = (bf16[8,96,384]{2,1,0:T(8,128)(2,1)S(1)}, bf16[8,96,384]{2,1,0:T(8,128)(2,1)S(1)}, u32[]{:S(2)}, u32[]{:S(2)}) collective-permute-start(bf16[8,96,384]{2,1,0:T(8,128)(2,1)S(1)} %get-tuple-element.8.own_ref), channel_id=1, source_target_pairs={{8,0},{65,1},{10,2},{67,3},{12,4},{69,5},{14,6},{71,7},{16,8},{73,... | collective-permute-start | bytes 1769480 | tf_op jit(solution)/shard_map/ppermute | solution.py:224
  76.2 12.7 %collective-permute-start.2 = (bf16[8,96,384]{2,1,0:T(8,128)(2,1)S(1)}, bf16[8,96,384]{2,1,0:T(8,128)(2,1)S(1)}, u32[]{:S(2)}, u32[]{:S(2)}) collective-permute-start(bf16[8,96,384]{2,1,0:T(8,128)(2,1)S(1)} %get-tuple-element.8.own_ref), channel_id=1, source_target_pairs={{56,0},{449,1},{58,2},{451,3},{60,4},{453,5},{62,6},{455,7},{0,8},... | collective-permute-start | bytes 1769480 | tf_op jit(solution)/shard_map/ppermute | solution.py:224
  79.6 16.1 %collective-permute-start.3 = (bf16[8,96,384]{2,1,0:T(8,128)(2,1)S(1)}, bf16[8,96,384]{2,1,0:T(8,128)(2,1)S(1)}, u32[]{:S(2)}, u32[]{:S(2)}) collective-permute-start(bf16[8,96,384]{2,1,0:T(8,128)(2,1)S(1)} %get-tuple-element.8.own_ref), channel_id=1, source_target_pairs={{64,0},{9,1},{66,2},{11,3},{68,4},{13,5},{70,6},{15,7},{72,8},{17,... | collective-permute-start | bytes 1769480 | tf_op jit(solution)/shard_map/ppermute | solution.py:224
  82.2 13.7 %collective-permute-start = (bf16[4,256,384]{2,1,0:T(8,128)(2,1)S(1)}, bf16[4,256,384]{2,1,0:T(8,128)(2,1)S(1)}, u32[]{:S(2)}, u32[]{:S(2)}) collective-permute-start(bf16[4,256,384]{2,1,0:T(8,128)(2,1)S(1)} %shard_map.87.x_ref), channel_id=1, source_target_pairs={{0,1},{1,0},{2,3},{3,2},{4,5},{5,4},{6,7},{7,6},{8,9},{9,8},{10,11... | collective-permute-start | bytes 2359304 | tf_op jit(solution)/shard_map/ppermute | solution.py:285
